TPU v7x, 32 devices: a whole 2x2x4 slice. The times are simulated.
32 devices in a mesh: seq: 8 (over y, x, core), shard: 4 (over z).
Axes of the slice: x: 2, y: 2, z: 4, core: 2. Of those that a mesh axis runs over, the one named last changes fastest.
Arguments:
- tokens: bfloat16 [40960, 768], P(('seq', 'shard')), may hold values from -6 to 6
- positions: int32 [40960], P(('seq', 'shard')), may hold values from 0 to 2430, as said below
- cotangent: bfloat16 [40960, 768], P(('seq', 'shard')), may hold values from -6 to 6
- qkv_weight: float32 [768, 2304], P('shard'), may hold values from -0.21875 to 0.21875
- attn_weight: float32 [768, 768], P('shard'), may hold values from -0.875 to 0.875
- mlp_weight: float32 [768, 2304], P('shard'), may hold values from -0.21875 to 0.21875
- down_weight: float32 [1152, 768], P('shard'), may hold values from -0.1875 to 0.1875
- norm_gains: float32 [2, 768], P(None, 'shard'), may hold values from 0.5 to 1.5
- qkv_first: float32 [768, 2304], P('shard'), may hold values from -64 to 64
- qkv_second: float32 [768, 2304], P('shard'), may hold values from 208.896 to 835.584
- attn_first: float32 [768, 768], P('shard'), may hold values from -32 to 32
- attn_second: float32 [768, 768], P('shard'), may hold values from 52.224 to 208.896
- mlp_first: float32 [768, 2304], P('shard'), may hold values from -64 to 64
- mlp_second: float32 [768, 2304], P('shard'), may hold values from 169.1648 to 676.6592
- down_first: float32 [1152, 768], P('shard'), may hold values from -80 to 80
- down_second: float32 [1152, 768], P('shard'), may hold values from 300.6464 to 1203.4048
- gains_first: float32 [2, 768], P(None, 'shard'), may hold values from -112 to 112
- gains_second: float32 [2, 768], P(None, 'shard'), may hold values from 534.9376 to 2139.7505
Outputs:
- layer_output: bfloat16 [40960, 768], P(('seq', 'shard'))
- input_grad: bfloat16 [40960, 768], P(('seq', 'shard'))
- qkv_first_new: float32 [768, 2304], P('shard')
- qkv_second_new: float32 [768, 2304], P('shard')
- qkv_new: float32 [768, 2304], P('shard')
- attn_first_new: float32 [768, 768], P('shard')
- attn_second_new: float32 [768, 768], P('shard')
- attn_new: float32 [768, 768], P('shard')
- mlp_first_new: float32 [768, 2304], P('shard')
- mlp_second_new: float32 [768, 2304], P('shard')
- mlp_new: float32 [768, 2304], P('shard')
- down_first_new: float32 [1152, 768], P('shard')
- down_second_new: float32 [1152, 768], P('shard')
- down_new: float32 [1152, 768], P('shard')
- gains_first_new: float32 [2, 768], P(None, 'shard')
- gains_second_new: float32 [2, 768], P(None, 'shard')
- gains_new: float32 [2, 768], P(None, 'shard')
Inputs may be any that keep to these rules, and one draw needn't show every extreme that they name: positions[t] counts the tokens of t's document before t. A document starts at token 0, and exactly once in each aligned run of 1280 tokens (the tokens of one device), never among the first 64 or the last 64 tokens of that run.
All inputs are finite; a program needn't handle non-finite values.
Results may differ from a plain program's by a relative error of at most 0.015.
Values may be sent and summed in bfloat16 or wider, within the bound.
No kernel may reach another device: no remote copies, remote signals or barrier semaphores. Data moves between devices by JAX's collectives and lax.ppermute only.
A program may use at most 320 MiB of HBM per device.

v0:
```python
import math

import jax
import jax.numpy as jnp
from jax import lax
from jax.sharding import PartitionSpec as P

HEADS = 12
HALF = 64
ADAM_STEP = 5


norm_epsilon = 1e-05
rope_theta = 10000.0
beta_first = 0.9
beta_second = 0.98
adam_epsilon = 1e-06
decay_rate = 1e-05
rate_matrix = 0.04
rate_gains = 0.2
masked_score = -1e30


def with_halo(cells, sides, width):
    for axis, dim in sides:
        count = lax.axis_size(axis)
        ends = count - 1
        head = lax.slice_in_dim(cells, 0, width, axis=dim)
        tail = lax.slice_in_dim(cells, cells.shape[dim] - width, cells.shape[dim], axis=dim)
        cells = jnp.concatenate(
            [
                lax.ppermute(tail, axis, [(i, (i + 1) % count) for i in range(ends)]),
                cells,
                lax.ppermute(head, axis, [((i + 1) % count, i) for i in range(ends)]),
            ],
            axis=dim,
        )
    return cells


def from_behind(value, axis, steps):
    count = lax.axis_size(axis)
    first, last = (max(0, -steps), min(count, count - steps))
    return lax.ppermute(value, axis, [(source, source + steps) for source in range(first, last)])


def layer_norm(hidden, gain_row):
    centered = hidden - jnp.mean(hidden, axis=-1, keepdims=True)
    inverse_dev = lax.rsqrt(jnp.mean(centered * centered, axis=-1, keepdims=True) + norm_epsilon)
    return centered * inverse_dev * gain_row


def rope_tables(positions, head_size):
    half_size = head_size // 2
    exponent = jnp.arange(half_size, dtype=jnp.float32) * (2.0 / head_size)
    inverse = rope_theta ** (-exponent)
    angles = positions.astype(jnp.float32)[:, None] * inverse[None, :]
    angles = jnp.concatenate([angles, angles], axis=-1)
    return (jnp.cos(angles)[:, None, :], jnp.sin(angles)[:, None, :])


def rotate_half(values):
    half_size = values.shape[-1] // 2
    return jnp.concatenate([-values[..., half_size:], values[..., :half_size]], axis=-1)


def rotate_back(values):
    half_size = values.shape[-1] // 2
    return jnp.concatenate([values[..., half_size:], -values[..., :half_size]], axis=-1)


def geglu(expanded):
    hidden_size = expanded.shape[-1] // 2
    return jax.nn.gelu(expanded[:, :hidden_size], approximate=False) * expanded[:, hidden_size:]


def adam_update(master, first_moment, second_moment, gradient, step_rate):
    new_first = beta_first * first_moment + (1.0 - beta_first) * gradient
    new_second = beta_second * second_moment + (1.0 - beta_second) * gradient * gradient
    first_hat = new_first / (1.0 - beta_first**ADAM_STEP)
    second_hat = new_second / (1.0 - beta_second**ADAM_STEP)
    new_master = master - step_rate * (
        decay_rate * master + first_hat / (jnp.sqrt(second_hat) + adam_epsilon)
    )
    return (new_first, new_second, new_master)


def allowed_mask(positions, first_row, query_rows, device, last_device):
    local_rows = positions.shape[0]
    padded_positions = jnp.pad(positions, (HALF, HALF))
    query_index = first_row + jnp.arange(query_rows, dtype=jnp.int32)
    key_index = first_row - HALF + jnp.arange(query_rows + 2 * HALF, dtype=jnp.int32)
    query_pos = positions[first_row : first_row + query_rows]
    key_pos = padded_positions[first_row : first_row + query_rows + 2 * HALF]
    distance = query_index[:, None] - key_index[None, :]
    within_reach = jnp.abs(distance) <= HALF
    inside_block = (key_index >= 0) & (key_index < local_rows)
    same_document = query_pos[:, None] - key_pos[None, :] == distance
    left_valid = (key_index < 0) & (device > 0)
    right_valid = (key_index >= local_rows) & (device < last_device)
    return within_reach & (
        inside_block[None, :] & same_document | left_valid[None, :] | right_valid[None, :]
    )


def per_device(
    tokens,
    positions,
    cotangent,
    qkv_weight,
    attn_weight,
    mlp_weight,
    down_weight,
    norm_gains,
    qkv_first,
    qkv_second,
    attn_first,
    attn_second,
    mlp_first,
    mlp_second,
    down_first,
    down_second,
    gains_first,
    gains_second,
):
    full_qkv, full_attn, full_mlp, full_down, full_gains = (
        lax.all_gather(qkv_weight.astype(jnp.bfloat16), "shard", axis=0, tiled=True),
        lax.all_gather(attn_weight.astype(jnp.bfloat16), "shard", axis=0, tiled=True),
        lax.all_gather(mlp_weight.astype(jnp.bfloat16), "shard", axis=0, tiled=True),
        lax.all_gather(down_weight.astype(jnp.bfloat16), "shard", axis=0, tiled=True),
        lax.all_gather(norm_gains.astype(jnp.bfloat16), "shard", axis=1, tiled=True),
    )
    local_rows = tokens.shape[0]
    model_width = tokens.shape[1]
    head_size = model_width // HEADS
    score_scale = 1.0 / math.sqrt(head_size)
    block_rows = min(640, local_rows)
    device = lax.axis_index(("seq", "shard"))
    last_device = lax.axis_size(("seq", "shard")) - 1
    gain_attn = full_gains[0].astype(jnp.float32)
    gain_mlp = full_gains[1].astype(jnp.float32)
    residual = tokens.astype(jnp.float32)
    first_norm, first_norm_back = jax.vjp(layer_norm, residual, gain_attn)
    first_low = first_norm.astype(jnp.bfloat16)
    projected = jnp.dot(first_low, full_qkv, preferred_element_type=jnp.float32)
    cos_table, sin_table = rope_tables(positions, head_size)
    queries_raw = projected[:, :model_width].reshape(local_rows, HEADS, head_size)
    keys_raw = projected[:, model_width : 2 * model_width].reshape(local_rows, HEADS, head_size)
    queries = (queries_raw * cos_table + rotate_half(queries_raw) * sin_table).astype(jnp.bfloat16)
    keys_low = (
        (keys_raw * cos_table + rotate_half(keys_raw) * sin_table)
        .astype(jnp.bfloat16)
        .reshape(local_rows, model_width)
    )
    values_low = projected[:, 2 * model_width :].astype(jnp.bfloat16)
    extended = with_halo(
        jnp.concatenate([keys_low, values_low], axis=1), ((("seq", "shard"), 0),), HALF
    )
    ext_keys = extended[:, :model_width].reshape(-1, HEADS, head_size)
    ext_values = extended[:, model_width:].reshape(-1, HEADS, head_size)
    attended_parts = []
    kept_tops = []
    kept_totals = []
    kept_masks = []
    for first_row in range(0, local_rows, block_rows):
        allowed = allowed_mask(positions, first_row, block_rows, device, last_device)
        query_block = queries[first_row : first_row + block_rows]
        key_block = ext_keys[first_row : first_row + block_rows + 2 * HALF]
        value_block = ext_values[first_row : first_row + block_rows + 2 * HALF]
        scores = (
            jnp.einsum("qhd,khd->hqk", query_block, key_block, preferred_element_type=jnp.float32)
            * score_scale
        )
        masked = jnp.where(allowed[None], scores, masked_score)
        row_top = jnp.max(masked, axis=-1, keepdims=True)
        weights = jnp.exp(masked - row_top)
        row_total = jnp.sum(weights, axis=-1, keepdims=True)
        probabilities = (weights / row_total).astype(jnp.bfloat16)
        attended_parts.append(
            jnp.einsum(
                "hqk,khd->qhd", probabilities, value_block, preferred_element_type=jnp.float32
            )
        )
        kept_tops.append(row_top)
        kept_totals.append(row_total)
        kept_masks.append(allowed)
    attended = (
        jnp.concatenate(attended_parts, axis=0)
        .reshape(local_rows, model_width)
        .astype(jnp.bfloat16)
    )
    middle = residual + jnp.dot(attended, full_attn, preferred_element_type=jnp.float32)
    second_norm, second_norm_back = jax.vjp(layer_norm, middle, gain_mlp)
    second_low = second_norm.astype(jnp.bfloat16)
    expanded = jnp.dot(second_low, full_mlp, preferred_element_type=jnp.float32)
    gated_value, gated_back = jax.vjp(geglu, expanded)
    gated_low = gated_value.astype(jnp.bfloat16)
    layer_output = (
        middle + jnp.dot(gated_low, full_down, preferred_element_type=jnp.float32)
    ).astype(jnp.bfloat16)
    full_qkv, full_attn, full_mlp, full_down = (
        lax.all_gather(qkv_weight.astype(jnp.bfloat16), "shard", axis=0, tiled=True),
        lax.all_gather(attn_weight.astype(jnp.bfloat16), "shard", axis=0, tiled=True),
        lax.all_gather(mlp_weight.astype(jnp.bfloat16), "shard", axis=0, tiled=True),
        lax.all_gather(down_weight.astype(jnp.bfloat16), "shard", axis=0, tiled=True),
    )
    grad_output = cotangent.astype(jnp.float32)
    down_grad = jnp.einsum("tf,td->fd", gated_low, cotangent, preferred_element_type=jnp.float32)
    grad_gated = jnp.einsum("td,fd->tf", cotangent, full_down, preferred_element_type=jnp.float32)
    (grad_expanded,) = gated_back(grad_gated)
    expanded_low = grad_expanded.astype(jnp.bfloat16)
    mlp_grad = jnp.einsum("tc,tf->cf", second_low, expanded_low, preferred_element_type=jnp.float32)
    grad_second = jnp.einsum(
        "tf,cf->tc", expanded_low, full_mlp, preferred_element_type=jnp.float32
    )
    grad_middle_norm, gain_mlp_grad = second_norm_back(grad_second)
    grad_middle = grad_output + grad_middle_norm
    middle_low = grad_middle.astype(jnp.bfloat16)
    attn_grad = jnp.einsum("tc,td->cd", attended, middle_low, preferred_element_type=jnp.float32)
    grad_attended = (
        jnp.einsum("td,cd->tc", middle_low, full_attn, preferred_element_type=jnp.float32)
        .astype(jnp.bfloat16)
        .reshape(local_rows, HEADS, head_size)
    )
    ext_grads = jnp.zeros((local_rows + 2 * HALF, 2 * model_width), jnp.float32)
    query_grads = []
    for block_number, first_row in enumerate(range(0, local_rows, block_rows)):
        query_block = queries[first_row : first_row + block_rows]
        key_block = ext_keys[first_row : first_row + block_rows + 2 * HALF]
        value_block = ext_values[first_row : first_row + block_rows + 2 * HALF]
        grad_block = grad_attended[first_row : first_row + block_rows]
        scores = (
            jnp.einsum("qhd,khd->hqk", query_block, key_block, preferred_element_type=jnp.float32)
            * score_scale
        )
        masked = jnp.where(kept_masks[block_number][None], scores, masked_score)
        prob_exact = jnp.exp(masked - kept_tops[block_number]) / kept_totals[block_number]
        prob_low = prob_exact.astype(jnp.bfloat16)
        value_grad = jnp.einsum(
            "hqk,qhd->khd", prob_low, grad_block, preferred_element_type=jnp.float32
        )
        grad_probs = jnp.einsum(
            "qhd,khd->hqk", grad_block, value_block, preferred_element_type=jnp.float32
        )
        inner_sum = jnp.sum(prob_exact * grad_probs, axis=-1, keepdims=True)
        grad_scores = (prob_exact * (grad_probs - inner_sum)).astype(jnp.bfloat16)
        query_grads.append(
            jnp.einsum("hqk,khd->qhd", grad_scores, key_block, preferred_element_type=jnp.float32)
            * score_scale
        )
        key_grad = (
            jnp.einsum("hqk,qhd->khd", grad_scores, query_block, preferred_element_type=jnp.float32)
            * score_scale
        )
        block_grads = jnp.concatenate(
            [key_grad.reshape(-1, model_width), value_grad.reshape(-1, model_width)], axis=1
        )
        ext_grads = ext_grads.at[first_row : first_row + block_rows + 2 * HALF].add(block_grads)
    from_right = from_behind(ext_grads[:HALF].astype(jnp.bfloat16), ("seq", "shard"), -1).astype(
        jnp.float32
    )
    from_left = from_behind(
        ext_grads[local_rows + HALF :].astype(jnp.bfloat16), ("seq", "shard"), 1
    ).astype(jnp.float32)
    own_grads = ext_grads[HALF : HALF + local_rows]
    own_grads = own_grads.at[:HALF].add(from_left)
    own_grads = own_grads.at[local_rows - HALF :].add(from_right)
    key_grad_rot = own_grads[:, :model_width].reshape(local_rows, HEADS, head_size)
    value_grad_all = own_grads[:, model_width:]
    query_grad_rot = jnp.concatenate(query_grads, axis=0)
    query_raw_grad = query_grad_rot * cos_table + rotate_back(query_grad_rot * sin_table)
    key_raw_grad = key_grad_rot * cos_table + rotate_back(key_grad_rot * sin_table)
    projected_grad = jnp.concatenate(
        [
            query_raw_grad.reshape(local_rows, model_width),
            key_raw_grad.reshape(local_rows, model_width),
            value_grad_all,
        ],
        axis=1,
    ).astype(jnp.bfloat16)
    qkv_grad = jnp.einsum(
        "tc,te->ce", first_low, projected_grad, preferred_element_type=jnp.float32
    )
    grad_first = jnp.einsum(
        "te,ce->tc", projected_grad, full_qkv, preferred_element_type=jnp.float32
    )
    grad_residual_norm, gain_attn_grad = first_norm_back(grad_first)
    input_grad = (grad_middle + grad_residual_norm).astype(jnp.bfloat16)
    gains_grad = jnp.stack([gain_attn_grad, gain_mlp_grad])
    qkv_owned, attn_owned, mlp_owned, down_owned, gains_owned = (
        lax.psum_scatter(
            qkv_grad.astype(jnp.bfloat16), "shard", scatter_dimension=0, tiled=True
        ).astype(jnp.float32),
        lax.psum_scatter(
            attn_grad.astype(jnp.bfloat16), "shard", scatter_dimension=0, tiled=True
        ).astype(jnp.float32),
        lax.psum_scatter(
            mlp_grad.astype(jnp.bfloat16), "shard", scatter_dimension=0, tiled=True
        ).astype(jnp.float32),
        lax.psum_scatter(
            down_grad.astype(jnp.bfloat16), "shard", scatter_dimension=0, tiled=True
        ).astype(jnp.float32),
        lax.psum_scatter(
            gains_grad.astype(jnp.bfloat16), "shard", scatter_dimension=1, tiled=True
        ).astype(jnp.float32),
    )
    qkv_total, attn_total, mlp_total, down_total, gains_total = lax.psum(
        (qkv_owned, attn_owned, mlp_owned, down_owned, gains_owned), "seq"
    )
    qkv_first_new, qkv_second_new, qkv_new = adam_update(
        qkv_weight, qkv_first, qkv_second, qkv_total, rate_matrix
    )
    attn_first_new, attn_second_new, attn_new = adam_update(
        attn_weight, attn_first, attn_second, attn_total, rate_matrix
    )
    mlp_first_new, mlp_second_new, mlp_new = adam_update(
        mlp_weight, mlp_first, mlp_second, mlp_total, rate_matrix
    )
    down_first_new, down_second_new, down_new = adam_update(
        down_weight, down_first, down_second, down_total, rate_matrix
    )
    gains_first_new, gains_second_new, gains_new = adam_update(
        norm_gains, gains_first, gains_second, gains_total, rate_gains
    )
    return (
        layer_output,
        input_grad,
        qkv_first_new,
        qkv_second_new,
        qkv_new,
        attn_first_new,
        attn_second_new,
        attn_new,
        mlp_first_new,
        mlp_second_new,
        mlp_new,
        down_first_new,
        down_second_new,
        down_new,
        gains_first_new,
        gains_second_new,
        gains_new,
    )


def solution(mesh):
    return jax.shard_map(
        per_device,
        mesh=mesh,
        in_specs=(
            P(("seq", "shard"), None),
            P(("seq", "shard")),
            P(("seq", "shard"), None),
            P("shard", None),
            P("shard", None),
            P("shard", None),
            P("shard", None),
            P(None, "shard"),
            P("shard", None),
            P("shard", None),
            P("shard", None),
            P("shard", None),
            P("shard", None),
            P("shard", None),
            P("shard", None),
            P("shard", None),
            P(None, "shard"),
            P(None, "shard"),
        ),
        out_specs=(
            P(("seq", "shard"), None),
            P(("seq", "shard"), None),
            P("shard", None),
            P("shard", None),
            P("shard", None),
            P("shard", None),
            P("shard", None),
            P("shard", None),
            P("shard", None),
            P("shard", None),
            P("shard", None),
            P("shard", None),
            P("shard", None),
            P("shard", None),
            P(None, "shard"),
            P(None, "shard"),
            P(None, "shard"),
        ),
        check_vma=False,
    )
```

profile of v0, /device:TPU:0, one launch (start us, length us, event | category | flops | bytes accessed | tf_op | source)
XLA Modules:
  0.0 814.7 jit_solution(18286915668300180959)
XLA Ops:
  13.1 12.7 %all-gather = bf16[4,192,2]{1,2,0:T(2,128)(2,1)S(1)} all-gather(bf16[1,192,2]{1,2,0:T(2,128)(2,1)S(1)} %convert_bitcast_fusion), channel_id=1, replica_groups=mesh['seq'=8,'shard'=4] {'shard'}, dimensions={0}, use_global_device_ids=true | all-gather | bytes 3840 | tf_op jit(solution)/shard_map/all_gather | solution.py:131
  46.3 36.7 %all-gather.6.cloned.1.call-done = bf16[768,2304]{1,0:T(8,128)(2,1)} async-done(((bf16[192,2304]{1,0:T(8,128)(2,1)}), bf16[768,2304]{1,0:T(8,128)(2,1)}) %all-gather.6.cloned.1.call-update) | async-done | bytes 3538960 | tf_op jit(solution)/shard_map/all_gather | solution.py:127
  82.9 7.0 fusion.93
  112.6 8.9 %fusion.130 = (f32[1280,768]{1,0:T(8,128)}, bf16[1280,768]{1,0:T(8,128)(2,1)}) fusion(f32[1280,2304]{1,0:T(8,128)} %copy-done.10, f32[1280,768]{1,0:T(8,128)} %copy.82, f32[1280,768]{1,0:T(8,128)} %copy.80), kind=kLoop, calls=%fused_computation.222 | loop fusion | flops 2949120 | bytes 21626880 | tf_op jit(solution)/shard_map/slice | solution.py:147
  139.2 12.9 %collective-permute-done.1 = bf16[64,1536]{1,0:T(8,128)(2,1)S(1)} collective-permute-done((bf16[64,1536]{1,0:T(8,128)(2,1)S(1)}, bf16[64,1536]{1,0:T(8,128)(2,1)S(1)}, u32[]{:S(2)}, u32[]{:S(2)}) %collective-permute-start.1) | collective-permute-done | bytes 196640 | tf_op jit(solution)/shard_map/ppermute | solution.py:34
  165.2 14.4 %fusion.135 = (f32[12,640]{1,0:T(8,128)S(1)}, f32[12,640,768]{2,1,0:T(8,128)}) fusion(pred[640,768]{1,0:T(8,128)(4,1)} %get-tuple-element.195, bf16[768,12,64]{0,2,1:T(8,128)(2,1)} %bitcast.101, bf16[1280,12,64]{0,2,1:T(8,128)(2,1)} %fusion.40), kind=kOutput, calls=%fused_computation.227 | convolution fusion | flops 778568448 | bytes 26277888 | tf_op jit(solution)/shard_map/sub | solution.py:176
  179.6 14.1 %fusion.140 = (f32[12,640]{1,0:T(8,128)S(1)}, f32[12,640,768]{2,1,0:T(8,128)}) fusion(pred[640,768]{1,0:T(8,128)(4,1)} %get-tuple-element.194, bf16[768,12,64]{0,2,1:T(8,128)(2,1)S(1)} %bitcast.99, bf16[1280,12,64]{0,2,1:T(8,128)(2,1)} %fusion.40), kind=kOutput, calls=%fused_computation.228 | convolution fusion | flops 778568448 | bytes 26277888 | tf_op jit(solution)/shard_map/sub | solution.py:176
  193.7 10.8 %fusion.64 = bf16[640,12,64]{0,2,1:T(8,128)(2,1)S(1)} fusion(bf16[768,12,64]{0,2,1:T(8,128)(2,1)} %bitcast.109, f32[12,640,768]{2,1,0:T(8,128)} %get-tuple-element.181, f32[12,640]{1,0:T(8,128)S(1)} %get-tuple-element.180), kind=kOutput, calls=%fused_computation.134 | convolution fusion | flops 767262720 | bytes 25786368 | tf_op jit(solution)/shard_map/hqk,khd->qhd/dot_general | solution.py:180
  204.6 9.8 %fusion.67 = bf16[640,12,64]{0,2,1:T(8,128)(2,1)S(1)} fusion(bf16[768,12,64]{0,2,1:T(8,128)(2,1)S(1)} %bitcast.107, f32[12,640,768]{2,1,0:T(8,128)} %get-tuple-element.183, f32[12,640]{1,0:T(8,128)S(1)} %get-tuple-element.182), kind=kOutput, calls=%fused_computation.135 | convolution fusion | flops 767262720 | bytes 25786368 | tf_op jit(solution)/shard_map/hqk,khd->qhd/dot_general | solution.py:180
  222.0 12.6 %fusion.122 = f32[1280,2304]{1,0:T(8,128)} fusion(bf16[768,2304]{1,0:T(8,128)(2,1)} %all-gather.10.cloned.1.call-done, f32[1280,768]{0,1:T(8,128)} %copy-done.12, f32[768]{0:T(1024)S(1)} %get-tuple-element.120, f32[1280]{0:T(1024)S(1)} %fusion.96, f32[1280]{0:T(1024)S(1)} %broadcast_multiply_fusion.2), kind=kOutput, calls=%fused_computation.220 | convolution fusion | flops 4533780480 | bytes 19280896 | tf_op jit(solution)/shard_map/dot_general | solution.py:195
  234.7 19.5 %fusion.55 = (f32[1280,1152]{1,0:T(8,128)}, f32[1280,1152]{1,0:T(8,128)}, f32[1280,1152]{1,0:T(8,128)}) fusion(f32[1280,2304]{1,0:T(8,128)} %fusion.122, bf16[1280,768]{1,0:T(8,128)(2,1)S(1)} %copy-done.32, bf16[1152,768]{1,0:T(8,128)(2,1)} %all-gather.12.cloned.1.call-done), kind=kOutput, calls=%fused_computation.120 | convolution fusion | flops 2360770560 | bytes 27328512 | tf_op jit(solution)/shard_map/td,fd->tf/dot_general | solution.py:209
  254.2 8.3 %multiply_add_fusion = (f32[1280,1152]{1,0:T(8,128)}, bf16[1280,1152]{1,0:T(8,128)(2,1)}) fusion(f32[1280,1152]{1,0:T(8,128)} %get-tuple-element.147, f32[1280,1152]{1,0:T(8,128)} %get-tuple-element.186, f32[1280,2304]{1,0:T(8,128)S(1)} %copy-done.15), kind=kLoop, calls=%fused_computation.28 | loop fusion | flops 25067520 | bytes 32440320 | tf_op jit(solution)/shard_map/transpose(jvp())/add_any | solution.py:74
  262.5 10.7 %multiply_reduce_fusion.2 = (bf16[768]{0:T(1024)(128)(2,1)}, f32[1280]{0:T(1024)S(1)}, f32[1280,768]{0,1:T(8,128)S(1)}) fusion(f32[1280,768]{0,1:T(8,128)S(1)} %copy-done.13, f32[1280]{0:T(1024)S(1)} %fusion.96, f32[1280]{0:T(1024)S(1)} %broadcast_multiply_fusion.2, f32[768]{0:T(1024)S(1)} %get-tuple-element.120, ...), kind=kOutput, calls=%fused_computation.86 | convolution fusion | flops 4542625792 | bytes 23219712 | tf_op jit(solution)/shard_map/tf,cf->tc/dot_general | solution.py:213
  279.7 10.7 %fusion.16 = f32[12,64,768]{2,1,0:T(8,128)} fusion(bf16[640,12,64]{0,2,1:T(8,128)(2,1)S(1)} %bitcast.113, f32[12,640,768]{2,1,0:T(8,128)} %get-tuple-element.181, f32[12,640]{1,0:T(8,128)S(1)} %get-tuple-element.180), kind=kOutput, calls=%fused_computation.42 | convolution fusion | flops 766771200 | bytes 26966016 | tf_op jit(solution)/shard_map/hqk,qhd->khd/dot_general | solution.py:239
  290.4 18.1 %multiply_reduce_fusion = (f32[12,640]{1,0:T(8,128)S(1)}, f32[12,640,768]{2,1,0:T(8,128)}) fusion(f32[12,640,768]{2,1,0:T(8,128)} %get-tuple-element.181, f32[12,640]{1,0:T(8,128)S(1)} %get-tuple-element.180, bf16[640,12,64]{0,2,1:T(8,128)(2,1)S(1)} %bitcast.114, bf16[768,12,64]{0,2,1:T(8,128)(2,1)S(1)} %bitcast.110), kind=kOutput, calls=%fused_computation.3 | convolution fusion | flops 772661760 | bytes 49410048 | tf_op jit(solution)/shard_map/qhd,khd->hqk/dot_general | solution.py:242
  308.5 15.5 %multiply_convert_fusion = bf16[12,640,768]{2,1,0:T(8,128)(2,1)S(1)} fusion(f32[12,640,768]{2,1,0:T(8,128)} %get-tuple-element.191, f32[12,640]{1,0:T(8,128)S(1)} %get-tuple-element.190, f32[12,640,768]{2,1,0:T(8,128)} %get-tuple-element.181, f32[12,640]{1,0:T(8,128)S(1)} %get-tuple-element.180), kind=kLoop, calls=%fused_computation.2 | loop fusion | flops 23592960 | bytes 59043840 | tf_op jit(solution)/shard_map/convert_element_type | solution.py:246
  333.2 10.5 %fusion.20 = f32[12,64,768]{2,1,0:T(8,128)} fusion(bf16[640,12,64]{0,2,1:T(8,128)(2,1)S(1)} %bitcast.112, f32[12,640,768]{2,1,0:T(8,128)} %get-tuple-element.183, f32[12,640]{1,0:T(8,128)S(1)} %copy-done.58), kind=kOutput, calls=%fused_computation.46 | convolution fusion | flops 766771200 | bytes 26966016 | tf_op jit(solution)/shard_map/hqk,qhd->khd/dot_general | solution.py:239
  343.7 15.4 %multiply_reduce_fusion.1 = (f32[12,640]{1,0:T(8,128)S(1)}, f32[12,640,768]{2,1,0:T(8,128)}) fusion(f32[12,640,768]{2,1,0:T(8,128)} %get-tuple-element.183, f32[12,640]{1,0:T(8,128)S(1)} %copy-done.58, bf16[640,12,64]{0,2,1:T(8,128)(2,1)} %bitcast.111, bf16[768,12,64]{0,2,1:T(8,128)(2,1)S(1)} %bitcast.108), kind=kOutput, calls=%fused_computation.5 | convolution fusion | flops 772661760 | bytes 49410048 | tf_op jit(solution)/shard_map/qhd,khd->hqk/dot_general | solution.py:242
  359.2 15.9 %multiply_convert_fusion.1 = bf16[12,640,768]{2,1,0:T(8,128)(2,1)S(1)} fusion(f32[12,640,768]{2,1,0:T(8,128)} %get-tuple-element.189, f32[12,640]{1,0:T(8,128)S(1)} %get-tuple-element.188, f32[12,640,768]{2,1,0:T(8,128)} %get-tuple-element.183, f32[12,640]{1,0:T(8,128)S(1)} %copy-done.58), kind=kLoop, calls=%fused_computation.4 | loop fusion | flops 23592960 | bytes 59043840 | tf_op jit(solution)/shard_map/convert_element_type | solution.py:246
  381.4 6.9 constant_dynamic-update-slice_fusion
  398.9 8.7 %slice.276 = f32[1280,1536]{0,1:T(8,128)} slice(f32[1408,1536]{0,1:T(8,128)} %get-tuple-element.142), slice={[64:1344], [0:1536]} | slice | bytes 15728640 | tf_op jit(solution)/shard_map/slice | solution.py:265
  437.6 7.8 fusion.42
  445.4 8.9 %fusion.38 = (f32[1280]{0:T(1024)S(1)}, f32[1280,768]{0,1:T(8,128)S(1)}) fusion(bf16[1280,768]{0,1:T(8,128)(2,1)S(1)} %copy-done.1, f32[768]{0:T(1024)S(1)} %copy-done.60, f32[1280]{0:T(1024)S(1)} %copy-done.47, bf16[768,2304]{1,0:T(8,128)(2,1)} %all-gather.6.cloned.1.call-done, bf16[1280,768]{0,1:T(8,128)(2,1)} %slice.342, ...), kind=kOutput, calls=%fused_computation.70 | convolution fusion | flops 4552457216 | bytes 15348736 | tf_op jit(solution)/shard_map/te,ce->tc/dot_general | solution.py:284
  463.8 6.2 convolution_convert_fusion.2
  470.2 12.3 %convolution_convert_fusion = bf16[768,2304]{1,0:T(8,128)(2,1)} fusion(f32[1280,1152]{1,0:T(8,128)} %get-tuple-element.148, f32[1280,1152]{1,0:T(8,128)} %get-tuple-element.146, f32[1280,768]{0,1:T(8,128)} %copy-done.12, f32[768]{0:T(1024)S(1)} %copy-done.64, f32[1280]{0:T(1024)S(1)} %copy-done.62, f32[1280]{0:T(1024)S(1)} %copy-done.56), kind=kOutput, calls=%fused_computation.60 | convolution fusion | flops 4541448192 | bytes 19280896 | tf_op jit(solution)/shard_map/tc,tf->cf/dot_general | solution.py:212
  482.7 9.5 %convolution_convert_fusion.1 = bf16[768,2304]{1,0:T(8,128)(2,1)} fusion(bf16[1280,768]{0,1:T(8,128)(2,1)} %slice.342, bf16[1280,768]{0,1:T(8,128)(2,1)} %get-tuple-element.171, bf16[1280,768]{0,1:T(8,128)(2,1)} %get-tuple-element.170, bf16[1280,768]{0,1:T(8,128)(2,1)S(1)} %copy-done.1, f32[768]{0:T(1024)S(1)} %copy-done.60, f32[1280]{0:T(1024)S(1)} %copy-done.52, ...), kind=kOutput, calls=%fused_computation.61 | convolution fusion | flops 4554227712 | bytes 11416576 | tf_op jit(solution)/shard_map/tc,te->ce/dot_general | solution.py:281
  492.2 7.6 add_convert_fusion.2
  503.8 5.8 add_convert_fusion.1
  514.6 36.6 %reduce-scatter.14.cloned.1.call-done = bf16[288,768]{1,0:T(8,128)(2,1)} async-done(((bf16[1152,768]{1,0:T(8,128)(2,1)}), bf16[288,768]{1,0:T(8,128)(2,1)}) %reduce-scatter.14.cloned.1.call-update) | async-done | bytes 442384 | tf_op jit(solution)/shard_map/reduce_scatter | solution.py:300
  551.2 67.8 %reduce-scatter.12.cloned.1.call-done = bf16[192,2304]{1,0:T(8,128)(2,1)} async-done(((bf16[768,2304]{1,0:T(8,128)(2,1)}), bf16[192,2304]{1,0:T(8,128)(2,1)}) %reduce-scatter.12.cloned.1.call-update) | async-done | bytes 884752 | tf_op jit(solution)/shard_map/reduce_scatter | solution.py:297
  619.0 69.0 %reduce-scatter.8.cloned.1.call-done = bf16[192,2304]{1,0:T(8,128)(2,1)} async-done(((bf16[768,2304]{1,0:T(8,128)(2,1)}), bf16[192,2304]{1,0:T(8,128)(2,1)}) %reduce-scatter.8.cloned.1.call-update) | async-done | bytes 884752 | tf_op jit(solution)/shard_map/reduce_scatter | solution.py:291
  688.0 104.7 %all-reduce.6 = (f32[192,2304]{1,0:T(8,128)}, f32[192,768]{1,0:T(8,128)}, f32[192,2304]{1,0:T(8,128)S(1)}, f32[288,768]{1,0:T(8,128)}, f32[2,192]{1,0:T(2,128)S(1)}) all-reduce(bf16[192,2304]{1,0:T(8,128)(2,1)} %reduce-scatter.8.cloned.1.call-done, ...), channel_id=1, replica_groups=mesh['seq'=8,'shard'=4] {'seq'}, use_global_device_ids=true, to_apply=%region_15.16 | all-reduce | flops 1253760 | bytes 7522560 | tf_op jit(solution)/shard_map/psum | solution.py:307
  (264 shorter events, 183.1 us)
Async XLA Ops:
  7.2 75.7 %all-gather.6.cloned.1.call-start = ((), (), s32[]{:S(2)}) async-start(), calls=%async_computation.5 | async-start | bytes 4423680 | tf_op jit(solution)/shard_map/all_gather | solution.py:127
  9.9 205.9 %all-gather.8.cloned.1.call-start = ((), (), s32[]{:S(2)}) async-start(), calls=%async_computation.6 | async-start | bytes 1474560 | tf_op jit(solution)/shard_map/all_gather | solution.py:128
  10.8 211.3 %all-gather.10.cloned.1.call-start = ((), (), s32[]{:S(2)}) async-start(), calls=%async_computation.7 | async-start | bytes 4423680 | tf_op jit(solution)/shard_map/all_gather | solution.py:129
  11.9 222.8 %all-gather.12.cloned.1.call-start = ((), (), s32[]{:S(2)}) async-start(), calls=%async_computation.8 | async-start | bytes 2211840 | tf_op jit(solution)/shard_map/all_gather | solution.py:130
  12.7 500.9 %reduce-scatter.16.cloned.1.call-start = ((), (), s32[]{:S(2)}) async-start(), calls=%async_computation.13 | async-start | bytes 245760
  25.9 57.0 %copy-start.59 = (f32[768]{0:T(1024)}, f32[768]{0:T(1024)S(1)}, u32[]{:S(2)}) copy-start(f32[768]{0:T(1024)S(1)} %get-tuple-element.121) | copy-start | bytes 9220
  25.9 247.3 %copy-start.63 = (f32[768]{0:T(1024)}, f32[768]{0:T(1024)S(1)}, u32[]{:S(2)}) copy-start(f32[768]{0:T(1024)S(1)} %get-tuple-element.120) | copy-start | bytes 9220
  27.2 104.5 %copy-start.20 = (f32[1280,64]{0,1:T(8,128)}, f32[1280,64]{0,1:T(8,128)S(1)}, u32[]{:S(2)}) copy-start(f32[1280,64]{0,1:T(8,128)S(1)} %get-tuple-element.174) | copy-start | bytes 983044
  27.2 104.5 %copy-start.22 = (f32[1280,64]{0,1:T(8,128)}, f32[1280,64]{0,1:T(8,128)S(1)}, u32[]{:S(2)}) copy-start(f32[1280,64]{0,1:T(8,128)S(1)} %get-tuple-element.175) | copy-start | bytes 983044
  30.2 185.7 %copy-start = (bf16[1280,768]{0,1:T(8,128)(2,1)}, bf16[1280,768]{0,1:T(8,128)(2,1)S(1)}, u32[]{:S(2)}) copy-start(bf16[1280,768]{0,1:T(8,128)(2,1)S(1)} %copy.78) | copy-start | bytes 5898244
  30.5 52.4 %copy-start.46 = (f32[1280]{0:T(1024)}, f32[1280]{0:T(1024)S(1)}, u32[]{:S(2)}) copy-start(f32[1280]{0:T(1024)S(1)} %broadcast_multiply_fusion.3) | copy-start | bytes 15364
  31.7 51.3 %copy-start.51 = (f32[1280]{0:T(1024)}, f32[1280]{0:T(1024)S(1)}, u32[]{:S(2)}) copy-start(f32[1280]{0:T(1024)S(1)} %fusion.95) | copy-start | bytes 15364
  128.4 10.9 %collective-permute-start = (bf16[64,1536]{1,0:T(8,128)(2,1)S(1)}, bf16[64,1536]{1,0:T(8,128)(2,1)S(1)}, u32[]{:S(2)}, u32[]{:S(2)}) collective-permute-start(bf16[64,1536]{1,0:T(8,128)(2,1)S(1)} %get-tuple-element.162), channel_id=1, source_target_pairs={{0,1},{1,2},{2,3},{3,4},{4,5},{5,6},{6,7},{7,8},{8,9},{9,10},{10,1... | collective-permute-start | bytes 589832 | tf_op jit(solution)/shard_map/ppermute | solution.py:32
  129.8 22.4 %collective-permute-start.1 = (bf16[64,1536]{1,0:T(8,128)(2,1)S(1)}, bf16[64,1536]{1,0:T(8,128)(2,1)S(1)}, u32[]{:S(2)}, u32[]{:S(2)}) collective-permute-start(bf16[64,1536]{1,0:T(8,128)(2,1)S(1)} %get-tuple-element.163), channel_id=1, source_target_pairs={{1,0},{2,1},{3,2},{4,3},{5,4},{6,5},{7,6},{8,7},{9,8},{10,9},{11,1... | collective-permute-start | bytes 589832 | tf_op jit(solution)/shard_map/ppermute | solution.py:34
  131.7 20.4 %copy-start.5 = (bf16[1280,768]{1,0:T(8,128)(2,1)S(1)}, bf16[1280,768]{1,0:T(8,128)(2,1)}, u32[]{:S(2)}) copy-start(bf16[1280,768]{1,0:T(8,128)(2,1)} %slice.343) | copy-start | bytes 5898244
  131.8 20.4 %copy-start.9 = (bf16[1280,768]{1,0:T(8,128)(2,1)S(1)}, bf16[1280,768]{1,0:T(8,128)(2,1)}, u32[]{:S(2)}) copy-start(bf16[1280,768]{1,0:T(8,128)(2,1)} %get-tuple-element.151) | copy-start | bytes 5898244
  157.7 22.0 %copy-start.24 = (bf16[768,768]{0,1:T(8,128)(2,1)}, bf16[768,768]{0,1:T(8,128)(2,1)S(1)}, u32[]{:S(2)}) copy-start(bf16[768,768]{0,1:T(8,128)(2,1)S(1)} %copy.85) | copy-start | bytes 3538948
  219.7 53.6 %copy-start.55 = (f32[1280]{0:T(1024)}, f32[1280]{0:T(1024)S(1)}, u32[]{:S(2)}) copy-start(f32[1280]{0:T(1024)S(1)} %broadcast_multiply_fusion.2) | copy-start | bytes 15364
  222.0 51.2 %copy-start.61 = (f32[1280]{0:T(1024)}, f32[1280]{0:T(1024)S(1)}, u32[]{:S(2)}) copy-start(f32[1280]{0:T(1024)S(1)} %fusion.96) | copy-start | bytes 15364
  234.7 19.5 %copy-start.15 = (f32[1280,2304]{1,0:T(8,128)S(1)}, f32[1280,2304]{1,0:T(8,128)}, u32[]{:S(2)}) copy-start(f32[1280,2304]{1,0:T(8,128)} %fusion.122) | copy-start | bytes 35389444
  327.6 103.3 %copy-start.6 = (f32[12,64,640]{2,1,0:T(8,128)}, f32[12,64,640]{2,1,0:T(8,128)S(1)}, u32[]{:S(2)}) copy-start(f32[12,64,640]{2,1,0:T(8,128)S(1)} %convolution_multiply_fusion.2) | copy-start | bytes 5898244
  389.4 19.5 %collective-permute-start.2 = (bf16[64,1536]{0,1:T(8,128)(2,1)S(1)}, bf16[64,1536]{0,1:T(8,128)(2,1)S(1)}, u32[]{:S(2)}, u32[]{:S(2)}) collective-permute-start(bf16[64,1536]{0,1:T(8,128)(2,1)S(1)} %slice.345), channel_id=1, source_target_pairs={{0,1},{1,2},{2,3},{3,4},{4,5},{5,6},{6,7},{7,8},{8,9},{9,10},{10,1... | collective-permute-start | bytes 589832 | tf_op jit(solution)/shard_map/ppermute | solution.py:44
  407.6 11.3 %collective-permute-start.3 = (bf16[64,1536]{0,1:T(8,128)(2,1)S(1)}, bf16[64,1536]{0,1:T(8,128)(2,1)S(1)}, u32[]{:S(2)}, u32[]{:S(2)}) collective-permute-start(bf16[64,1536]{0,1:T(8,128)(2,1)S(1)} %slice.344), channel_id=1, source_target_pairs={{1,0},{2,1},{3,2},{4,3},{5,4},{6,5},{7,6},{8,7},{9,8},{10,9},{11,1... | collective-permute-start | bytes 589832 | tf_op jit(solution)/shard_map/ppermute | solution.py:44
  458.7 55.9 %reduce-scatter.10.cloned.1.call-start = ((), (), s32[]{:S(2)}) async-start(), calls=%async_computation.10 | async-start | bytes 1474560 | tf_op jit(solution)/shard_map/reduce_scatter | solution.py:294
  463.7 87.5 %reduce-scatter.14.cloned.1.call-start = ((), (), s32[]{:S(2)}) async-start(), calls=%async_computation.12 | async-start | bytes 2211840 | tf_op jit(solution)/shard_map/reduce_scatter | solution.py:300
  469.9 149.1 %reduce-scatter.12.cloned.1.call-start = ((), (), s32[]{:S(2)}) async-start(), calls=%async_computation.11 | async-start | bytes 4423680 | tf_op jit(solution)/shard_map/reduce_scatter | solution.py:297
  482.6 205.4 %reduce-scatter.8.cloned.1.call-start = ((), (), s32[]{:S(2)}) async-start(), calls=%async_computation.9 | async-start | bytes 4423680 | tf_op jit(solution)/shard_map/reduce_scatter | solution.py:291
  509.6 283.1 %copy-start.66 = (f32[2,192]{1,0:T(2,128)S(1)}, f32[2,192]{1,0:T(2,128)}, u32[]{:S(2)}) copy-start(f32[2,192]{1,0:T(2,128)} %param.33) | copy-start | bytes 4612
  509.6 283.1 %copy-start.67 = (f32[2,192]{1,0:T(2,128)S(1)}, f32[2,192]{1,0:T(2,128)}, u32[]{:S(2)}) copy-start(f32[2,192]{1,0:T(2,128)} %param.43) | copy-start | bytes 4612
  509.6 283.1 %copy-start.68 = (f32[2,192]{1,0:T(2,128)S(1)}, f32[2,192]{1,0:T(2,128)}, u32[]{:S(2)}) copy-start(f32[2,192]{1,0:T(2,128)} %param.42) | copy-start | bytes 4612
  509.6 283.7 %copy-start.31 = (f32[192,768]{1,0:T(8,128)S(1)}, f32[192,768]{1,0:T(8,128)}, u32[]{:S(2)}) copy-start(f32[192,768]{1,0:T(8,128)} %param.30) | copy-start | bytes 1769476
  513.7 282.7 %copy-start.28 = (f32[288,768]{1,0:T(8,128)S(1)}, f32[288,768]{1,0:T(8,128)}, u32[]{:S(2)}) copy-start(f32[288,768]{1,0:T(8,128)} %param.32) | copy-start | bytes 2654212
  (52 other events, 283.8 us)
Sparse Core Ops, SparseCore 0:
  10.2 72.6 all-gather.5
  84.5 29.0 all-gather.7
  115.7 77.3 all-gather.9
  195.1 38.8 all-gather.11
  458.8 21.9 reduce-scatter.15
  483.7 27.3 reduce-scatter.9
  514.1 37.0 reduce-scatter.13
  553.5 65.4 reduce-scatter.11
  621.3 66.6 reduce-scatter.7
where the time goes:
time: 825 us; the launch traced here: 815 us
  waiting for transfers between devices  232 us (28%)
  matrix products  225 us (27%)
  other arithmetic  122 us (15%)
  blocking collectives  117 us (14%)
  local copies, waits for them, and re-layouts  94.7 us (11%)
  between operations  15.2 us (2%)
  starting transfers between devices  8.26 us (1%)
    psum x1, blocking collectives, per_device(): lax.psum((qkv_owned, attn_owned, mlp_owned, down_owned, gains_owned), 'seq')  105 us
    reduce_scatter x1, waiting for transfers between devices, per_device(): lax.psum_scatter(qkv_grad.astype(jnp.bfloat16), 'shard', scatter_dimensio...  69 us
    reduce_scatter x1, waiting for transfers between devices, per_device(): lax.psum_scatter(mlp_grad.astype(jnp.bfloat16), 'shard', scatter_dimensio...  67.8 us
    all_gather x1, waiting for transfers between devices, per_device(): lax.all_gather(qkv_weight.astype(jnp.bfloat16), 'shard', axis=0, tiled=True)  36.7 us
    reduce_scatter x1, waiting for transfers between devices, per_device(): lax.psum_scatter(down_grad.astype(jnp.bfloat16), 'shard', scatter_dimensi...  36.6 us
    dot_general x2, matrix products, per_device(): jnp.einsum('qhd,khd->hqk', grad_block, value_block, preferred_element_typ...  33.5 us
    convert_element_type x2, other arithmetic, per_device(): grad_scores = (prob_exact * (grad_probs - inner_sum)).astype(jnp.bfloat16)  31.4 us
    unnamed x149, local copies, waits for them, and re-layouts  29.7 us
  transfers between devices with their start and end apart: 13, of which 7 were waited for; matrix products, arithmetic and copies ran while one was open for 27% of the time, Pallas kernels for 0%

commit v1 on v0

--- a/solution.py
+++ b/solution.py
@@ -36,6 +36,52 @@
             axis=dim,
         )
     return cells
+
+
+def gather_weight(weight, two_steps):
+    count = lax.axis_size("seq")
+    low = weight.astype(jnp.bfloat16)
+    if weight.shape[0] % count:
+        return lax.all_gather(low, "shard", axis=0, tiled=True)
+    rows = weight.shape[0] // count
+    part = lax.dynamic_slice_in_dim(weight, lax.axis_index("seq") * rows, rows, 0)
+    part = part.astype(jnp.bfloat16)
+    padded = -(-rows // 8) * 8
+    part = jnp.pad(part, ((0, padded - rows), (0, 0)))
+    if two_steps:
+        part = lax.all_gather(part, "shard", axis=0, tiled=False)
+        full = lax.all_gather(part, "seq", axis=1, tiled=False)
+    else:
+        full = lax.all_gather(part, ("shard", "seq"), axis=0, tiled=False)
+    full = full.reshape(-1, padded, weight.shape[1])[:, :rows]
+    return full.reshape(-1, weight.shape[1])
+
+
+def reduce_grad(grad, two_steps):
+    count = lax.axis_size("seq")
+    shards = lax.axis_size("shard")
+    low = grad.astype(jnp.bfloat16)
+    if grad.shape[0] % (count * shards):
+        owned = lax.psum_scatter(low, "shard", scatter_dimension=0, tiled=True)
+        return lax.psum(owned.astype(jnp.float32), "seq")
+    rows = grad.shape[0] // (count * shards)
+    padded = -(-rows // 8) * 8
+    low = jnp.pad(low.reshape(-1, rows, grad.shape[1]), ((0, 0), (0, padded - rows), (0, 0)))
+    if two_steps:
+        low = low.reshape(shards, count * padded, grad.shape[1])
+        owned = lax.psum_scatter(low, "seq", scatter_dimension=1, tiled=True)
+        owned = lax.psum_scatter(owned, "shard", scatter_dimension=0, tiled=False)
+    else:
+        low = low.reshape(-1, grad.shape[1])
+        owned = lax.psum_scatter(low, ("shard", "seq"), scatter_dimension=0, tiled=True)
+    total = lax.all_gather(owned, "seq", axis=0, tiled=False)
+    return total[:, :rows].reshape(-1, grad.shape[1]).astype(jnp.float32)
+
+
+def reduce_gains(grad):
+    total = lax.psum(grad, ("seq", "shard"))
+    columns = grad.shape[1] // lax.axis_size("shard")
+    return lax.dynamic_slice_in_dim(total, lax.axis_index("shard") * columns, columns, 1)
 
 
 def from_behind(value, axis, steps):
@@ -123,13 +169,13 @@
     gains_first,
     gains_second,
 ):
-    full_qkv, full_attn, full_mlp, full_down, full_gains = (
-        lax.all_gather(qkv_weight.astype(jnp.bfloat16), "shard", axis=0, tiled=True),
-        lax.all_gather(attn_weight.astype(jnp.bfloat16), "shard", axis=0, tiled=True),
-        lax.all_gather(mlp_weight.astype(jnp.bfloat16), "shard", axis=0, tiled=True),
-        lax.all_gather(down_weight.astype(jnp.bfloat16), "shard", axis=0, tiled=True),
-        lax.all_gather(norm_gains.astype(jnp.bfloat16), "shard", axis=1, tiled=True),
-    )
+    full_qkv, full_attn, full_mlp, full_down = (
+        gather_weight(qkv_weight, False),
+        gather_weight(attn_weight, False),
+        gather_weight(mlp_weight, True),
+        gather_weight(down_weight, False),
+    )
+    full_gains = lax.all_gather(norm_gains.astype(jnp.bfloat16), "shard", axis=1, tiled=True)
     local_rows = tokens.shape[0]
     model_width = tokens.shape[1]
     head_size = model_width // HEADS
@@ -198,12 +244,6 @@
     layer_output = (
         middle + jnp.dot(gated_low, full_down, preferred_element_type=jnp.float32)
     ).astype(jnp.bfloat16)
-    full_qkv, full_attn, full_mlp, full_down = (
-        lax.all_gather(qkv_weight.astype(jnp.bfloat16), "shard", axis=0, tiled=True),
-        lax.all_gather(attn_weight.astype(jnp.bfloat16), "shard", axis=0, tiled=True),
-        lax.all_gather(mlp_weight.astype(jnp.bfloat16), "shard", axis=0, tiled=True),
-        lax.all_gather(down_weight.astype(jnp.bfloat16), "shard", axis=0, tiled=True),
-    )
     grad_output = cotangent.astype(jnp.float32)
     down_grad = jnp.einsum("tf,td->fd", gated_low, cotangent, preferred_element_type=jnp.float32)
     grad_gated = jnp.einsum("td,fd->tf", cotangent, full_down, preferred_element_type=jnp.float32)
@@ -287,26 +327,11 @@
     grad_residual_norm, gain_attn_grad = first_norm_back(grad_first)
     input_grad = (grad_middle + grad_residual_norm).astype(jnp.bfloat16)
     gains_grad = jnp.stack([gain_attn_grad, gain_mlp_grad])
-    qkv_owned, attn_owned, mlp_owned, down_owned, gains_owned = (
-        lax.psum_scatter(
-            qkv_grad.astype(jnp.bfloat16), "shard", scatter_dimension=0, tiled=True
-        ).astype(jnp.float32),
-        lax.psum_scatter(
-            attn_grad.astype(jnp.bfloat16), "shard", scatter_dimension=0, tiled=True
-        ).astype(jnp.float32),
-        lax.psum_scatter(
-            mlp_grad.astype(jnp.bfloat16), "shard", scatter_dimension=0, tiled=True
-        ).astype(jnp.float32),
-        lax.psum_scatter(
-            down_grad.astype(jnp.bfloat16), "shard", scatter_dimension=0, tiled=True
-        ).astype(jnp.float32),
-        lax.psum_scatter(
-            gains_grad.astype(jnp.bfloat16), "shard", scatter_dimension=1, tiled=True
-        ).astype(jnp.float32),
-    )
-    qkv_total, attn_total, mlp_total, down_total, gains_total = lax.psum(
-        (qkv_owned, attn_owned, mlp_owned, down_owned, gains_owned), "seq"
-    )
+    down_total = reduce_grad(down_grad, False)
+    mlp_total = reduce_grad(mlp_grad, True)
+    attn_total = reduce_grad(attn_grad, False)
+    qkv_total = reduce_grad(qkv_grad, False)
+    gains_total = reduce_gains(gains_grad)
     qkv_first_new, qkv_second_new, qkv_new = adam_update(
         qkv_weight, qkv_first, qkv_second, qkv_total, rate_matrix
     )

time: 825 us -> 789 us (0.956)
  waiting for transfers between devices: 232 us -> 192 us
  local copies, waits for them, and re-layouts: 94.7 us -> 113 us
  matrix products: 225 us -> 216 us
    reduce_scatter x4, waiting for transfers between devices: 173 us -> 75.2 us  [the longest x3 58.6 us: reduce_grad(): lax.psum_scatter(low, ('shard', 'seq'), scatter_dimension=0, tiled=True)]
    psum x1, blocking collectives: 105 us -> 40.4 us  [reduce_gains(): total = lax.psum(grad, ('seq', 'shard'))]
    all_gather x0 -> x5, blocking collectives: none -> 58.9 us  [the longest x4 41.2 us: reduce_grad(): total = lax.all_gather(owned, 'seq', axis=0, tiled=False)]
    unnamed x10, waiting for transfers between devices: 0.15 us -> 40 us
    all_gather x4, waiting for transfers between devices: 36.7 us -> 63 us  [the longest x3 63 us: gather_weight(): full = lax.all_gather(part, ('shard', 'seq'), axis=0, tiled=False)]
    unnamed x149 -> x131, local copies, waits for them, and re-layouts: 29.7 us -> 34.1 us
  transfers between devices with their start and end apart: 13 -> 13, of which waited for: 7 -> 8; matrix products, arithmetic and copies ran while one was open for 27% -> 41% of each run, Pallas kernels for 0% -> 0%
where the time goes in v1:
time: 789 us; the launch traced here: 778 us
  matrix products  216 us (27%)
  waiting for transfers between devices  192 us (24%)
  other arithmetic  120 us (15%)
  local copies, waits for them, and re-layouts  113 us (14%)
  blocking collectives  111 us (14%)
  between operations  15 us (2%)
  starting transfers between devices  10.6 us (1%)
    all_gather x3, waiting for transfers between devices, gather_weight(): full = lax.all_gather(part, ('shard', 'seq'), axis=0, tiled=False)  63 us
    reduce_scatter x3, waiting for transfers between devices, reduce_grad(): lax.psum_scatter(low, ('shard', 'seq'), scatter_dimension=0, tiled=True)  58.6 us
    all_gather x4, blocking collectives, reduce_grad(): total = lax.all_gather(owned, 'seq', axis=0, tiled=False)  41.2 us
    psum x1, blocking collectives, reduce_gains(): total = lax.psum(grad, ('seq', 'shard'))  40.4 us
    unnamed x10, waiting for transfers between devices  40 us
    dot_general x2, matrix products, per_device(): jnp.einsum('qhd,khd->hqk', grad_block, value_block, preferred_element_typ...  35.3 us
    unnamed x131, local copies, waits for them, and re-layouts  34.1 us
    convert_element_type x2, other arithmetic, per_device(): grad_scores = (prob_exact * (grad_probs - inner_sum)).astype(jnp.bfloat16)  31.6 us
  transfers between devices with their start and end apart: 13, of which 8 were waited for; matrix products, arithmetic and copies ran while one was open for 41% of the time, Pallas kernels for 0%

profile of v1, /device:TPU:0, one launch (start us, length us, event | category | flops | bytes accessed | tf_op | source)
XLA Modules:
  0.0 777.9 jit_solution(8154501552885249526)
XLA Ops:
  13.1 17.7 %all-gather.2 = bf16[96,2304]{1,0:T(8,128)(2,1)} all-gather(bf16[24,2304]{1,0:T(8,128)(2,1)S(1)} %dynamic-slice_convert_fusion), channel_id=4, replica_groups=mesh['seq'=8,'shard'=4] {'shard'}, dimensions={0}, use_global_device_ids=true | all-gather | bytes 552960 | tf_op jit(solution)/shard_map/all_gather | solution.py:52
  34.0 11.9 %all-gather.8 = bf16[4,192,2]{1,2,0:T(2,128)(2,1)S(1)} all-gather(bf16[1,192,2]{1,2,0:T(2,128)(2,1)S(1)} %convert_bitcast_fusion), channel_id=1, replica_groups=mesh['seq'=8,'shard'=4] {'shard'}, dimensions={0}, use_global_device_ids=true | all-gather | bytes 3840 | tf_op jit(solution)/shard_map/all_gather | solution.py:178
  74.2 58.8 %all-gather.14.cloned.1.call-done = bf16[768,2304]{1,0:T(8,128)(2,1)} async-done(((bf16[24,2304]{1,0:T(8,128)(2,1)}), bf16[768,2304]{1,0:T(8,128)(2,1)}) %all-gather.14.cloned.1.call-update) | async-done | bytes 3538960 | tf_op jit(solution)/shard_map/all_gather | solution.py:55
  162.6 8.9 %fusion.134 = (f32[1280,768]{1,0:T(8,128)}, bf16[1280,768]{1,0:T(8,128)(2,1)}) fusion(f32[1280,2304]{1,0:T(8,128)} %copy-done.13, f32[1280,768]{1,0:T(8,128)} %copy.84, f32[1280,768]{1,0:T(8,128)} %copy.82), kind=kLoop, calls=%fused_computation.237 | loop fusion | flops 2949120 | bytes 21626880 | tf_op jit(solution)/shard_map/slice | solution.py:193
  186.6 7.6 collective-permute-done.1
  207.3 14.4 %fusion.139 = (f32[12,640]{1,0:T(8,128)S(1)}, f32[12,640,768]{2,1,0:T(8,128)}) fusion(pred[640,768]{1,0:T(8,128)(4,1)} %get-tuple-element.190, bf16[768,12,64]{0,2,1:T(8,128)(2,1)} %bitcast.124, bf16[1280,12,64]{0,2,1:T(8,128)(2,1)} %fusion.40), kind=kOutput, calls=%fused_computation.242 | convolution fusion | flops 778568448 | bytes 26277888 | tf_op jit(solution)/shard_map/sub | solution.py:222
  221.6 14.1 %fusion.144 = (f32[12,640]{1,0:T(8,128)S(1)}, f32[12,640,768]{2,1,0:T(8,128)}) fusion(pred[640,768]{1,0:T(8,128)(4,1)} %get-tuple-element.189, bf16[768,12,64]{0,2,1:T(8,128)(2,1)S(1)} %bitcast.122, bf16[1280,12,64]{0,2,1:T(8,128)(2,1)} %fusion.40), kind=kOutput, calls=%fused_computation.243 | convolution fusion | flops 778568448 | bytes 26277888 | tf_op jit(solution)/shard_map/sub | solution.py:222
  235.8 10.3 %fusion.66 = bf16[12,64,640]{2,1,0:T(8,128)(2,1)S(1)} fusion(bf16[768,12,64]{0,2,1:T(8,128)(2,1)} %bitcast.136, f32[12,640,768]{2,1,0:T(8,128)} %get-tuple-element.176, f32[12,640]{1,0:T(8,128)S(1)} %get-tuple-element.175), kind=kOutput, calls=%fused_computation.141 | convolution fusion | flops 767262720 | bytes 25786368 | tf_op jit(solution)/shard_map/hqk,khd->qhd/dot_general | solution.py:226
  246.1 11.0 %fusion.63 = bf16[12,64,640]{2,1,0:T(8,128)(2,1)} fusion(bf16[768,12,64]{0,2,1:T(8,128)(2,1)S(1)} %bitcast.135, f32[12,640,768]{2,1,0:T(8,128)} %get-tuple-element.178, f32[12,640]{1,0:T(8,128)S(1)} %get-tuple-element.177), kind=kOutput, calls=%fused_computation.140 | convolution fusion | flops 767262720 | bytes 25786368 | tf_op jit(solution)/shard_map/hqk,khd->qhd/dot_general | solution.py:226
  263.1 8.4 %fusion.123 = f32[1280,2304]{1,0:T(8,128)S(1)} fusion(bf16[768,2304]{1,0:T(8,128)(2,1)} %bitcast.147, f32[1280,768]{0,1:T(8,128)} %copy-done.14, f32[768]{0:T(1024)S(1)} %get-tuple-element.120, f32[1280]{0:T(1024)S(1)} %fusion.96, f32[1280]{0:T(1024)S(1)} %broadcast_multiply_fusion.2), kind=kOutput, calls=%fused_computation.235 | convolution fusion | flops 4533780480 | bytes 19280896 | tf_op jit(solution)/shard_map/dot_general | solution.py:241
  271.5 16.3 %fusion.58 = (f32[1280,1152]{1,0:T(8,128)}, f32[1280,1152]{1,0:T(8,128)}, f32[1280,1152]{1,0:T(8,128)}) fusion(f32[1280,2304]{1,0:T(8,128)S(1)} %fusion.123, bf16[1152,768]{1,0:T(8,128)(2,1)S(1)} %copy-done.27, bf16[1280,768]{1,0:T(8,128)(2,1)S(1)} %copy-done.24), kind=kOutput, calls=%fused_computation.128 | convolution fusion | flops 2360770560 | bytes 27328512 | tf_op jit(solution)/shard_map/td,fd->tf/dot_general | solution.py:249
  287.8 8.4 %multiply_add_fusion = (f32[1280,1152]{1,0:T(8,128)}, bf16[1280,1152]{1,0:T(8,128)(2,1)}) fusion(f32[1280,1152]{1,0:T(8,128)} %get-tuple-element.142, f32[1280,1152]{1,0:T(8,128)} %get-tuple-element.181, f32[1280,2304]{1,0:T(8,128)S(1)} %fusion.123), kind=kLoop, calls=%fused_computation.29 | loop fusion | flops 25067520 | bytes 32440320 | tf_op jit(solution)/shard_map/transpose(jvp())/add_any | solution.py:120
  296.2 10.7 %multiply_reduce_fusion.2 = (f32[768]{0:T(1024)}, f32[1280]{0:T(1024)S(1)}, f32[1280,768]{0,1:T(8,128)S(1)}) fusion(f32[1280,768]{0,1:T(8,128)S(1)} %copy-done.15, f32[1280]{0:T(1024)S(1)} %fusion.96, f32[1280]{0:T(1024)S(1)} %broadcast_multiply_fusion.2, f32[768]{0:T(1024)S(1)} %get-tuple-element.120, bf16[768,2304]{1,0:T(8,128)(2,1)} %bitcast.148, ...), kind=kOutput, calls=%fused_computation.87 | convolution fusion | flops 4542625792 | bytes 23221248 | tf_op jit(solution)/shard_map/tf,cf->tc/dot_general | solution.py:253
  313.4 10.5 %fusion.16 = f32[12,64,768]{2,1,0:T(8,128)} fusion(bf16[640,12,64]{0,2,1:T(8,128)(2,1)S(1)} %bitcast.144, f32[12,640,768]{2,1,0:T(8,128)} %get-tuple-element.176, f32[12,640]{1,0:T(8,128)S(1)} %get-tuple-element.175), kind=kOutput, calls=%fused_computation.43 | convolution fusion | flops 766771200 | bytes 26966016 | tf_op jit(solution)/shard_map/hqk,qhd->khd/dot_general | solution.py:279
  324.0 18.1 %multiply_reduce_fusion = (f32[12,640]{1,0:T(8,128)S(1)}, f32[12,640,768]{2,1,0:T(8,128)}) fusion(f32[12,640,768]{2,1,0:T(8,128)} %get-tuple-element.176, f32[12,640]{1,0:T(8,128)S(1)} %get-tuple-element.175, bf16[640,12,64]{0,2,1:T(8,128)(2,1)S(1)} %bitcast.145, bf16[768,12,64]{0,2,1:T(8,128)(2,1)S(1)} %bitcast.137), kind=kOutput, calls=%fused_computation.3 | convolution fusion | flops 772661760 | bytes 49410048 | tf_op jit(solution)/shard_map/qhd,khd->hqk/dot_general | solution.py:282
  342.1 9.3 %fusion.20 = f32[12,64,768]{2,1,0:T(8,128)S(1)} fusion(bf16[640,12,64]{0,2,1:T(8,128)(2,1)} %bitcast.142, f32[12,640,768]{2,1,0:T(8,128)} %get-tuple-element.178, f32[12,640]{1,0:T(8,128)S(1)} %get-tuple-element.177), kind=kOutput, calls=%fused_computation.47 | convolution fusion | flops 766771200 | bytes 26966016 | tf_op jit(solution)/shard_map/hqk,qhd->khd/dot_general | solution.py:279
  351.4 17.2 %multiply_reduce_fusion.1 = (f32[12,640]{1,0:T(8,128)}, f32[12,640,768]{2,1,0:T(8,128)}) fusion(f32[12,640,768]{2,1,0:T(8,128)} %get-tuple-element.178, f32[12,640]{1,0:T(8,128)S(1)} %get-tuple-element.177, bf16[640,12,64]{0,2,1:T(8,128)(2,1)} %bitcast.143, bf16[768,12,64]{0,2,1:T(8,128)(2,1)} %bitcast.134), kind=kOutput, calls=%fused_computation.5 | convolution fusion | flops 772661760 | bytes 49410048 | tf_op jit(solution)/shard_map/qhd,khd->hqk/dot_general | solution.py:282
  373.2 15.8 %multiply_convert_fusion = bf16[12,640,768]{2,1,0:T(8,128)(2,1)S(1)} fusion(f32[12,640,768]{2,1,0:T(8,128)} %get-tuple-element.186, f32[12,640]{1,0:T(8,128)S(1)} %get-tuple-element.185, f32[12,640,768]{2,1,0:T(8,128)} %get-tuple-element.176, f32[12,640]{1,0:T(8,128)S(1)} %get-tuple-element.175), kind=kLoop, calls=%fused_computation.2 | loop fusion | flops 23592960 | bytes 59043840 | tf_op jit(solution)/shard_map/convert_element_type | solution.py:286
  393.4 15.8 %multiply_convert_fusion.1 = bf16[12,640,768]{2,1,0:T(8,128)(2,1)S(1)} fusion(f32[12,640,768]{2,1,0:T(8,128)} %get-tuple-element.184, f32[12,640]{1,0:T(8,128)S(1)} %copy-done.46, f32[12,640,768]{2,1,0:T(8,128)} %get-tuple-element.178, f32[12,640]{1,0:T(8,128)S(1)} %get-tuple-element.177), kind=kLoop, calls=%fused_computation.4 | loop fusion | flops 23592960 | bytes 59043840 | tf_op jit(solution)/shard_map/convert_element_type | solution.py:286
  422.0 8.4 %convolution_multiply_fusion.2 = f32[12,64,640]{2,1,0:T(8,128)S(1)} fusion(bf16[768,12,64]{0,2,1:T(8,128)(2,1)} %bitcast.125, bf16[12,640,768]{2,1,0:T(8,128)(2,1)} %copy-done), kind=kOutput, calls=%fused_computation.137 | convolution fusion | flops 755466240 | bytes 14942208 | tf_op jit(solution)/shard_map/hqk,khd->qhd/dot_general | solution.py:288
  491.2 7.9 %fusion.42 = (bf16[1280,768]{0,1:T(8,128)(2,1)}, bf16[1280,768]{0,1:T(8,128)(2,1)}) fusion(f32[640,768]{0,1:T(8,128)S(1)} %bitcast.110, f32[640,768]{0,1:T(8,128)S(1)} %bitcast.112, f32[1280,12,64]{0,2,1:T(8,128)} %pad_maximum_fusion.1, f32[1280,64]{0,1:T(8,128)S(1)} %copy-done.18, f32[1280,12,64]{0,2,1:T(8,128)} %pad_maximum_fusion.2, ...), kind=kLoop, calls=%fused_computation.80 | loop fusion | flops 6881280 | bytes 19988480 | tf_op jit(solution)/shard_map/convert.8
  499.2 9.5 %convolution_convert_fusion.1 = bf16[768,2304]{1,0:T(8,128)(2,1)} fusion(bf16[1280,768]{0,1:T(8,128)(2,1)} %slice.353, bf16[1280,768]{0,1:T(8,128)(2,1)} %get-tuple-element.166, bf16[1280,768]{0,1:T(8,128)(2,1)} %get-tuple-element.165, bf16[1280,768]{0,1:T(8,128)(2,1)S(1)} %copy-done.2, f32[768]{0:T(1024)S(1)} %copy-done.48, f32[1280]{0:T(1024)S(1)} %copy-done.41, ...), kind=kOutput, calls=%fused_computation.62 | convolution fusion | flops 4554227712 | bytes 11416576 | tf_op jit(solution)/shard_map/tc,te->ce/dot_general | solution.py:321
  509.0 10.6 %convolution_convert_fusion = bf16[768,2304]{1,0:T(8,128)(2,1)S(1)} fusion(f32[1280,1152]{1,0:T(8,128)} %get-tuple-element.143, f32[1280,1152]{1,0:T(8,128)} %get-tuple-element.141, f32[1280,768]{0,1:T(8,128)} %copy-done.14, f32[768]{0:T(1024)S(1)} %copy-done.52, f32[1280]{0:T(1024)S(1)} %copy-done.50, f32[1280]{0:T(1024)S(1)} %copy-done.45), kind=kOutput, calls=%fused_computation.61 | convolution fusion | flops 4541448192 | bytes 19280896 | tf_op jit(solution)/shard_map/tc,tf->cf/dot_general | solution.py:252
  536.8 8.9 %fusion.38 = (f32[1280]{0:T(1024)S(1)}, f32[1280,768]{0,1:T(8,128)S(1)}) fusion(bf16[1280,768]{0,1:T(8,128)(2,1)S(1)} %copy-done.2, f32[768]{0:T(1024)S(1)} %copy-done.48, f32[1280]{0:T(1024)S(1)} %copy-done.37, bf16[768,2304]{1,0:T(8,128)(2,1)} %all-gather.14.cloned.1.call-done, bf16[1280,768]{0,1:T(8,128)(2,1)} %slice.353, ...), kind=kOutput, calls=%fused_computation.71 | convolution fusion | flops 4552457216 | bytes 15348736 | tf_op jit(solution)/shard_map/te,ce->tc/dot_general | solution.py:324
  555.7 40.4 %psum.7 = f32[2,768]{1,0:T(2,128)S(1)} all-reduce(f32[2,768]{1,0:T(2,128)S(1)} %pad_maximum_fusion.15), channel_id=1, replica_groups=mesh['seq'=8,'shard'=4] {'seq','shard'}, use_global_device_ids=true, to_apply=%region_21.22 | all-reduce | flops 1536 | bytes 12288 | tf_op jit(solution)/shard_map/psum | solution.py:82
  596.8 10.2 %all-gather.6 = bf16[192,768]{1,0:T(8,128)(2,1)S(1)} all-gather(bf16[24,768]{1,0:T(8,128)(2,1)} %reduce-scatter.10.cloned.1.call-done), channel_id=8, replica_groups=mesh['seq'=8,'shard'=4] {'seq'}, dimensions={0}, use_global_device_ids=true | all-gather | bytes 331776 | tf_op jit(solution)/shard_map/all_gather | solution.py:77
  608.5 9.2 %all-gather.7 = bf16[320,768]{1,0:T(8,128)(2,1)S(1)} all-gather(bf16[40,768]{1,0:T(8,128)(2,1)} %reduce-scatter.14.cloned.1.call-done), channel_id=9, replica_groups=mesh['seq'=8,'shard'=4] {'seq'}, dimensions={0}, use_global_device_ids=true | all-gather | bytes 552960 | tf_op jit(solution)/shard_map/all_gather | solution.py:77
  621.1 58.6 %reduce-scatter.8.cloned.1.call-done = bf16[24,2304]{1,0:T(8,128)(2,1)} async-done(((bf16[768,2304]{1,0:T(8,128)(2,1)}), bf16[24,2304]{1,0:T(8,128)(2,1)}) %reduce-scatter.8.cloned.1.call-update) | async-done | bytes 110608 | tf_op jit(solution)/shard_map/reduce_scatter | solution.py:76
  679.8 10.9 %all-gather.5 = bf16[192,2304]{1,0:T(8,128)(2,1)S(1)} all-gather(bf16[24,2304]{1,0:T(8,128)(2,1)} %reduce-scatter.8.cloned.1.call-done), channel_id=7, replica_groups=mesh['seq'=8,'shard'=4] {'seq'}, dimensions={0}, use_global_device_ids=true | all-gather | bytes 995328 | tf_op jit(solution)/shard_map/all_gather | solution.py:77
  690.7 39.8 %reduce-scatter.16.cloned.1.call-done = bf16[24,9216]{1,0:T(8,128)(2,1)} async-done(((bf16[192,9216]{1,0:T(8,128)(2,1)}), bf16[24,9216]{1,0:T(8,128)(2,1)}) %reduce-scatter.16.cloned.1.call-update) | async-done | bytes 442384
  737.9 16.5 %reduce-scatter.12.cloned.1.call-done = bf16[1,24,2304]{2,1,0:T(8,128)(2,1)} async-done(((bf16[4,24,2304]{2,1,0:T(8,128)(2,1)}), bf16[1,24,2304]{2,1,0:T(8,128)(2,1)}) %reduce-scatter.12.cloned.1.call-update) | async-done | bytes 110608 | tf_op jit(solution)/shard_map/reduce_scatter | solution.py:73
  754.4 11.0 %all_gather.69 = bf16[8,24,2304]{2,1,0:T(8,128)(2,1)S(1)} all-gather(bf16[1,24,2304]{2,1,0:T(8,128)(2,1)} %reduce-scatter.12.cloned.1.call-done), channel_id=1, replica_groups=mesh['seq'=8,'shard'=4] {'seq'}, dimensions={0}, use_global_device_ids=true | all-gather | bytes 995328 | tf_op jit(solution)/shard_map/all_gather | solution.py:77
  (258 shorter events, 235.8 us)
Async XLA Ops:
  7.2 63.4 %all-gather.20.cloned.1.call-start = ((), (), s32[]{:S(2)}) async-start(), calls=%async_computation.12 | async-start | bytes 2027520 | tf_op jit(solution)/shard_map/all_gather | solution.py:55
  8.8 124.1 %all-gather.14.cloned.1.call-start = ((), (), s32[]{:S(2)}) async-start(), calls=%async_computation.9 | async-start | bytes 3649536 | tf_op jit(solution)/shard_map/all_gather | solution.py:55
  10.5 246.6 %all-gather.16.cloned.1.call-start = ((), (), s32[]{:S(2)}) async-start(), calls=%async_computation.10 | async-start | bytes 1216512 | tf_op jit(solution)/shard_map/all_gather | solution.py:55
  12.1 251.0 %all-gather.18.cloned.1.call-start = ((), (), s32[]{:S(2)}) async-start(), calls=%async_computation.11 | async-start | bytes 3981312 | tf_op jit(solution)/shard_map/all_gather | solution.py:53
  30.8 566.0 %reduce-scatter.10.cloned.1.call-start = ((), (), s32[]{:S(2)}) async-start(), calls=%async_computation.6 | async-start | bytes 1216512 | tf_op jit(solution)/shard_map/reduce_scatter | solution.py:76
  46.0 87.0 %copy-start.47 = (f32[768]{0:T(1024)}, f32[768]{0:T(1024)S(1)}, u32[]{:S(2)}) copy-start(f32[768]{0:T(1024)S(1)} %get-tuple-element.121) | copy-start | bytes 9220
  46.0 261.0 %copy-start.51 = (f32[768]{0:T(1024)}, f32[768]{0:T(1024)S(1)}, u32[]{:S(2)}) copy-start(f32[768]{0:T(1024)S(1)} %get-tuple-element.120) | copy-start | bytes 9220
  47.3 136.0 %copy-start.17 = (f32[1280,64]{0,1:T(8,128)}, f32[1280,64]{0,1:T(8,128)S(1)}, u32[]{:S(2)}) copy-start(f32[1280,64]{0,1:T(8,128)S(1)} %get-tuple-element.169) | copy-start | bytes 983044
  47.3 136.0 %copy-start.19 = (f32[1280,64]{0,1:T(8,128)}, f32[1280,64]{0,1:T(8,128)S(1)}, u32[]{:S(2)}) copy-start(f32[1280,64]{0,1:T(8,128)S(1)} %get-tuple-element.170) | copy-start | bytes 983044
  50.2 206.9 %copy-start.1 = (bf16[1280,768]{0,1:T(8,128)(2,1)}, bf16[1280,768]{0,1:T(8,128)(2,1)S(1)}, u32[]{:S(2)}) copy-start(bf16[1280,768]{0,1:T(8,128)(2,1)S(1)} %copy.80) | copy-start | bytes 5898244
  50.5 82.4 %copy-start.36 = (f32[1280]{0:T(1024)}, f32[1280]{0:T(1024)S(1)}, u32[]{:S(2)}) copy-start(f32[1280]{0:T(1024)S(1)} %broadcast_multiply_fusion.3) | copy-start | bytes 15364
  51.7 81.3 %copy-start.40 = (f32[1280]{0:T(1024)}, f32[1280]{0:T(1024)S(1)}, u32[]{:S(2)}) copy-start(f32[1280]{0:T(1024)S(1)} %fusion.95) | copy-start | bytes 15364
  178.2 8.5 %collective-permute-start = (bf16[64,1536]{1,0:T(8,128)(2,1)S(1)}, bf16[64,1536]{1,0:T(8,128)(2,1)S(1)}, u32[]{:S(2)}, u32[]{:S(2)}) collective-permute-start(bf16[64,1536]{1,0:T(8,128)(2,1)S(1)} %get-tuple-element.157), channel_id=1, source_target_pairs={{0,1},{1,2},{2,3},{3,4},{4,5},{5,6},{6,7},{7,8},{8,9},{9,10},{10,1... | collective-permute-start | bytes 589832 | tf_op jit(solution)/shard_map/ppermute | solution.py:32
  181.1 13.1 %collective-permute-start.1 = (bf16[64,1536]{1,0:T(8,128)(2,1)S(1)}, bf16[64,1536]{1,0:T(8,128)(2,1)S(1)}, u32[]{:S(2)}, u32[]{:S(2)}) collective-permute-start(bf16[64,1536]{1,0:T(8,128)(2,1)S(1)} %get-tuple-element.158), channel_id=1, source_target_pairs={{1,0},{2,1},{3,2},{4,3},{5,4},{6,5},{7,6},{8,7},{9,8},{10,9},{11,1... | collective-permute-start | bytes 589832 | tf_op jit(solution)/shard_map/ppermute | solution.py:34
  199.7 21.9 %copy-start.21 = (bf16[768,768]{0,1:T(8,128)(2,1)}, bf16[768,768]{0,1:T(8,128)(2,1)S(1)}, u32[]{:S(2)}) copy-start(bf16[768,768]{0,1:T(8,128)(2,1)S(1)} %copy.87) | copy-start | bytes 3538948
  260.7 46.3 %copy-start.44 = (f32[1280]{0:T(1024)}, f32[1280]{0:T(1024)S(1)}, u32[]{:S(2)}) copy-start(f32[1280]{0:T(1024)S(1)} %broadcast_multiply_fusion.2) | copy-start | bytes 15364
  263.0 43.9 %copy-start.49 = (f32[1280]{0:T(1024)}, f32[1280]{0:T(1024)S(1)}, u32[]{:S(2)}) copy-start(f32[1280]{0:T(1024)S(1)} %fusion.96) | copy-start | bytes 15364
  351.4 17.2 %copy-start.32 = (bf16[12,64,640]{2,1,0:T(8,128)(2,1)S(1)}, bf16[12,64,640]{2,1,0:T(8,128)(2,1)}, u32[]{:S(2)}) copy-start(bf16[12,64,640]{2,1,0:T(8,128)(2,1)} %copy-done.31) | copy-start | bytes 2949124
  373.2 235.3 %reduce-scatter.14.cloned.1.call-start = ((), (), s32[]{:S(2)}) async-start(), calls=%async_computation.8 | async-start | bytes 2027520 | tf_op jit(solution)/shard_map/reduce_scatter | solution.py:76
  430.5 50.4 %copy-start.9 = (f32[12,64,640]{2,1,0:T(8,128)}, f32[12,64,640]{2,1,0:T(8,128)S(1)}, u32[]{:S(2)}) copy-start(f32[12,64,640]{2,1,0:T(8,128)S(1)} %convolution_multiply_fusion.2) | copy-start | bytes 5898244
  432.0 29.1 %collective-permute-start.2 = (bf16[64,1536]{0,1:T(8,128)(2,1)S(1)}, bf16[64,1536]{0,1:T(8,128)(2,1)}, u32[]{:S(2)}, u32[]{:S(2)}) collective-permute-start(bf16[64,1536]{0,1:T(8,128)(2,1)S(1)} %slice.356), channel_id=1, source_target_pairs={{0,1},{1,2},{2,3},{3,4},{4,5},{5,6},{6,7},{7,8},{8,9},{9,10},{10,1... | collective-permute-start | bytes 589832 | tf_op jit(solution)/shard_map/ppermute | solution.py:90
  459.5 12.7 %collective-permute-start.3 = (bf16[64,1536]{0,1:T(8,128)(2,1)S(1)}, bf16[64,1536]{0,1:T(8,128)(2,1)}, u32[]{:S(2)}, u32[]{:S(2)}) collective-permute-start(bf16[64,1536]{0,1:T(8,128)(2,1)S(1)} %slice.355), channel_id=1, source_target_pairs={{1,0},{2,1},{3,2},{4,3},{5,4},{6,5},{7,6},{8,7},{9,8},{10,9},{11,1... | collective-permute-start | bytes 589832 | tf_op jit(solution)/shard_map/ppermute | solution.py:90
  460.8 219.0 %reduce-scatter.8.cloned.1.call-start = ((), (), s32[]{:S(2)}) async-start(), calls=%async_computation.5 | async-start | bytes 3649536 | tf_op jit(solution)/shard_map/reduce_scatter | solution.py:76
  508.7 221.8 %reduce-scatter.16.cloned.1.call-start = ((), (), s32[]{:S(2)}) async-start(), calls=%async_computation.13 | async-start | bytes 3981312
  524.7 229.7 %reduce-scatter.12.cloned.1.call-start = ((), (), s32[]{:S(2)}) async-start(), calls=%async_computation.7 | async-start | bytes 552960 | tf_op jit(solution)/shard_map/reduce_scatter | solution.py:73
  551.5 44.5 %copy-start.53 = (f32[2,192]{1,0:T(2,128)S(1)}, f32[2,192]{1,0:T(2,128)}, u32[]{:S(2)}) copy-start(f32[2,192]{1,0:T(2,128)} %param.33) | copy-start | bytes 4612
  551.5 44.5 %copy-start.55 = (f32[2,192]{1,0:T(2,128)S(1)}, f32[2,192]{1,0:T(2,128)}, u32[]{:S(2)}) copy-start(f32[2,192]{1,0:T(2,128)} %param.43) | copy-start | bytes 4612
  551.5 44.5 %copy-start.56 = (f32[2,192]{1,0:T(2,128)S(1)}, f32[2,192]{1,0:T(2,128)}, u32[]{:S(2)}) copy-start(f32[2,192]{1,0:T(2,128)} %param.42) | copy-start | bytes 4612
  551.5 55.4 %copy-start.33 = (f32[192,768]{1,0:T(8,128)S(1)}, f32[192,768]{1,0:T(8,128)}, u32[]{:S(2)}) copy-start(f32[192,768]{1,0:T(8,128)} %param.30) | copy-start | bytes 1769476
  551.5 55.4 %copy-start.34 = (f32[192,768]{1,0:T(8,128)S(1)}, f32[192,768]{1,0:T(8,128)}, u32[]{:S(2)}) copy-start(f32[192,768]{1,0:T(8,128)} %param.37) | copy-start | bytes 1769476
  551.5 55.4 %copy-start.35 = (f32[192,768]{1,0:T(8,128)S(1)}, f32[192,768]{1,0:T(8,128)}, u32[]{:S(2)}) copy-start(f32[192,768]{1,0:T(8,128)} %param.36) | copy-start | bytes 1769476
  621.1 111.5 %copy-start.23 = (f32[192,2304]{1,0:T(8,128)S(1)}, f32[192,2304]{1,0:T(8,128)}, u32[]{:S(2)}) copy-start(f32[192,2304]{1,0:T(8,128)} %param.29) | copy-start | bytes 5308420
  (42 other events, 265.5 us)
Sparse Core Ops, SparseCore 0:
  11.5 59.0 all-gather.19
  74.0 58.8 all-gather.13
  135.9 56.1 all-gather.15
  193.8 31.0 all-gather.17
  373.3 95.9 reduce-scatter.9
  474.4 97.9 reduce-scatter.13
  577.8 101.9 reduce-scatter.7
  683.3 47.1 reduce-scatter.15
  733.3 21.0 reduce-scatter.11

commit v2 on v0

v2 whole, which is shorter than its diff:
```python
import functools
import math

import jax
import jax.numpy as jnp
from jax import lax
from jax.experimental import pallas as pl
from jax.experimental.pallas import tpu as pltpu
from jax.sharding import PartitionSpec as P

HEADS = 12
HALF = 64
ADAM_STEP = 5
LANES = 128
ROWS = 128
TILE = 256


norm_epsilon = 1e-05
rope_theta = 10000.0
beta_first = 0.9
beta_second = 0.98
adam_epsilon = 1e-06
decay_rate = 1e-05
rate_matrix = 0.04
rate_gains = 0.2
masked_score = -1e30
vmem_bytes = 60 * 1024 * 1024

f32 = jnp.float32
bf16 = jnp.bfloat16


def swap(value, axis, flip):
    count = lax.axis_size(axis)
    return lax.ppermute(value, axis, [(i, i ^ flip) for i in range(count)])


def spread(part, axis, unit, index, count, dim):
    out = jnp.zeros(part.shape[:dim] + (count,) + part.shape[dim:], part.dtype)
    pieces = [part] + [swap(part, axis, unit * d) for d in range(1, count)]
    for d, piece in enumerate(pieces):
        out = lax.dynamic_update_slice_in_dim(out, jnp.expand_dims(piece, dim), index ^ d, dim)
    return out


def places():
    core = lax.axis_index("seq") % 2
    return core, lax.axis_index("seq") // 2, lax.axis_index("shard")


def by_core(core, own, other):
    return jnp.where(core == 0, own, other), jnp.where(core == 0, other, own)


def split_pays():
    count, shards = lax.axis_size("seq"), lax.axis_size("shard")
    return count in (2, 4, 8) and shards in (1, 2, 4)


def halves(weight, core):
    width = weight.shape[1] // 2
    return lax.dynamic_slice_in_dim(weight, core * width, width, 1)


def gather_parts(block):
    core, quarter, shard = places()
    quarters = lax.axis_size("seq") // 2
    rows = block.shape[0] // quarters
    part = lax.dynamic_slice_in_dim(block, quarter * rows, rows, 0)
    part = spread(part, "shard", 1, shard, lax.axis_size("shard"), 0)
    part = spread(part, "seq", 2, quarter, quarters, 1)
    part = part.reshape(-1, block.shape[1])
    return by_core(core, part, swap(part, "seq", 1))


def gather_weights(qkv, attn, mlp, down):
    qkv, attn, mlp, down = (w.astype(bf16) for w in (qkv, attn, mlp, down))
    if not split_pays():
        return tuple(lax.all_gather(w, "shard", axis=0, tiled=True) for w in (qkv, attn, mlp, down))
    core, _, _ = places()
    full_qkv = jnp.concatenate(gather_parts(halves(qkv, core)), axis=1)
    first, second = gather_parts(
        jnp.concatenate([halves(mlp, core), halves(attn, core)], axis=1)
    )
    width = mlp.shape[1] // 2
    full_mlp = jnp.concatenate([first[:, :width], second[:, :width]], axis=1)
    full_attn = jnp.concatenate([first[:, width:], second[:, width:]], axis=1)
    full_down = jnp.concatenate(gather_parts(halves(down, core)), axis=1)
    return full_qkv, full_attn, full_mlp, full_down


def gather_gains(gains):
    shards = lax.axis_size("shard")
    low = gains.astype(bf16)
    if not split_pays():
        return lax.all_gather(low, "shard", axis=1, tiled=True).astype(f32)
    full = spread(low, "shard", 1, lax.axis_index("shard"), shards, 1)
    return full.reshape(gains.shape[0], -1).astype(f32)


def total_of(pieces):
    total = pieces[0].astype(f32)
    for piece in pieces[1:]:
        total = total + piece.astype(f32)
    return total.astype(bf16)


def reduce_parts(own, other):
    core, quarter, shard = places()
    quarters, shards = lax.axis_size("seq") // 2, lax.axis_size("shard")
    rows = own.shape[0] // (quarters * shards)
    half = total_of([own, swap(other, "seq", 1)]).reshape(shards, quarters, rows, -1)

    def at(value, index, dim):
        return lax.dynamic_index_in_dim(value, index, dim, keepdims=False)

    half = total_of(
        [at(half, quarter, 1)]
        + [swap(at(half, quarter ^ d, 1), "seq", 2 * d) for d in range(1, quarters)]
    )
    half = total_of(
        [at(half, shard, 0)] + [swap(at(half, shard ^ d, 0), "shard", d) for d in range(1, shards)]
    )
    half = spread(half, "seq", 2, quarter, quarters, 0).reshape(quarters * rows, -1)
    return by_core(core, half, swap(half, "seq", 1))


def reduce_whole(grad):
    owned = lax.psum_scatter(grad, "shard", scatter_dimension=0, tiled=True)
    return lax.psum(owned.astype(f32), "seq")


def reduce_pair(grad):
    core, _, _ = places()
    return reduce_parts(halves(grad, core), halves(grad, 1 - core))


def reduce_gains(grad):
    columns = grad.shape[1] // lax.axis_size("shard")
    owned = lax.psum(grad, "seq")
    owned = lax.psum(owned, "shard")
    return lax.dynamic_slice_in_dim(owned, lax.axis_index("shard") * columns, columns, 1)


def to_right(value):
    axes = ("seq", "shard")
    ends = lax.axis_size(axes) - 1
    return lax.ppermute(value, axes, [(i, i + 1) for i in range(ends)])


def to_left(value):
    axes = ("seq", "shard")
    ends = lax.axis_size(axes) - 1
    return lax.ppermute(value, axes, [(i + 1, i) for i in range(ends)])


def normed(hidden):
    centered = hidden - jnp.mean(hidden, axis=-1, keepdims=True)
    inverse = lax.rsqrt(jnp.mean(centered * centered, axis=-1, keepdims=True) + norm_epsilon)
    return centered * inverse, inverse


def normed_back(grad, gain, unit, inverse):
    inner = grad * gain
    mean = jnp.mean(inner, axis=-1, keepdims=True)
    slope = jnp.mean(inner * unit, axis=-1, keepdims=True)
    return inverse * (inner - mean - unit * slope)


def dot(a, b):
    return jnp.dot(a, b, preferred_element_type=f32)


def dot_rows(a, b):
    return lax.dot_general(a, b, (((1,), (1,)), ((), ())), preferred_element_type=f32)


def dot_columns(a, b):
    return lax.dot_general(a, b, (((0,), (0,)), ((), ())), preferred_element_type=f32)


def turned(values):
    lane = lax.broadcasted_iota(jnp.int32, values.shape, 1)
    up = pltpu.roll(values, LANES - 32, 1)
    down = pltpu.roll(values, 32, 1)
    return jnp.where(lane % 64 < 32, up, down)


def rope(values, cos, sin):
    return values * cos + turned(values) * sin


def rope_back(values, cos, sin):
    return values * cos - turned(values) * sin


def mask_bias(meta_ref, block, keys):
    first = block * ROWS
    shape = (keys, ROWS)
    key = lax.broadcasted_iota(jnp.int32, shape, 0) + (first - HALF)
    query = lax.broadcasted_iota(jnp.int32, shape, 1) + first
    start, low, high = meta_ref[0], meta_ref[1], meta_ref[2]
    apart = jnp.abs(query - key) > HALF
    other = (query >= start) != (key >= start)
    outside = (key < low) | (key >= high)
    return jnp.where(apart | other | outside, masked_score, 0.0).astype(f32)


def stacked(values):
    lane = lax.broadcasted_iota(jnp.int32, values.shape, 1)
    zero = jnp.zeros_like(values)
    return jnp.concatenate(
        [jnp.where(lane < 64, values, zero), jnp.where(lane < 64, zero, values)], axis=0
    )


def unstacked(values):
    depth = lax.broadcasted_iota(jnp.int32, (LANES, ROWS), 0)
    return jnp.where(depth < 64, values[:, :ROWS], values[:, ROWS:]).T


def window(block):
    return slice(block * ROWS, block * ROWS + ROWS + 2 * HALF)


def project_kernel(x_ref, gain_ref, w_ref, cos_ref, sin_ref, h_ref, q_ref, k_ref, v_ref):
    unit, _ = normed(x_ref[...].astype(f32))
    low = (unit * gain_ref[0:1, :]).astype(bf16)
    h_ref[...] = low
    width = low.shape[1]
    cos, sin = cos_ref[...], sin_ref[...]
    for ref, at, scale in ((q_ref, 0, 0.125), (k_ref, width, None)):
        out = dot(low, w_ref[:, at : at + width])
        for j in range(0, width, LANES):
            value = rope(out[:, j : j + LANES], cos, sin)
            if scale is not None:
                value = value * scale
            ref[:, j : j + LANES] = value.astype(bf16)
    v_ref[...] = dot(low, w_ref[:, 2 * width :]).astype(bf16)


def fill(dst, left, middle, right):
    rows = middle.shape[0]
    dst[0:HALF, :] = left[...]
    dst[HALF : HALF + rows, :] = middle[...]
    dst[HALF + rows :, :] = right[...]


def attend_kernel(meta_ref, q_ref, k_ref, v_ref, kl_ref, vl_ref, kr_ref, vr_ref, o_ref, lse_ref, kx, vx, bias):
    blocks = q_ref.shape[0] // ROWS

    @pl.when(pl.program_id(0) == 0)
    def _():
        for n in range(blocks):
            bias[n] = mask_bias(meta_ref, n, ROWS + 2 * HALF)

    fill(kx, kl_ref, k_ref, kr_ref)
    fill(vx, vl_ref, v_ref, vr_ref)
    for n in range(blocks):
        own = slice(n * ROWS, (n + 1) * ROWS)
        queries = stacked(q_ref[own, :])
        mask = bias[n]
        scores = dot_rows(kx[window(n), :], queries) + jnp.concatenate([mask, mask], axis=1)
        top = jnp.max(scores, axis=0, keepdims=True)
        weights = jnp.exp(scores - top)
        total = jnp.sum(weights, axis=0, keepdims=True)
        out = dot_columns(vx[window(n), :], weights.astype(bf16)) * (1.0 / total)
        o_ref[own, :] = unstacked(out).astype(bf16)
        lse = top + jnp.log(total)
        lse_ref[0, 0:1, own] = lse[:, :ROWS]
        lse_ref[0, 1:2, own] = lse[:, ROWS:]


def attend_back_kernel(
    meta_ref, q_ref, k_ref, v_ref, do_ref, kl_ref, vl_ref, kr_ref, vr_ref, lse_ref, cos_ref, sin_ref,
    dq_ref, dk_ref, dv_ref, hk_ref, hv_ref, ek_ref, ev_ref,
    kx, vx, bias, dkx, dvx,
):
    rows = q_ref.shape[0]
    blocks = rows // ROWS

    @pl.when(pl.program_id(0) == 0)
    def _():
        for n in range(blocks):
            bias[n] = mask_bias(meta_ref, n, ROWS + 2 * HALF)

    fill(kx, kl_ref, k_ref, kr_ref)
    fill(vx, vl_ref, v_ref, vr_ref)
    dkx[...] = jnp.zeros_like(dkx)
    dvx[...] = jnp.zeros_like(dvx)
    for n in range(blocks):
        own = slice(n * ROWS, (n + 1) * ROWS)
        queries = stacked(q_ref[own, :])
        grads = stacked(do_ref[own, :])
        keys = kx[window(n), :]
        mask = bias[n]
        lse = jnp.concatenate([lse_ref[0, 0:1, own], lse_ref[0, 1:2, own]], axis=1)
        scores = dot_rows(keys, queries) + jnp.concatenate([mask, mask], axis=1)
        probs = jnp.exp(scores - lse)
        grad_probs = dot_rows(vx[window(n), :], grads)
        inner = jnp.sum(probs * grad_probs, axis=0, keepdims=True)
        grad_scores = (probs * (grad_probs - inner)).astype(bf16)
        dvx[window(n), :] += dot(probs.astype(bf16), grads)
        dkx[window(n), :] += dot(grad_scores, queries)
        grad_query = unstacked(dot_columns(keys, grad_scores)) * 0.125
        dq_ref[own, :] = rope_back(grad_query, cos_ref[own, :], sin_ref[own, :]).astype(bf16)
    middle = slice(HALF, HALF + rows)
    dk_ref[...] = rope_back(dkx[middle, :], cos_ref[...], sin_ref[...]).astype(bf16)
    dv_ref[...] = dvx[middle, :].astype(bf16)
    for ref, acc in ((hk_ref, dkx), (hv_ref, dvx)):
        ref[0:HALF, :] = acc[0:HALF, :].astype(bf16)
        ref[HALF:, :] = acc[HALF + rows :, :].astype(bf16)
    for ref, acc in ((ek_ref, dkx), (ev_ref, dvx)):
        ref[0:HALF, :] = acc[HALF : 2 * HALF, :]
        ref[HALF:, :] = acc[rows : rows + HALF, :]


def middle_kernel(
    x_ref, o_ref, ct_ref, gain_ref, wa_ref, wm_ref, wd_ref,
    out_ref, dmid_ref, do_ref, gd_ref, gm_ref, ga_ref, gg_ref,
    acc_d, acc_m, acc_a,
):
    step = pl.program_id(0)

    @pl.when(step == 0)
    def _():
        acc_d[...] = jnp.zeros_like(acc_d)
        acc_m[...] = jnp.zeros_like(acc_m)
        acc_a[...] = jnp.zeros_like(acc_a)
        gg_ref[...] = jnp.zeros_like(gg_ref)

    gain = gain_ref[1:2, :]
    hidden = wd_ref.shape[0]
    ct = ct_ref[...]
    mid = x_ref[...].astype(f32) + dot(o_ref[...], wa_ref[...])
    unit, inverse = normed(mid)
    low = (unit * gain).astype(bf16)
    a1 = dot(low, wm_ref[:, :hidden])
    a2 = dot(low, wm_ref[:, hidden:])
    phi = 0.5 * (1.0 + lax.erf(a1 * (1.0 / math.sqrt(2.0))))
    gate = a1 * phi
    u = (gate * a2).astype(bf16)
    out_ref[...] = (mid + dot(u, wd_ref[...])).astype(bf16)
    acc_d[...] += dot_columns(u, ct)
    du = dot_rows(ct, wd_ref[...])
    slope = phi + a1 * (jnp.exp(-0.5 * a1 * a1) * (1.0 / math.sqrt(2.0 * math.pi)))
    da1 = (du * a2 * slope).astype(bf16)
    da2 = (du * gate).astype(bf16)
    acc_m[:, :hidden] += dot_columns(low, da1)
    acc_m[:, hidden:] += dot_columns(low, da2)
    dh = dot_rows(da1, wm_ref[:, :hidden]) + dot_rows(da2, wm_ref[:, hidden:])
    gg_ref[...] += jnp.sum(dh * unit, axis=0, keepdims=True)
    dmid = ct.astype(f32) + normed_back(dh, gain, unit, inverse)
    dmid_ref[...] = dmid
    dmr = dmid.astype(bf16)
    acc_a[...] += dot_columns(o_ref[...], dmr)
    do_ref[...] = dot_rows(dmr, wa_ref[...]).astype(bf16)

    @pl.when(step == pl.num_programs(0) - 1)
    def _():
        gd_ref[...] = acc_d[...].astype(bf16)
        gm_ref[...] = acc_m[...].astype(bf16)
        ga_ref[...] = acc_a[...].astype(bf16)


def patched(step, steps, rows, value_ref, edge_ref):
    value = value_ref[...]
    edge = edge_ref[...]
    head = jnp.concatenate([edge[:HALF], value[HALF:]], axis=0)
    value = jnp.where(step == 0, head, value)
    tail = jnp.concatenate([value[: rows - HALF], edge[HALF:]], axis=0)
    return jnp.where(step == steps - 1, tail, value)


def qkv_grad_kernel(h_ref, dq_ref, dk_ref, dv_ref, ek_ref, ev_ref, g_ref, acc):
    step, steps = pl.program_id(0), pl.num_programs(0)
    rows, width = h_ref.shape

    @pl.when(step == 0)
    def _():
        acc[...] = jnp.zeros_like(acc)

    low = h_ref[...]
    acc[:, :width] += dot_columns(low, dq_ref[...])
    acc[:, width : 2 * width] += dot_columns(low, patched(step, steps, rows, dk_ref, ek_ref))
    acc[:, 2 * width :] += dot_columns(low, patched(step, steps, rows, dv_ref, ev_ref))

    @pl.when(step == steps - 1)
    def _():
        g_ref[...] = acc[...].astype(bf16)


def input_kernel(x_ref, gain_ref, w_ref, dmid_ref, dq_ref, dk_ref, dv_ref, ek_ref, ev_ref, dx_ref, gg_ref):
    step, steps = pl.program_id(0), pl.num_programs(0)
    rows, width = x_ref.shape

    @pl.when(step == 0)
    def _():
        gg_ref[...] = jnp.zeros_like(gg_ref)

    dh = dot_rows(dq_ref[...], w_ref[:, :width])
    dh = dh + dot_rows(patched(step, steps, rows, dk_ref, ek_ref), w_ref[:, width : 2 * width])
    dh = dh + dot_rows(patched(step, steps, rows, dv_ref, ev_ref), w_ref[:, 2 * width :])
    unit, inverse = normed(x_ref[...].astype(f32))
    gg_ref[...] += jnp.sum(dh * unit, axis=0, keepdims=True)
    dx = dmid_ref[...] + normed_back(dh, gain_ref[0:1, :], unit, inverse)
    dx_ref[...] = dx.astype(bf16)


def shaped(shape, dtype):
    return jax.ShapeDtypeStruct(shape, dtype)


def tiles(rows, columns):
    return pl.BlockSpec((rows, columns), lambda i: (i, 0))


def pairs(rows, offset=0):
    return pl.BlockSpec((rows, LANES), lambda i: (0, i + offset))


def kept(*shape):
    return pl.BlockSpec(shape, lambda i: (0,) * len(shape), pipeline_mode=pl.Buffered(1))


def held(*shape):
    return pl.BlockSpec(shape, lambda i: (0,) * len(shape))


def call(kernel, grid, in_specs, out_specs, out_shape, scratch, flops, moved):
    return pl.pallas_call(
        kernel,
        grid=(grid,),
        in_specs=in_specs,
        out_specs=out_specs,
        out_shape=out_shape,
        scratch_shapes=scratch,
        compiler_params=pltpu.CompilerParams(
            vmem_limit_bytes=vmem_bytes, dimension_semantics=("arbitrary",)
        ),
        cost_estimate=pl.CostEstimate(flops=flops, bytes_accessed=moved, transcendentals=0),
    )


def project(x, gains, weight, cos, sin):
    rows, width = x.shape
    tile = min(TILE, rows)
    return call(
        project_kernel,
        rows // tile,
        [tiles(tile, width), held(2, width), kept(*weight.shape), tiles(tile, LANES), tiles(tile, LANES)],
        [tiles(tile, width)] * 4,
        [shaped((rows, width), bf16)] * 4,
        [],
        2 * rows * width * 3 * width,
        rows * width * 10 + weight.size * 2,
    )(x, gains, weight, cos, sin)


def attend_scratch(rows):
    extended = rows + 2 * HALF
    return [
        pltpu.VMEM((extended, LANES), bf16),
        pltpu.VMEM((extended, LANES), bf16),
        pltpu.VMEM((rows // ROWS, ROWS + 2 * HALF, ROWS), f32),
    ]


def attend(meta, q, k, v, left, right):
    rows, width = q.shape
    steps = width // LANES
    return call(
        attend_kernel,
        steps,
        [pl.BlockSpec(memory_space=pltpu.SMEM)]
        + [pairs(rows)] * 3
        + [pairs(HALF), pairs(HALF, steps)] * 2,
        [pairs(rows), pl.BlockSpec((1, 2, rows), lambda i: (i, 0, 0))],
        [shaped((rows, width), bf16), shaped((steps, 2, rows), f32)],
        attend_scratch(rows),
        8 * rows * width * 256,
        rows * width * 8,
    )(meta, q, k, v, left, left, right, right)


def attend_back(meta, q, k, v, do, left, right, lse, cos, sin):
    rows, width = q.shape
    steps = width // LANES
    extended = rows + 2 * HALF
    return call(
        attend_back_kernel,
        steps,
        [pl.BlockSpec(memory_space=pltpu.SMEM)]
        + [pairs(rows)] * 4
        + [pairs(HALF), pairs(HALF, steps)] * 2
        + [pl.BlockSpec((1, 2, rows), lambda i: (i, 0, 0)), held(rows, LANES), held(rows, LANES)],
        [pairs(rows)] * 3 + [pairs(2 * HALF)] * 4,
        [shaped((rows, width), bf16)] * 3
        + [shaped((2 * HALF, width), bf16)] * 2
        + [shaped((2 * HALF, width), f32)] * 2,
        attend_scratch(rows)
        + [pltpu.VMEM((extended, LANES), f32), pltpu.VMEM((extended, LANES), f32)],
        20 * rows * width * 256,
        rows * width * 14,
    )(meta, q, k, v, do, left, left, right, right, lse, cos, sin)


def middle(x, o, ct, gains, wa, wm, wd):
    rows, width = x.shape
    tile = min(TILE, rows)
    return call(
        middle_kernel,
        rows // tile,
        [tiles(tile, width)] * 3 + [held(2, width), kept(*wa.shape), kept(*wm.shape), kept(*wd.shape)],
        [tiles(tile, width)] * 3 + [held(*wd.shape), held(*wm.shape), held(*wa.shape), held(1, width)],
        [
            shaped((rows, width), bf16),
            shaped((rows, width), f32),
            shaped((rows, width), bf16),
            shaped(wd.shape, bf16),
            shaped(wm.shape, bf16),
            shaped(wa.shape, bf16),
            shaped((1, width), f32),
        ],
        [pltpu.VMEM(wd.shape, f32), pltpu.VMEM(wm.shape, f32), pltpu.VMEM(wa.shape, f32)],
        6 * rows * (wa.size + wm.size + wd.size),
        rows * width * 14 + 4 * (wa.size + wm.size + wd.size),
    )(x, o, ct, gains, wa, wm, wd)


def qkv_gradient(h, dq, dk, dv, ek, ev):
    rows, width = h.shape
    tile = min(TILE, rows)
    return call(
        qkv_grad_kernel,
        rows // tile,
        [tiles(tile, width)] * 4 + [held(2 * HALF, width)] * 2,
        held(width, 3 * width),
        shaped((width, 3 * width), bf16),
        [pltpu.VMEM((width, 3 * width), f32)],
        6 * rows * width * width,
        rows * width * 8 + 6 * width * width,
    )(h, dq, dk, dv, ek, ev)


def input_gradient(x, gains, weight, dmid, dq, dk, dv, ek, ev):
    rows, width = x.shape
    tile = min(TILE, rows)
    return call(
        input_kernel,
        rows // tile,
        [tiles(tile, width), held(2, width), kept(*weight.shape)]
        + [tiles(tile, width)] * 4
        + [held(2 * HALF, width)] * 2,
        [tiles(tile, width), held(1, width)],
        [shaped((rows, width), bf16), shaped((1, width), f32)],
        [],
        6 * rows * width * width,
        rows * width * 14 + 6 * width * width,
    )(x, gains, weight, dmid, dq, dk, dv, ek, ev)


def rope_tables(positions, head_size):
    half_size = head_size // 2
    exponent = jnp.arange(half_size, dtype=f32) * (2.0 / head_size)
    inverse = rope_theta ** (-exponent)
    inverse = jnp.tile(inverse, LANES // half_size)
    angles = positions.astype(f32)[:, None] * inverse[None, :]
    sign = jnp.where(jnp.arange(LANES) % head_size < half_size, -1.0, 1.0).astype(f32)
    return jnp.cos(angles), jnp.sin(angles) * sign


def adam_update(master, first_moment, second_moment, gradient, step_rate):
    gradient = gradient.astype(f32)
    new_first = beta_first * first_moment + (1.0 - beta_first) * gradient
    new_second = beta_second * second_moment + (1.0 - beta_second) * gradient * gradient
    first_hat = new_first / (1.0 - beta_first**ADAM_STEP)
    second_hat = new_second / (1.0 - beta_second**ADAM_STEP)
    new_master = master - step_rate * (
        decay_rate * master + first_hat / (jnp.sqrt(second_hat) + adam_epsilon)
    )
    return (new_first, new_second, new_master)


def edge_rows(value):
    return value[:HALF], value[value.shape[0] - HALF :]


def rope_back_wide(values, cos, sin):
    half = 32
    rows, width = values.shape
    parts = values.reshape(rows, width // (2 * half), 2, half)
    wide_cos = cos[:, None, : 2 * half].reshape(rows, 1, 2, half)
    wide_sin = sin[:, None, : 2 * half].reshape(rows, 1, 2, half)
    return (parts * wide_cos - parts[:, :, ::-1] * wide_sin).reshape(rows, width)


def per_device(
    tokens,
    positions,
    cotangent,
    qkv_weight,
    attn_weight,
    mlp_weight,
    down_weight,
    norm_gains,
    qkv_first,
    qkv_second,
    attn_first,
    attn_second,
    mlp_first,
    mlp_second,
    down_first,
    down_second,
    gains_first,
    gains_second,
):
    rows, width = tokens.shape
    device = lax.axis_index(("seq", "shard"))
    last_device = lax.axis_size(("seq", "shard")) - 1
    full_qkv, full_attn, full_mlp, full_down = gather_weights(
        qkv_weight, attn_weight, mlp_weight, down_weight
    )
    gains = gather_gains(norm_gains)
    cos, sin = rope_tables(positions, width // HEADS)
    start = jnp.max(jnp.where(positions == 0, jnp.arange(rows, dtype=jnp.int32), 0))
    low = jnp.where(device > 0, -HALF, 0)
    high = jnp.where(device < last_device, rows + HALF, rows)
    meta = jnp.stack([start, low, high]).astype(jnp.int32)

    h, q, k, v = project(tokens, gains, full_qkv, cos, sin)
    k_head, k_tail = edge_rows(k)
    v_head, v_tail = edge_rows(v)
    left = to_right(jnp.concatenate([k_tail, v_tail], axis=1))
    right = to_left(jnp.concatenate([k_head, v_head], axis=1))
    o, lse = attend(meta, q, k, v, left, right)
    layer_output, dmid, do, down_grad, mlp_grad, attn_grad, gain_mlp_grad = middle(
        tokens, o, cotangent, gains, full_attn, full_mlp, full_down
    )
    dq, dk, dv, halo_k, halo_v, edge_k, edge_v = attend_back(
        meta, q, k, v, do, left, right, lse, cos, sin
    )
    halo = jnp.concatenate([halo_k, halo_v], axis=1)
    from_right = to_left(halo[:HALF])
    from_left = to_right(halo[HALF:])
    arrived = jnp.concatenate([from_left, from_right], axis=0).astype(f32)
    edge_cos = jnp.concatenate(edge_rows(cos), axis=0)
    edge_sin = jnp.concatenate(edge_rows(sin), axis=0)
    edge_k = rope_back_wide(edge_k + arrived[:, :width], edge_cos, edge_sin).astype(bf16)
    edge_v = (edge_v + arrived[:, width:]).astype(bf16)
    qkv_grad = qkv_gradient(h, dq, dk, dv, edge_k, edge_v)
    input_grad, gain_attn_grad = input_gradient(
        tokens, gains, full_qkv, dmid, dq, dk, dv, edge_k, edge_v
    )
    gains_total = reduce_gains(jnp.concatenate([gain_attn_grad, gain_mlp_grad], axis=0))
    if split_pays():
        core, _, _ = places()
        wide = mlp_weight.shape[1] // 2
        down_total = jnp.concatenate(reduce_pair(down_grad), axis=1)
        own, other = (
            jnp.concatenate([halves(mlp_grad, c), halves(attn_grad, c)], axis=1)
            for c in (core, 1 - core)
        )
        first, second = reduce_parts(own, other)
        mlp_total = jnp.concatenate([first[:, :wide], second[:, :wide]], axis=1)
        attn_total = jnp.concatenate([first[:, wide:], second[:, wide:]], axis=1)
        qkv_total = jnp.concatenate(reduce_pair(qkv_grad), axis=1)
    else:
        down_total, mlp_total, attn_total, qkv_total = (
            reduce_whole(g) for g in (down_grad, mlp_grad, attn_grad, qkv_grad)
        )
    qkv_new = adam_update(qkv_weight, qkv_first, qkv_second, qkv_total, rate_matrix)
    attn_new = adam_update(attn_weight, attn_first, attn_second, attn_total, rate_matrix)
    mlp_new = adam_update(mlp_weight, mlp_first, mlp_second, mlp_total, rate_matrix)
    down_new = adam_update(down_weight, down_first, down_second, down_total, rate_matrix)
    gains_new = adam_update(norm_gains, gains_first, gains_second, gains_total, rate_gains)
    return (layer_output, input_grad, *qkv_new, *attn_new, *mlp_new, *down_new, *gains_new)


def solution(mesh):
    tokens, rows, columns = P(("seq", "shard"), None), P("shard", None), P(None, "shard")
    matrices = (rows,) * 4
    return jax.shard_map(
        per_device,
        mesh=mesh,
        in_specs=(tokens, P(("seq", "shard")), tokens, *matrices, columns)
        + (rows,) * 8
        + (columns,) * 2,
        out_specs=(tokens, tokens) + (rows,) * 12 + (columns,) * 3,
        check_vma=False,
    )
```

time: 825 us -> 426 us (0.52)
  matrix products: 225 us -> 0 us
  Pallas kernels: 0 us -> 121 us
  waiting for transfers between devices: 232 us -> 119 us
  blocking collectives: 117 us -> 24 us
  other arithmetic: 122 us -> 37.9 us
  starting transfers between devices: 8.26 us -> 90.5 us
  local copies, waits for them, and re-layouts: 94.7 us -> 22.5 us
  between operations: 15.2 us -> 2.27 us
    dot_general x22 -> x0, matrix products: 196 us -> none  [the longest x2 33.5 us: per_device(): jnp.einsum('qhd,khd->hqk', grad_block, value_block, preferred_element_typ...]
    reduce_scatter x4 -> x0, waiting for transfers between devices: 173 us -> none  [the longest x1 69 us: per_device(): lax.psum_scatter(qkv_grad.astype(jnp.bfloat16), 'shard', scatter_dimensio...]
    pallas_call x0 -> x6, Pallas kernels: none -> 121 us  [the longest x1 42.7 us: middle(): call(middle_kernel, rows // tile, [tiles(tile, width)] * 3 + [held(2, wid...]
    ppermute x4 -> x61, waiting for transfers between devices: 22.1 us -> 119 us  [the longest x57 114 us: swap(): return lax.ppermute(value, axis, [(i, i ^ flip) for i in range(count)])]
    ppermute x4 -> x61, starting transfers between devices: 7.68 us -> 90.5 us  [the longest x57 78.9 us: swap(): return lax.ppermute(value, axis, [(i, i ^ flip) for i in range(count)])]
    psum x1 -> x2, blocking collectives: 105 us -> 24 us  [the longest x1 12.4 us: reduce_gains(): owned = lax.psum(grad, 'seq')]
    slice x16 -> x13, local copies, waits for them, and re-layouts: 42.3 us -> 2.98 us  [the longest x2 1.07 us: edge_rows(): return (value[:HALF], value[value.shape[0] - HALF:])]
    all_gather x4 -> x0, waiting for transfers between devices: 36.7 us -> none  [the longest x1 36.7 us: per_device(): lax.all_gather(qkv_weight.astype(jnp.bfloat16), 'shard', axis=0, tiled=True)]
  transfers between devices with their start and end apart: 13 -> 61, of which waited for: 7 -> 27; matrix products, arithmetic and copies ran while one was open for 27% -> 10% of each run, Pallas kernels for 0% -> 13%
where the time goes in v2:
time: 426 us; the launch traced here: 418 us
  Pallas kernels  121 us (28%)
  waiting for transfers between devices  119 us (28%)
  starting transfers between devices  90.5 us (21%)
  other arithmetic  37.9 us (9%)
  blocking collectives  24 us (6%)
  local copies, waits for them, and re-layouts  22.5 us (5%)
    ppermute x57, waiting for transfers between devices, swap(): return lax.ppermute(value, axis, [(i, i ^ flip) for i in range(count)])  114 us
    ppermute x57, starting transfers between devices, swap(): return lax.ppermute(value, axis, [(i, i ^ flip) for i in range(count)])  78.9 us
    pallas_call x1, Pallas kernels, middle(): call(middle_kernel, rows // tile, [tiles(tile, width)] * 3 + [held(2, wid...  42.7 us
    pallas_call x1, Pallas kernels, attend_back(): call(attend_back_kernel, steps, [pl.BlockSpec(memory_space=pltpu.SMEM)] +...  24.4 us
    pallas_call x1, Pallas kernels, attend(): call(attend_kernel, steps, [pl.BlockSpec(memory_space=pltpu.SMEM)] + [pai...  22.1 us
    psum x1, blocking collectives, reduce_gains(): owned = lax.psum(grad, 'seq')  12.4 us
    psum x1, blocking collectives, reduce_gains(): owned = lax.psum(owned, 'shard')  11.6 us
    pallas_call x1, Pallas kernels, input_gradient(): call(input_kernel, rows // tile, [tiles(tile, width), held(2, width), kep...  11.4 us
  transfers between devices with their start and end apart: 61, of which 27 were waited for; matrix products, arithmetic and copies ran while one was open for 10% of the time, Pallas kernels for 13%

profile of v2, /device:TPU:0, one launch (start us, length us, event | category | flops | bytes accessed | tf_op | source)
XLA Modules:
  0.0 417.7 jit_solution(1211828266281948081)
XLA Ops:
  2.4 3.0 collective-permute-start.19
  9.1 3.9 collective-permute-start.2
  24.3 4.3 %collective-permute-start.13 = (bf16[48,1536]{1,0:T(8,128)(2,1)S(1)}, bf16[48,1536]{1,0:T(8,128)(2,1)S(1)}, u32[]{:S(2)}, u32[]{:S(2)}) collective-permute-start(bf16[48,1536]{1,0:T(8,128)(2,1)S(1)} %get-tuple-element.85), channel_id=1, source_target_pairs={{0,2},{1,3},{2,0},{3,1},{4,6},{5,7},{6,4},{7,5},{8,10},{9,11},{10,... | collective-permute-start | bytes 442376 | tf_op jit(solution)/shard_map/ppermute | solution.py:36
  31.2 2.8 collective-permute-start.4
  37.5 4.7 %collective-permute-start.5 = (bf16[48,1152]{1,0:T(8,128)(2,1)S(1)}, bf16[48,1152]{1,0:T(8,128)(2,1)S(1)}, u32[]{:S(2)}, u32[]{:S(2)}) collective-permute-start(bf16[48,1152]{1,0:T(8,128)(2,1)S(1)} %get-tuple-element.87), channel_id=1, source_target_pairs={{0,3},{1,2},{2,1},{3,0},{4,7},{5,6},{6,5},{7,4},{8,11},{9,10},{10,... | collective-permute-start | bytes 331784 | tf_op jit(solution)/shard_map/ppermute | solution.py:36
  42.2 7.4 %collective-permute-done.4 = bf16[48,1152]{1,0:T(8,128)(2,1)S(1)} collective-permute-done((bf16[48,1152]{1,0:T(8,128)(2,1)S(1)}, bf16[48,1152]{1,0:T(8,128)(2,1)S(1)}, u32[]{:S(2)}, u32[]{:S(2)}) %collective-permute-start.4) | collective-permute-done | bytes 110624 | tf_op jit(solution)/shard_map/ppermute | solution.py:36
  64.2 8.0 %collective-permute-done.6 = bf16[4,48,1152]{2,1,0:T(8,128)(2,1)S(1)} collective-permute-done((bf16[4,48,1152]{2,1,0:T(8,128)(2,1)S(1)}, bf16[4,48,1152]{2,1,0:T(8,128)(2,1)S(1)}, u32[]{:S(2)}, u32[]{:S(2)}) %collective-permute-start.6) | collective-permute-done | bytes 442400 | tf_op jit(solution)/shard_map/ppermute | solution.py:36
  74.8 6.6 %collective-permute-done.7 = bf16[4,48,1152]{2,1,0:T(8,128)(2,1)S(1)} collective-permute-done((bf16[4,48,1152]{2,1,0:T(8,128)(2,1)S(1)}, bf16[4,48,1152]{2,1,0:T(8,128)(2,1)S(1)}, u32[]{:S(2)}, u32[]{:S(2)}) %collective-permute-start.7) | collective-permute-done | bytes 442400 | tf_op jit(solution)/shard_map/ppermute | solution.py:36
  82.8 11.6 %collective-permute-done.15 = bf16[4,48,1536]{2,1,0:T(8,128)(2,1)S(1)} collective-permute-done((bf16[4,48,1536]{2,1,0:T(8,128)(2,1)S(1)}, bf16[4,48,1536]{2,1,0:T(8,128)(2,1)S(1)}, u32[]{:S(2)}, u32[]{:S(2)}) %collective-permute-start.15) | collective-permute-done | bytes 589856 | tf_op jit(solution)/shard_map/ppermute | solution.py:36
  94.4 9.2 %collective-permute-done.16 = bf16[4,48,1536]{2,1,0:T(8,128)(2,1)S(1)} collective-permute-done((bf16[4,48,1536]{2,1,0:T(8,128)(2,1)S(1)}, bf16[4,48,1536]{2,1,0:T(8,128)(2,1)S(1)}, u32[]{:S(2)}, u32[]{:S(2)}) %collective-permute-start.16) | collective-permute-done | bytes 589856 | tf_op jit(solution)/shard_map/ppermute | solution.py:36
  107.6 10.1 %shard_map.305 = (bf16[1280,768]{1,0:T(8,128)(2,1)}, bf16[1280,768]{1,0:T(8,128)(2,1)}, bf16[1280,768]{1,0:T(8,128)(2,1)}, bf16[1280,768]{1,0:T(8,128)(2,1)}) custom-call(bf16[1280,768]{1,0:T(8,128)(2,1)} %x_ref.5, f32[2,768]{1,0:T(2,128)} %reshape.112.gain_ref, bf16[768,2304]{1,0:T(8,128)(2,1)} %pad_maximum_fusion.w_ref, f32[1280,128]{1,0:T(8,128)} %copy-done.15, ...), custom_call_target="tpu_custom_call" | custom-call | flops 4529848320 | bytes 13369344 | tf_op jit(solution)/shard_map/pallas_call | solution.py:449
  120.1 4.6 %collective-permute-start.10 = (bf16[64,1536]{1,0:T(8,128)(2,1)S(1)}, bf16[64,1536]{1,0:T(8,128)(2,1)S(1)}, u32[]{:S(2)}, u32[]{:S(2)}) collective-permute-start(bf16[64,1536]{1,0:T(8,128)(2,1)S(1)} %pad_maximum_fusion.9), channel_id=1, source_target_pairs={{0,1},{1,2},{2,3},{3,4},{4,5},{5,6},{6,7},{7,8},{8,9},{9,10},{10,1... | collective-permute-start | bytes 589832 | tf_op jit(solution)/shard_map/ppermute | solution.py:149
  129.8 22.1 %shard_map.306 = (bf16[1280,768]{1,0:T(8,128)(2,1)}, f32[6,2,1280]{2,1,0:T(2,128)}) custom-call(s32[3]{0:T(128)} %pad_add_fusion.meta_ref, bf16[1280,768]{1,0:T(8,128)(2,1)} %get-tuple-element.39.q_ref, bf16[1280,768]{1,0:T(8,128)(2,1)} %get-tuple-element.40.k_ref, bf16[1280,768]{1,0:T(8,128)(2,1)} %get-tuple-element.41.v_ref, bf16[64,1536]{1,0:T(8,128)(2,1)} %copy-done.27, ...), custom_call_target="tpu_custom_call" | custom-call | flops 2013265920 | bytes 7864320 | tf_op jit(solution)/shard_map/pallas_call | solution.py:473
  157.6 42.7 %shard_map.307 = (bf16[1280,768]{1,0:T(8,128)(2,1)}, f32[1280,768]{1,0:T(8,128)}, bf16[1280,768]{1,0:T(8,128)(2,1)}, bf16[1152,768]{1,0:T(8,128)(2,1)}, bf16[768...) custom-call(bf16[1280,768]{1,0:T(8,128)(2,1)} %x_ref.5, bf16[1280,768]{1,0:T(8,128)(2,1)} %get-tuple-element.42.o_ref, ...), custom_call_target="tpu_custom_call" | custom-call | flops 24914165760 | bytes 26738688 | tf_op jit(solution)/shard_map/pallas_call | solution.py:512
  200.3 24.4 %shard_map.308 = (bf16[1280,768]{1,0:T(8,128)(2,1)}, bf16[1280,768]{1,0:T(8,128)(2,1)}, bf16[1280,768]{1,0:T(8,128)(2,1)}, bf16[128,768]{1,0:T(8,128)(2,1)}, bf1...) custom-call(s32[3]{0:T(128)} %pad_add_fusion.meta_ref, bf16[1280,768]{1,0:T(8,128)(2,1)} %get-tuple-element.39.q_ref, ...), custom_call_target="tpu_custom_call" | custom-call | flops 5033164800 | bytes 13762560 | tf_op jit(solution)/shard_map/pallas_call | solution.py:491
  226.7 4.4 %collective-permute-start.26 = (bf16[64,1536]{1,0:T(8,128)(2,1)S(1)}, bf16[64,1536]{1,0:T(8,128)(2,1)S(1)}, u32[]{:S(2)}, u32[]{:S(2)}) collective-permute-start(bf16[64,1536]{1,0:T(8,128)(2,1)S(1)} %get-tuple-element.129), channel_id=1, source_target_pairs={{0,1},{1,2},{2,3},{3,4},{4,5},{5,6},{6,7},{7,8},{8,9},{9,10},{10,1... | collective-permute-start | bytes 589832 | tf_op jit(solution)/shard_map/ppermute | solution.py:149
  233.4 5.9 %collective-permute-start.50 = (bf16[1152,384]{1,0:T(8,128)(2,1)}, bf16[1152,384]{1,0:T(8,128)(2,1)}, u32[]{:S(2)}, u32[]{:S(2)}) collective-permute-start(bf16[1152,384]{1,0:T(8,128)(2,1)} %constant_dynamic-slice_fusion.1), channel_id=1, source_target_pairs={{0,4},{4,0},{8,12},{12,8},{16,20},{20,16},{24,28},{28,24},{1,5},{5... | collective-permute-start | bytes 2654216 | tf_op jit(solution)/shard_map/ppermute | solution.py:36
  246.2 10.4 %shard_map.310 = bf16[768,2304]{1,0:T(8,128)(2,1)} custom-call(bf16[1280,768]{1,0:T(8,128)(2,1)} %get-tuple-element.55.h_ref, bf16[1280,768]{1,0:T(8,128)(2,1)} %get-tuple-element.47.dq_ref, bf16[1280,768]{1,0:T(8,128)(2,1)} %get-tuple-element.48.dk_ref, bf16[1280,768]{1,0:T(8,128)(2,1)} %get-tuple-element.49.dv_ref, bf16[128,768]{1,0:T(8,128)(2,1)} %copy.66.ek_ref, ...), custom_call_target="tpu_custom_call" | custom-call | flops 4529848320 | bytes 11403264 | tf_op jit(solution)/shard_map/pallas_call | solution.py:535
  256.7 2.9 constant_dynamic-slice_fusion.6
  266.6 11.4 %shard_map.309 = (bf16[1280,768]{1,0:T(8,128)(2,1)}, f32[1,768]{1,0:T(1,128)}) custom-call(bf16[1280,768]{1,0:T(8,128)(2,1)} %x_ref.5, f32[2,768]{1,0:T(2,128)} %reshape.112.gain_ref, bf16[768,2304]{1,0:T(8,128)(2,1)} %pad_maximum_fusion.w_ref, f32[1280,768]{1,0:T(8,128)} %get-tuple-element.44.dmid_ref, bf16[1280,768]{1,0:T(8,128)(2,1)} %get-tuple-element.47.dq_ref, ...), custom_call_target="tpu_custom_call" | custom-call | flops 4529848320 | bytes 17301504 | tf_op jit(solution)/shard_map/pallas_call | solution.py:550
  279.5 3.6 collective-permute-start.55
  284.4 12.4 %psum.14 = f32[2,768]{1,0:T(2,128)S(1)} all-reduce(f32[2,768]{1,0:T(2,128)S(1)} %pad_maximum_fusion.13), channel_id=1, replica_groups=mesh['seq'=8,'shard'=4] {'seq'}, use_global_device_ids=true, to_apply=%region_1.2 | all-reduce | flops 1536 | bytes 12288 | tf_op jit(solution)/shard_map/psum | solution.py:141
  296.8 11.6 %psum.15 = f32[2,768]{1,0:T(2,128)S(1)} all-reduce(f32[2,768]{1,0:T(2,128)S(1)} %psum.14), channel_id=1, replica_groups=mesh['seq'=8,'shard'=4] {'shard'}, use_global_device_ids=true, to_apply=%region_2.3 | all-reduce | flops 1536 | bytes 12288 | tf_op jit(solution)/shard_map/psum | solution.py:142
  324.2 7.5 %collective-permute-done.29 = bf16[4,48,1152]{2,1,0:T(8,128)(2,1)S(1)} collective-permute-done((bf16[4,48,1152]{2,1,0:T(8,128)(2,1)S(1)}, bf16[4,48,1152]{2,1,0:T(8,128)(2,1)S(1)}, u32[]{:S(2)}, u32[]{:S(2)}) %collective-permute-start.29) | collective-permute-done | bytes 442400 | tf_op jit(solution)/shard_map/ppermute | solution.py:36
  331.7 10.7 %collective-permute-done.30 = bf16[4,48,1152]{2,1,0:T(8,128)(2,1)S(1)} collective-permute-done((bf16[4,48,1152]{2,1,0:T(8,128)(2,1)S(1)}, bf16[4,48,1152]{2,1,0:T(8,128)(2,1)S(1)}, u32[]{:S(2)}, u32[]{:S(2)}) %collective-permute-start.30) | collective-permute-done | bytes 442400 | tf_op jit(solution)/shard_map/ppermute | solution.py:36
  343.0 4.1 collective-permute-start.34
  349.4 4.7 %collective-permute-done.33 = bf16[48,1152]{1,0:T(8,128)(2,1)S(1)} collective-permute-done((bf16[48,1152]{1,0:T(8,128)(2,1)S(1)}, bf16[48,1152]{1,0:T(8,128)(2,1)S(1)}, u32[]{:S(2)}, u32[]{:S(2)}) %collective-permute-start.33) | collective-permute-done | bytes 110624 | tf_op jit(solution)/shard_map/ppermute | solution.py:36
  361.7 24.4 %collective-permute-done.36 = bf16[48,1152]{1,0:T(8,128)(2,1)S(1)} collective-permute-done((bf16[48,1152]{1,0:T(8,128)(2,1)S(1)}, bf16[48,1152]{1,0:T(8,128)(2,1)S(1)}, u32[]{:S(2)}, u32[]{:S(2)}) %collective-permute-start.36) | collective-permute-done | bytes 110624 | tf_op jit(solution)/shard_map/ppermute | solution.py:36
  386.6 2.7 collective-permute-start.43
  393.1 5.4 %collective-permute-done.44 = bf16[48,1536]{1,0:T(8,128)(2,1)S(1)} collective-permute-done((bf16[48,1536]{1,0:T(8,128)(2,1)S(1)}, bf16[48,1536]{1,0:T(8,128)(2,1)S(1)}, u32[]{:S(2)}, u32[]{:S(2)}) %collective-permute-start.44) | collective-permute-done | bytes 147488 | tf_op jit(solution)/shard_map/ppermute | solution.py:36
  407.2 3.3 multiply_subtract_fusion.1
  412.5 3.3 multiply_subtract_fusion
  (277 shorter events, 121.4 us)
Async XLA Ops:
  2.4 27.0 %collective-permute-start.19 = (bf16[72,384]{1,0:T(8,128)(2,1)}, bf16[72,384]{1,0:T(8,128)(2,1)S(1)}, u32[]{:S(2)}, u32[]{:S(2)}) collective-permute-start(bf16[72,384]{1,0:T(8,128)(2,1)} %get-tuple-element.83), channel_id=1, source_target_pairs={{0,1},{1,0},{2,3},{3,2},{4,5},{5,4},{6,7},{7,6},{8,9},{9,8},{10,11... | collective-permute-start | bytes 165896 | tf_op jit(solution)/shard_map/ppermute | solution.py:36
  5.4 24.1 %collective-permute-start.20 = (bf16[72,384]{1,0:T(8,128)(2,1)}, bf16[72,384]{1,0:T(8,128)(2,1)S(1)}, u32[]{:S(2)}, u32[]{:S(2)}) collective-permute-start(bf16[72,384]{1,0:T(8,128)(2,1)} %get-tuple-element.83), channel_id=1, source_target_pairs={{0,2},{1,3},{2,0},{3,1},{4,6},{5,7},{6,4},{7,5},{8,10},{9,11},{10,... | collective-permute-start | bytes 165896 | tf_op jit(solution)/shard_map/ppermute | solution.py:36
  8.7 15.5 %collective-permute-start = (bf16[2,192]{1,0:T(2,128)(2,1)S(1)}, bf16[2,192]{1,0:T(2,128)(2,1)S(1)}, u32[]{:S(2)}, u32[]{:S(2)}) collective-permute-start(bf16[2,192]{1,0:T(2,128)(2,1)S(1)} %convert_element_type.181), channel_id=1, source_target_pairs={{0,1},{1,0},{2,3},{3,2},{4,5},{5,4},{6,7},{7,6},{8,9},{9,8},{10,11... | collective-permute-start | bytes 2312 | tf_op jit(solution)/shard_map/ppermute | solution.py:36
  9.1 15.2 %collective-permute-start.2 = (bf16[2,192]{1,0:T(2,128)(2,1)S(1)}, bf16[2,192]{1,0:T(2,128)(2,1)S(1)}, u32[]{:S(2)}, u32[]{:S(2)}) collective-permute-start(bf16[2,192]{1,0:T(2,128)(2,1)S(1)} %convert_element_type.181), channel_id=1, source_target_pairs={{0,3},{1,2},{2,1},{3,0},{4,7},{5,6},{6,5},{7,4},{8,11},{9,10},{10,... | collective-permute-start | bytes 2312 | tf_op jit(solution)/shard_map/ppermute | solution.py:36
  24.2 28.8 %collective-permute-start.12 = (bf16[48,1536]{1,0:T(8,128)(2,1)S(1)}, bf16[48,1536]{1,0:T(8,128)(2,1)S(1)}, u32[]{:S(2)}, u32[]{:S(2)}) collective-permute-start(bf16[48,1536]{1,0:T(8,128)(2,1)S(1)} %get-tuple-element.85), channel_id=1, source_target_pairs={{0,1},{1,0},{2,3},{3,2},{4,5},{5,4},{6,7},{7,6},{8,9},{9,8},{10,11... | collective-permute-start | bytes 442376 | tf_op jit(solution)/shard_map/ppermute | solution.py:36
  24.3 29.2 %collective-permute-start.13 = (bf16[48,1536]{1,0:T(8,128)(2,1)S(1)}, bf16[48,1536]{1,0:T(8,128)(2,1)S(1)}, u32[]{:S(2)}, u32[]{:S(2)}) collective-permute-start(bf16[48,1536]{1,0:T(8,128)(2,1)S(1)} %get-tuple-element.85), channel_id=1, source_target_pairs={{0,2},{1,3},{2,0},{3,1},{4,6},{5,7},{6,4},{7,5},{8,10},{9,11},{10,... | collective-permute-start | bytes 442376 | tf_op jit(solution)/shard_map/ppermute | solution.py:36
  29.4 25.7 %collective-permute-start.14 = (bf16[48,1536]{1,0:T(8,128)(2,1)S(1)}, bf16[48,1536]{1,0:T(8,128)(2,1)S(1)}, u32[]{:S(2)}, u32[]{:S(2)}) collective-permute-start(bf16[48,1536]{1,0:T(8,128)(2,1)S(1)} %get-tuple-element.85), channel_id=1, source_target_pairs={{0,3},{1,2},{2,1},{3,0},{4,7},{5,6},{6,5},{7,4},{8,11},{9,10},{10,... | collective-permute-start | bytes 442376 | tf_op jit(solution)/shard_map/ppermute | solution.py:36
  31.2 18.4 %collective-permute-start.4 = (bf16[48,1152]{1,0:T(8,128)(2,1)S(1)}, bf16[48,1152]{1,0:T(8,128)(2,1)S(1)}, u32[]{:S(2)}, u32[]{:S(2)}) collective-permute-start(bf16[48,1152]{1,0:T(8,128)(2,1)S(1)} %get-tuple-element.87), channel_id=1, source_target_pairs={{0,2},{1,3},{2,0},{3,1},{4,6},{5,7},{6,4},{7,5},{8,10},{9,11},{10,... | collective-permute-start | bytes 331784 | tf_op jit(solution)/shard_map/ppermute | solution.py:36
  53.6 18.6 %collective-permute-start.6 = (bf16[4,48,1152]{2,1,0:T(8,128)(2,1)S(1)}, bf16[4,48,1152]{2,1,0:T(8,128)(2,1)S(1)}, u32[]{:S(2)}, u32[]{:S(2)}) collective-permute-start(bf16[4,48,1152]{2,1,0:T(8,128)(2,1)S(1)} %bitcast_dynamic-update-slice_fusion.24), channel_id=1, source_target_pairs={{0,8},{4,12},{8,0},{12,4},{16,24},{20,28},{24,16},{28,20},{1,9},{5... | collective-permute-start | bytes 1327112 | tf_op jit(solution)/shard_map/ppermute | solution.py:36
  55.2 26.3 %collective-permute-start.7 = (bf16[4,48,1152]{2,1,0:T(8,128)(2,1)S(1)}, bf16[4,48,1152]{2,1,0:T(8,128)(2,1)S(1)}, u32[]{:S(2)}, u32[]{:S(2)}) collective-permute-start(bf16[4,48,1152]{2,1,0:T(8,128)(2,1)S(1)} %bitcast_dynamic-update-slice_fusion.24), channel_id=1, source_target_pairs={{0,16},{4,20},{8,24},{12,28},{16,0},{20,4},{24,8},{28,12},{1,17},{... | collective-permute-start | bytes 1327112 | tf_op jit(solution)/shard_map/ppermute | solution.py:36
  58.0 24.7 %collective-permute-start.8 = (bf16[4,48,1152]{2,1,0:T(8,128)(2,1)S(1)}, bf16[4,48,1152]{2,1,0:T(8,128)(2,1)S(1)}, u32[]{:S(2)}, u32[]{:S(2)}) collective-permute-start(bf16[4,48,1152]{2,1,0:T(8,128)(2,1)S(1)} %bitcast_dynamic-update-slice_fusion.24), channel_id=1, source_target_pairs={{0,24},{4,28},{8,16},{12,20},{16,8},{20,12},{24,0},{28,4},{1,25},{... | collective-permute-start | bytes 1327112 | tf_op jit(solution)/shard_map/ppermute | solution.py:36
  62.5 31.9 %collective-permute-start.15 = (bf16[4,48,1536]{2,1,0:T(8,128)(2,1)S(1)}, bf16[4,48,1536]{2,1,0:T(8,128)(2,1)S(1)}, u32[]{:S(2)}, u32[]{:S(2)}) collective-permute-start(bf16[4,48,1536]{2,1,0:T(8,128)(2,1)S(1)} %bitcast_dynamic-update-slice_fusion.16), channel_id=1, source_target_pairs={{0,8},{4,12},{8,0},{12,4},{16,24},{20,28},{24,16},{28,20},{1,9},{5... | collective-permute-start | bytes 1769480 | tf_op jit(solution)/shard_map/ppermute | solution.py:36
  63.7 40.0 %collective-permute-start.16 = (bf16[4,48,1536]{2,1,0:T(8,128)(2,1)S(1)}, bf16[4,48,1536]{2,1,0:T(8,128)(2,1)S(1)}, u32[]{:S(2)}, u32[]{:S(2)}) collective-permute-start(bf16[4,48,1536]{2,1,0:T(8,128)(2,1)S(1)} %bitcast_dynamic-update-slice_fusion.16), channel_id=1, source_target_pairs={{0,16},{4,20},{8,24},{12,28},{16,0},{20,4},{24,8},{28,12},{1,17},{... | collective-permute-start | bytes 1769480 | tf_op jit(solution)/shard_map/ppermute | solution.py:36
  72.2 32.5 %collective-permute-start.17 = (bf16[4,48,1536]{2,1,0:T(8,128)(2,1)S(1)}, bf16[4,48,1536]{2,1,0:T(8,128)(2,1)S(1)}, u32[]{:S(2)}, u32[]{:S(2)}) collective-permute-start(bf16[4,48,1536]{2,1,0:T(8,128)(2,1)S(1)} %bitcast_dynamic-update-slice_fusion.16), channel_id=1, source_target_pairs={{0,24},{4,28},{8,16},{12,20},{16,8},{20,12},{24,0},{28,4},{1,25},{... | collective-permute-start | bytes 1769480 | tf_op jit(solution)/shard_map/ppermute | solution.py:36
  81.4 23.4 %collective-permute-start.25 = (bf16[1152,384]{1,0:T(8,128)(2,1)S(1)}, bf16[1152,384]{1,0:T(8,128)(2,1)S(1)}, u32[]{:S(2)}, u32[]{:S(2)}) collective-permute-start(bf16[1152,384]{1,0:T(8,128)(2,1)S(1)} %bitcast.192), channel_id=1, source_target_pairs={{0,4},{4,0},{8,12},{12,8},{16,20},{20,16},{24,28},{28,24},{1,5},{5... | collective-permute-start | bytes 2654216 | tf_op jit(solution)/shard_map/ppermute | solution.py:36
  82.7 22.4 %collective-permute-start.9 = (bf16[768,1152]{1,0:T(8,128)(2,1)S(1)}, bf16[768,1152]{1,0:T(8,128)(2,1)S(1)}, u32[]{:S(2)}, u32[]{:S(2)}) collective-permute-start(bf16[768,1152]{1,0:T(8,128)(2,1)S(1)} %bitcast.187), channel_id=1, source_target_pairs={{0,4},{4,0},{8,12},{12,8},{16,20},{20,16},{24,28},{28,24},{1,5},{5... | collective-permute-start | bytes 5308424 | tf_op jit(solution)/shard_map/ppermute | solution.py:36
  104.7 47.2 %collective-permute-start.18 = (bf16[768,1536]{1,0:T(8,128)(2,1)S(1)}, bf16[768,1536]{1,0:T(8,128)(2,1)}, u32[]{:S(2)}, u32[]{:S(2)}) collective-permute-start(bf16[768,1536]{1,0:T(8,128)(2,1)S(1)} %bitcast.186), channel_id=1, source_target_pairs={{0,4},{4,0},{8,12},{12,8},{16,20},{20,16},{24,28},{28,24},{1,5},{5... | collective-permute-start | bytes 7077896 | tf_op jit(solution)/shard_map/ppermute | solution.py:36
  226.7 15.8 %collective-permute-start.26 = (bf16[64,1536]{1,0:T(8,128)(2,1)S(1)}, bf16[64,1536]{1,0:T(8,128)(2,1)S(1)}, u32[]{:S(2)}, u32[]{:S(2)}) collective-permute-start(bf16[64,1536]{1,0:T(8,128)(2,1)S(1)} %get-tuple-element.129), channel_id=1, source_target_pairs={{0,1},{1,2},{2,3},{3,4},{4,5},{5,6},{6,7},{7,8},{8,9},{9,10},{10,1... | collective-permute-start | bytes 589832 | tf_op jit(solution)/shard_map/ppermute | solution.py:149
  233.4 26.7 %collective-permute-start.50 = (bf16[1152,384]{1,0:T(8,128)(2,1)}, bf16[1152,384]{1,0:T(8,128)(2,1)}, u32[]{:S(2)}, u32[]{:S(2)}) collective-permute-start(bf16[1152,384]{1,0:T(8,128)(2,1)} %constant_dynamic-slice_fusion.1), channel_id=1, source_target_pairs={{0,4},{4,0},{8,12},{12,8},{16,20},{20,16},{24,28},{28,24},{1,5},{5... | collective-permute-start | bytes 2654216 | tf_op jit(solution)/shard_map/ppermute | solution.py:36
  241.5 105.6 %collective-permute-start.39 = (bf16[768,1536]{1,0:T(8,128)(2,1)}, bf16[768,1536]{1,0:T(8,128)(2,1)}, u32[]{:S(2)}, u32[]{:S(2)}) collective-permute-start(bf16[768,1536]{1,0:T(8,128)(2,1)} %pad_maximum_fusion.2), channel_id=1, source_target_pairs={{0,4},{4,0},{8,12},{12,8},{16,20},{20,16},{24,28},{28,24},{1,5},{5... | collective-permute-start | bytes 7077896 | tf_op jit(solution)/shard_map/ppermute | solution.py:36
  259.6 56.3 %collective-permute-start.28 = (bf16[768,1152]{1,0:T(8,128)(2,1)}, bf16[768,1152]{1,0:T(8,128)(2,1)}, u32[]{:S(2)}, u32[]{:S(2)}) collective-permute-start(bf16[768,1152]{1,0:T(8,128)(2,1)} %constant_dynamic-slice_fusion.6), channel_id=1, source_target_pairs={{0,4},{4,0},{8,12},{12,8},{16,20},{20,16},{24,28},{28,24},{1,5},{5... | collective-permute-start | bytes 5308424 | tf_op jit(solution)/shard_map/ppermute | solution.py:36
  262.4 15.7 %collective-permute-start.51 = (bf16[4,72,384]{2,1,0:T(8,128)(2,1)}, bf16[4,72,384]{2,1,0:T(8,128)(2,1)S(1)}, u32[]{:S(2)}, u32[]{:S(2)}) collective-permute-start(bf16[4,72,384]{2,1,0:T(8,128)(2,1)} %get-tuple-element.110), channel_id=1, source_target_pairs={{0,8},{4,12},{8,0},{12,4},{16,24},{20,28},{24,16},{28,20},{1,9},{5... | collective-permute-start | bytes 663560 | tf_op jit(solution)/shard_map/ppermute | solution.py:36
  279.3 29.2 %collective-permute-start.54 = (bf16[72,384]{1,0:T(8,128)(2,1)S(1)}, bf16[72,384]{1,0:T(8,128)(2,1)S(1)}, u32[]{:S(2)}, u32[]{:S(2)}) collective-permute-start(bf16[72,384]{1,0:T(8,128)(2,1)S(1)} %get-tuple-element.131), channel_id=1, source_target_pairs={{0,1},{1,0},{2,3},{3,2},{4,5},{5,4},{6,7},{7,6},{8,9},{9,8},{10,11... | collective-permute-start | bytes 165896 | tf_op jit(solution)/shard_map/ppermute | solution.py:36
  279.5 29.0 %collective-permute-start.55 = (bf16[72,384]{1,0:T(8,128)(2,1)S(1)}, bf16[72,384]{1,0:T(8,128)(2,1)S(1)}, u32[]{:S(2)}, u32[]{:S(2)}) collective-permute-start(bf16[72,384]{1,0:T(8,128)(2,1)S(1)} %get-tuple-element.133), channel_id=1, source_target_pairs={{0,2},{1,3},{2,0},{3,1},{4,6},{5,7},{6,4},{7,5},{8,10},{9,11},{10,... | collective-permute-start | bytes 165896 | tf_op jit(solution)/shard_map/ppermute | solution.py:36
  283.1 25.4 %collective-permute-start.56 = (bf16[72,384]{1,0:T(8,128)(2,1)S(1)}, bf16[72,384]{1,0:T(8,128)(2,1)S(1)}, u32[]{:S(2)}, u32[]{:S(2)}) collective-permute-start(bf16[72,384]{1,0:T(8,128)(2,1)S(1)} %get-tuple-element.132), channel_id=1, source_target_pairs={{0,3},{1,2},{2,1},{3,0},{4,7},{5,6},{6,5},{7,4},{8,11},{9,10},{10,... | collective-permute-start | bytes 165896 | tf_op jit(solution)/shard_map/ppermute | solution.py:36
  320.6 21.8 %collective-permute-start.30 = (bf16[4,48,1152]{2,1,0:T(8,128)(2,1)S(1)}, bf16[4,48,1152]{2,1,0:T(8,128)(2,1)S(1)}, u32[]{:S(2)}, u32[]{:S(2)}) collective-permute-start(bf16[4,48,1152]{2,1,0:T(8,128)(2,1)S(1)} %get-tuple-element.103), channel_id=1, source_target_pairs={{0,16},{4,20},{8,24},{12,28},{16,0},{20,4},{24,8},{28,12},{1,17},{... | collective-permute-start | bytes 1327112 | tf_op jit(solution)/shard_map/ppermute | solution.py:36
  321.2 21.2 %collective-permute-start.31 = (bf16[4,48,1152]{2,1,0:T(8,128)(2,1)S(1)}, bf16[4,48,1152]{2,1,0:T(8,128)(2,1)S(1)}, u32[]{:S(2)}, u32[]{:S(2)}) collective-permute-start(bf16[4,48,1152]{2,1,0:T(8,128)(2,1)S(1)} %get-tuple-element.102), channel_id=1, source_target_pairs={{0,24},{4,28},{8,16},{12,20},{16,8},{20,12},{24,0},{28,4},{1,25},{... | collective-permute-start | bytes 1327112 | tf_op jit(solution)/shard_map/ppermute | solution.py:36
  355.0 31.2 %collective-permute-start.40 = (bf16[4,48,1536]{2,1,0:T(8,128)(2,1)S(1)}, bf16[4,48,1536]{2,1,0:T(8,128)(2,1)S(1)}, u32[]{:S(2)}, u32[]{:S(2)}) collective-permute-start(bf16[4,48,1536]{2,1,0:T(8,128)(2,1)S(1)} %get-tuple-element.94), channel_id=1, source_target_pairs={{0,8},{4,12},{8,0},{12,4},{16,24},{20,28},{24,16},{28,20},{1,9},{5... | collective-permute-start | bytes 1769480 | tf_op jit(solution)/shard_map/ppermute | solution.py:36
  356.4 29.7 %collective-permute-start.41 = (bf16[4,48,1536]{2,1,0:T(8,128)(2,1)S(1)}, bf16[4,48,1536]{2,1,0:T(8,128)(2,1)S(1)}, u32[]{:S(2)}, u32[]{:S(2)}) collective-permute-start(bf16[4,48,1536]{2,1,0:T(8,128)(2,1)S(1)} %get-tuple-element.96), channel_id=1, source_target_pairs={{0,16},{4,20},{8,24},{12,28},{16,0},{20,4},{24,8},{28,12},{1,17},{... | collective-permute-start | bytes 1769480 | tf_op jit(solution)/shard_map/ppermute | solution.py:36
  356.9 29.2 %collective-permute-start.42 = (bf16[4,48,1536]{2,1,0:T(8,128)(2,1)S(1)}, bf16[4,48,1536]{2,1,0:T(8,128)(2,1)S(1)}, u32[]{:S(2)}, u32[]{:S(2)}) collective-permute-start(bf16[4,48,1536]{2,1,0:T(8,128)(2,1)S(1)} %get-tuple-element.95), channel_id=1, source_target_pairs={{0,24},{4,28},{8,16},{12,20},{16,8},{20,12},{24,0},{28,4},{1,25},{... | collective-permute-start | bytes 1769480 | tf_op jit(solution)/shard_map/ppermute | solution.py:36
  358.5 27.6 %collective-permute-start.36 = (bf16[48,1152]{1,0:T(8,128)(2,1)S(1)}, bf16[48,1152]{1,0:T(8,128)(2,1)S(1)}, u32[]{:S(2)}, u32[]{:S(2)}) collective-permute-start(bf16[48,1152]{1,0:T(8,128)(2,1)S(1)} %get-tuple-element.81), channel_id=1, source_target_pairs={{0,16},{4,20},{8,24},{12,28},{16,0},{20,4},{24,8},{28,12},{1,17},{... | collective-permute-start | bytes 331784 | tf_op jit(solution)/shard_map/ppermute | solution.py:36
  360.2 31.5 %collective-permute-start.37 = (bf16[48,1152]{1,0:T(8,128)(2,1)S(1)}, bf16[48,1152]{1,0:T(8,128)(2,1)S(1)}, u32[]{:S(2)}, u32[]{:S(2)}) collective-permute-start(bf16[48,1152]{1,0:T(8,128)(2,1)S(1)} %get-tuple-element.81), channel_id=1, source_target_pairs={{0,24},{4,28},{8,16},{12,20},{16,8},{20,12},{24,0},{28,4},{1,25},{... | collective-permute-start | bytes 331784 | tf_op jit(solution)/shard_map/ppermute | solution.py:36
  (57 other events, 529.4 us)

commit v3 on v2

--- a/solution.py
+++ b/solution.py
@@ -36,12 +36,16 @@
     return lax.ppermute(value, axis, [(i, i ^ flip) for i in range(count)])
 
 
-def spread(part, axis, unit, index, count, dim):
+def after(value, *others):
+    return lax.optimization_barrier((value, *others))[0]
+
+
+def spread(part, axis, unit, index, count, dim, then=()):
     out = jnp.zeros(part.shape[:dim] + (count,) + part.shape[dim:], part.dtype)
-    pieces = [part] + [swap(part, axis, unit * d) for d in range(1, count)]
+    pieces = [part] + [after(swap(part, axis, unit * d), *then) for d in range(1, count)]
     for d, piece in enumerate(pieces):
         out = lax.dynamic_update_slice_in_dim(out, jnp.expand_dims(piece, dim), index ^ d, dim)
-    return out
+    return out, pieces[1:]
 
 
 def places():
@@ -63,40 +67,38 @@
     return lax.dynamic_slice_in_dim(weight, core * width, width, 1)
 
 
-def gather_parts(block):
-    core, quarter, shard = places()
+def quarter_rows(block):
     quarters = lax.axis_size("seq") // 2
     rows = block.shape[0] // quarters
-    part = lax.dynamic_slice_in_dim(block, quarter * rows, rows, 0)
-    part = spread(part, "shard", 1, shard, lax.axis_size("shard"), 0)
-    part = spread(part, "seq", 2, quarter, quarters, 1)
-    part = part.reshape(-1, block.shape[1])
-    return by_core(core, part, swap(part, "seq", 1))
-
-
-def gather_weights(qkv, attn, mlp, down):
-    qkv, attn, mlp, down = (w.astype(bf16) for w in (qkv, attn, mlp, down))
-    if not split_pays():
-        return tuple(lax.all_gather(w, "shard", axis=0, tiled=True) for w in (qkv, attn, mlp, down))
-    core, _, _ = places()
-    full_qkv = jnp.concatenate(gather_parts(halves(qkv, core)), axis=1)
-    first, second = gather_parts(
-        jnp.concatenate([halves(mlp, core), halves(attn, core)], axis=1)
-    )
-    width = mlp.shape[1] // 2
-    full_mlp = jnp.concatenate([first[:, :width], second[:, :width]], axis=1)
-    full_attn = jnp.concatenate([first[:, width:], second[:, width:]], axis=1)
-    full_down = jnp.concatenate(gather_parts(halves(down, core)), axis=1)
-    return full_qkv, full_attn, full_mlp, full_down
-
-
-def gather_gains(gains):
-    shards = lax.axis_size("shard")
-    low = gains.astype(bf16)
-    if not split_pays():
-        return lax.all_gather(low, "shard", axis=1, tiled=True).astype(f32)
-    full = spread(low, "shard", 1, lax.axis_index("shard"), shards, 1)
-    return full.reshape(gains.shape[0], -1).astype(f32)
+    return lax.dynamic_slice_in_dim(block, (lax.axis_index("seq") // 2) * rows, rows, 0)
+
+
+def over_shard(part):
+    return spread(part, "shard", 1, lax.axis_index("shard"), lax.axis_size("shard"), 0)
+
+
+def over_quarters(part, then=()):
+    count = lax.axis_size("seq")
+    part, _ = spread(part, "seq", 2, lax.axis_index("seq") // 2, count // 2, 1, then)
+    return part.reshape(-1, part.shape[-1])
+
+
+def pack_down(blocks, rows):
+    rest = blocks.shape[1] - rows
+    second = jnp.pad(blocks[:, rows:], ((0, 0), (0, rows - rest), (0, 0)))
+    columns = blocks.shape[2]
+    return [blocks[:, :rows].reshape(-1, columns), second.reshape(-1, columns)]
+
+
+def unpack_down(packed, blocks, rest):
+    columns = packed.shape[1] // 2
+    packed = packed.reshape(blocks, -1, 2 * columns)
+    whole = jnp.concatenate([packed[:, :, :columns], packed[:, :rest, columns:]], axis=1)
+    return whole.reshape(-1, columns)
+
+
+def side_by_side(first, second):
+    return jnp.concatenate([first, second], axis=1)
 
 
 def total_of(pieces):
@@ -106,24 +108,34 @@
     return total.astype(bf16)
 
 
-def reduce_parts(own, other):
-    core, quarter, shard = places()
-    quarters, shards = lax.axis_size("seq") // 2, lax.axis_size("shard")
-    rows = own.shape[0] // (quarters * shards)
-    half = total_of([own, swap(other, "seq", 1)]).reshape(shards, quarters, rows, -1)
-
-    def at(value, index, dim):
-        return lax.dynamic_index_in_dim(value, index, dim, keepdims=False)
-
-    half = total_of(
-        [at(half, quarter, 1)]
-        + [swap(at(half, quarter ^ d, 1), "seq", 2 * d) for d in range(1, quarters)]
-    )
-    half = total_of(
-        [at(half, shard, 0)] + [swap(at(half, shard ^ d, 0), "shard", d) for d in range(1, shards)]
-    )
-    half = spread(half, "seq", 2, quarter, quarters, 0).reshape(quarters * rows, -1)
-    return by_core(core, half, swap(half, "seq", 1))
+def keep_half(own, got):
+    shards, quarters = lax.axis_size("shard"), lax.axis_size("seq") // 2
+    return total_of([own, got]).reshape(shards, quarters, -1, own.shape[1])
+
+
+def sum_after(parts, *others):
+    return total_of(parts[:1] + [after(part, *others) for part in parts[1:]])
+
+
+def pieces(value, axis, unit, index, count, dim):
+    def at(place):
+        return lax.dynamic_index_in_dim(value, place, dim, keepdims=False)
+
+    return [at(index)] + [swap(at(index ^ d), axis, unit * d) for d in range(1, count)]
+
+
+def quarter_pieces(half):
+    return pieces(half, "seq", 2, lax.axis_index("seq") // 2, lax.axis_size("seq") // 2, 1)
+
+
+def shard_pieces(half):
+    return pieces(half, "shard", 1, lax.axis_index("shard"), lax.axis_size("shard"), 0)
+
+
+def owners_half(part, then=()):
+    count = lax.axis_size("seq")
+    part, _ = spread(part, "seq", 2, lax.axis_index("seq") // 2, count // 2, 0, then)
+    return part.reshape(-1, part.shape[-1])
 
 
 def reduce_whole(grad):
@@ -131,16 +143,9 @@
     return lax.psum(owned.astype(f32), "seq")
 
 
-def reduce_pair(grad):
-    core, _, _ = places()
-    return reduce_parts(halves(grad, core), halves(grad, 1 - core))
-
-
-def reduce_gains(grad):
-    columns = grad.shape[1] // lax.axis_size("shard")
-    owned = lax.psum(grad, "seq")
-    owned = lax.psum(owned, "shard")
-    return lax.dynamic_slice_in_dim(owned, lax.axis_index("shard") * columns, columns, 1)
+def gain_grad(weight, gradient, gain):
+    low = weight.astype(bf16).astype(f32)
+    return jnp.sum(low * gradient.astype(f32), axis=1) / gain.astype(bf16).astype(f32)
 
 
 def to_right(value):
@@ -238,6 +243,21 @@
                 value = value * scale
             ref[:, j : j + LANES] = value.astype(bf16)
     v_ref[...] = dot(low, w_ref[:, 2 * width :]).astype(bf16)
+
+
+def project_edges_kernel(x_ref, gain_ref, w_ref, cos_ref, sin_ref, head_ref, tail_ref):
+    unit, _ = normed(x_ref[...].astype(f32))
+    low = (unit * gain_ref[0:1, :]).astype(bf16)
+    width = low.shape[1]
+    cos, sin = cos_ref[...], sin_ref[...]
+    keys = dot(low, w_ref[:, width : 2 * width])
+    for j in range(0, width, LANES):
+        value = rope(keys[:, j : j + LANES], cos, sin).astype(bf16)
+        head_ref[:, j : j + LANES] = value[:HALF]
+        tail_ref[:, j : j + LANES] = value[HALF:]
+    values = dot(low, w_ref[:, 2 * width :]).astype(bf16)
+    head_ref[:, width:] = values[:HALF]
+    tail_ref[:, width:] = values[HALF:]
 
 
 def fill(dst, left, middle, right):
@@ -272,24 +292,8 @@
         lse_ref[0, 1:2, own] = lse[:, ROWS:]
 
 
-def attend_back_kernel(
-    meta_ref, q_ref, k_ref, v_ref, do_ref, kl_ref, vl_ref, kr_ref, vr_ref, lse_ref, cos_ref, sin_ref,
-    dq_ref, dk_ref, dv_ref, hk_ref, hv_ref, ek_ref, ev_ref,
-    kx, vx, bias, dkx, dvx,
-):
-    rows = q_ref.shape[0]
-    blocks = rows // ROWS
-
-    @pl.when(pl.program_id(0) == 0)
-    def _():
-        for n in range(blocks):
-            bias[n] = mask_bias(meta_ref, n, ROWS + 2 * HALF)
-
-    fill(kx, kl_ref, k_ref, kr_ref)
-    fill(vx, vl_ref, v_ref, vr_ref)
-    dkx[...] = jnp.zeros_like(dkx)
-    dvx[...] = jnp.zeros_like(dvx)
-    for n in range(blocks):
+def back_blocks(blocks, dq_at, q_ref, do_ref, kx, vx, bias, lse_ref, cos_ref, sin_ref, dq_ref, dkx, dvx):
+    for n in blocks:
         own = slice(n * ROWS, (n + 1) * ROWS)
         queries = stacked(q_ref[own, :])
         grads = stacked(do_ref[own, :])
@@ -304,21 +308,79 @@
         dvx[window(n), :] += dot(probs.astype(bf16), grads)
         dkx[window(n), :] += dot(grad_scores, queries)
         grad_query = unstacked(dot_columns(keys, grad_scores)) * 0.125
-        dq_ref[own, :] = rope_back(grad_query, cos_ref[own, :], sin_ref[own, :]).astype(bf16)
+        at = dq_at(n) * ROWS
+        dq_ref[at : at + ROWS, :] = rope_back(
+            grad_query, cos_ref[own, :], sin_ref[own, :]
+        ).astype(bf16)
+
+
+def attend_back_edges_kernel(
+    meta_ref, q_ref, k_ref, v_ref, do_ref, kl_ref, vl_ref, kr_ref, vr_ref, lse_ref, cos_ref, sin_ref,
+    dq_ref, wk_ref, wv_ref, hk_ref, hv_ref,
+    kx, vx, bias, dkx, dvx,
+):
+    rows = q_ref.shape[0]
+    blocks = rows // ROWS
+    span = ROWS + 2 * HALF
+
+    @pl.when(pl.program_id(0) == 0)
+    def _():
+        for n in (0, blocks - 1):
+            bias[n] = mask_bias(meta_ref, n, span)
+
+    fill(kx, kl_ref, k_ref, kr_ref)
+    fill(vx, vl_ref, v_ref, vr_ref)
+    for acc in (dkx, dvx):
+        acc[window(0), :] = jnp.zeros((span, LANES), f32)
+        acc[window(blocks - 1), :] = jnp.zeros((span, LANES), f32)
+    back_blocks(
+        (0, blocks - 1), lambda n: min(n, 1),
+        q_ref, do_ref, kx, vx, bias, lse_ref, cos_ref, sin_ref, dq_ref, dkx, dvx,
+    )
+    for ref, acc in ((wk_ref, dkx), (wv_ref, dvx)):
+        ref[:span, :] = acc[window(0), :]
+        ref[span:, :] = acc[window(blocks - 1), :]
+    for ref, acc in ((hk_ref, dkx), (hv_ref, dvx)):
+        ref[0:HALF, :] = acc[0:HALF, :].astype(bf16)
+        ref[HALF:, :] = acc[HALF + rows :, :].astype(bf16)
+
+
+def attend_back_kernel(
+    meta_ref, q_ref, k_ref, v_ref, do_ref, kl_ref, vl_ref, kr_ref, vr_ref, lse_ref, cos_ref, sin_ref,
+    eq_ref, wk_ref, wv_ref,
+    dq_ref, dk_ref, dv_ref,
+    kx, vx, bias, dkx, dvx,
+):
+    rows = q_ref.shape[0]
+    blocks = rows // ROWS
+    span = ROWS + 2 * HALF
+
+    @pl.when(pl.program_id(0) == 0)
+    def _():
+        for n in range(1, blocks - 1):
+            bias[n] = mask_bias(meta_ref, n, span)
+
+    fill(kx, kl_ref, k_ref, kr_ref)
+    fill(vx, vl_ref, v_ref, vr_ref)
+    last = window(blocks - 1)
+    for acc, ref in ((dkx, wk_ref), (dvx, wv_ref)):
+        acc[window(0), :] = ref[:span, :]
+        acc[span : last.start, :] = jnp.zeros((last.start - span, LANES), f32)
+        acc[last, :] = ref[span:, :]
+    dq_ref[:ROWS, :] = eq_ref[:ROWS, :]
+    dq_ref[rows - ROWS :, :] = eq_ref[ROWS:, :]
+    back_blocks(
+        range(1, blocks - 1), lambda n: n,
+        q_ref, do_ref, kx, vx, bias, lse_ref, cos_ref, sin_ref, dq_ref, dkx, dvx,
+    )
     middle = slice(HALF, HALF + rows)
     dk_ref[...] = rope_back(dkx[middle, :], cos_ref[...], sin_ref[...]).astype(bf16)
     dv_ref[...] = dvx[middle, :].astype(bf16)
-    for ref, acc in ((hk_ref, dkx), (hv_ref, dvx)):
-        ref[0:HALF, :] = acc[0:HALF, :].astype(bf16)
-        ref[HALF:, :] = acc[HALF + rows :, :].astype(bf16)
-    for ref, acc in ((ek_ref, dkx), (ev_ref, dvx)):
-        ref[0:HALF, :] = acc[HALF : 2 * HALF, :]
-        ref[HALF:, :] = acc[rows : rows + HALF, :]
 
 
 def middle_kernel(
     x_ref, o_ref, ct_ref, gain_ref, wa_ref, wm_ref, wd_ref,
-    out_ref, dmid_ref, do_ref, gd_ref, gm_ref, ga_ref, gg_ref,
+    out_ref, dmid_ref, do_ref, gd_ref, gm_ref, ga_ref,
     acc_d, acc_m, acc_a,
 ):
     step = pl.program_id(0)
@@ -328,7 +390,6 @@
         acc_d[...] = jnp.zeros_like(acc_d)
         acc_m[...] = jnp.zeros_like(acc_m)
         acc_a[...] = jnp.zeros_like(acc_a)
-        gg_ref[...] = jnp.zeros_like(gg_ref)
 
     gain = gain_ref[1:2, :]
     hidden = wd_ref.shape[0]
@@ -350,7 +411,6 @@
     acc_m[:, :hidden] += dot_columns(low, da1)
     acc_m[:, hidden:] += dot_columns(low, da2)
     dh = dot_rows(da1, wm_ref[:, :hidden]) + dot_rows(da2, wm_ref[:, hidden:])
-    gg_ref[...] += jnp.sum(dh * unit, axis=0, keepdims=True)
     dmid = ct.astype(f32) + normed_back(dh, gain, unit, inverse)
     dmid_ref[...] = dmid
     dmr = dmid.astype(bf16)
@@ -391,19 +451,14 @@
         g_ref[...] = acc[...].astype(bf16)
 
 
-def input_kernel(x_ref, gain_ref, w_ref, dmid_ref, dq_ref, dk_ref, dv_ref, ek_ref, ev_ref, dx_ref, gg_ref):
+def input_kernel(x_ref, gain_ref, w_ref, dmid_ref, dq_ref, dk_ref, dv_ref, ek_ref, ev_ref, dx_ref):
     step, steps = pl.program_id(0), pl.num_programs(0)
     rows, width = x_ref.shape
-
-    @pl.when(step == 0)
-    def _():
-        gg_ref[...] = jnp.zeros_like(gg_ref)
 
     dh = dot_rows(dq_ref[...], w_ref[:, :width])
     dh = dh + dot_rows(patched(step, steps, rows, dk_ref, ek_ref), w_ref[:, width : 2 * width])
     dh = dh + dot_rows(patched(step, steps, rows, dv_ref, ev_ref), w_ref[:, 2 * width :])
     unit, inverse = normed(x_ref[...].astype(f32))
-    gg_ref[...] += jnp.sum(dh * unit, axis=0, keepdims=True)
     dx = dmid_ref[...] + normed_back(dh, gain_ref[0:1, :], unit, inverse)
     dx_ref[...] = dx.astype(bf16)
 
@@ -439,7 +494,9 @@
         compiler_params=pltpu.CompilerParams(
             vmem_limit_bytes=vmem_bytes, dimension_semantics=("arbitrary",)
         ),
-        cost_estimate=pl.CostEstimate(flops=flops, bytes_accessed=moved, transcendentals=0),
+        cost_estimate=pl.CostEstimate(
+            flops=flops // 8, bytes_accessed=moved // 8, transcendentals=0
+        ),
     )
 
 
@@ -455,6 +512,20 @@
         [],
         2 * rows * width * 3 * width,
         rows * width * 10 + weight.size * 2,
+    )(x, gains, weight, cos, sin)
+
+
+def project_edges(x, gains, weight, cos, sin):
+    rows, width = x.shape
+    return call(
+        project_edges_kernel,
+        1,
+        [held(rows, width), held(2, width), kept(*weight.shape), held(rows, LANES), held(rows, LANES)],
+        [held(HALF, 2 * width)] * 2,
+        [shaped((HALF, 2 * width), bf16)] * 2,
+        [],
+        4 * rows * width * width,
+        rows * width * 6 + weight.size * 2,
     )(x, gains, weight, cos, sin)
 
 
@@ -484,26 +555,52 @@
     )(meta, q, k, v, left, left, right, right)
 
 
-def attend_back(meta, q, k, v, do, left, right, lse, cos, sin):
+def back_specs(rows, steps):
+    return (
+        [pl.BlockSpec(memory_space=pltpu.SMEM)]
+        + [pairs(rows)] * 4
+        + [pairs(HALF), pairs(HALF, steps)] * 2
+        + [pl.BlockSpec((1, 2, rows), lambda i: (i, 0, 0)), held(rows, LANES), held(rows, LANES)]
+    )
+
+
+def back_scratch(rows):
+    extended = rows + 2 * HALF
+    return attend_scratch(rows) + [pltpu.VMEM((extended, LANES), f32)] * 2
+
+
+def attend_back_edges(meta, q, k, v, do, left, right, lse, cos, sin):
     rows, width = q.shape
     steps = width // LANES
-    extended = rows + 2 * HALF
+    span = 2 * (ROWS + 2 * HALF)
+    return call(
+        attend_back_edges_kernel,
+        steps,
+        back_specs(rows, steps),
+        [pairs(2 * ROWS)] + [pairs(span)] * 2 + [pairs(2 * HALF)] * 2,
+        [shaped((2 * ROWS, width), bf16)]
+        + [shaped((span, width), f32)] * 2
+        + [shaped((2 * HALF, width), bf16)] * 2,
+        back_scratch(rows),
+        20 * 2 * ROWS * width * 256,
+        rows * width * 10,
+    )(meta, q, k, v, do, left, left, right, right, lse, cos, sin)
+
+
+def attend_back(meta, q, k, v, do, left, right, lse, cos, sin, edges):
+    rows, width = q.shape
+    steps = width // LANES
+    span = 2 * (ROWS + 2 * HALF)
     return call(
         attend_back_kernel,
         steps,
-        [pl.BlockSpec(memory_space=pltpu.SMEM)]
-        + [pairs(rows)] * 4
-        + [pairs(HALF), pairs(HALF, steps)] * 2
-        + [pl.BlockSpec((1, 2, rows), lambda i: (i, 0, 0)), held(rows, LANES), held(rows, LANES)],
-        [pairs(rows)] * 3 + [pairs(2 * HALF)] * 4,
-        [shaped((rows, width), bf16)] * 3
-        + [shaped((2 * HALF, width), bf16)] * 2
-        + [shaped((2 * HALF, width), f32)] * 2,
-        attend_scratch(rows)
-        + [pltpu.VMEM((extended, LANES), f32), pltpu.VMEM((extended, LANES), f32)],
+        back_specs(rows, steps) + [pairs(2 * ROWS)] + [pairs(span)] * 2,
+        [pairs(rows)] * 3,
+        [shaped((rows, width), bf16)] * 3,
+        back_scratch(rows),
         20 * rows * width * 256,
         rows * width * 14,
-    )(meta, q, k, v, do, left, left, right, right, lse, cos, sin)
+    )(meta, q, k, v, do, left, left, right, right, lse, cos, sin, *edges)
 
 
 def middle(x, o, ct, gains, wa, wm, wd):
@@ -513,7 +610,7 @@
         middle_kernel,
         rows // tile,
         [tiles(tile, width)] * 3 + [held(2, width), kept(*wa.shape), kept(*wm.shape), kept(*wd.shape)],
-        [tiles(tile, width)] * 3 + [held(*wd.shape), held(*wm.shape), held(*wa.shape), held(1, width)],
+        [tiles(tile, width)] * 3 + [held(*wd.shape), held(*wm.shape), held(*wa.shape)],
         [
             shaped((rows, width), bf16),
             shaped((rows, width), f32),
@@ -521,7 +618,6 @@
             shaped(wd.shape, bf16),
             shaped(wm.shape, bf16),
             shaped(wa.shape, bf16),
-            shaped((1, width), f32),
         ],
         [pltpu.VMEM(wd.shape, f32), pltpu.VMEM(wm.shape, f32), pltpu.VMEM(wa.shape, f32)],
         6 * rows * (wa.size + wm.size + wd.size),
@@ -553,8 +649,8 @@
         [tiles(tile, width), held(2, width), kept(*weight.shape)]
         + [tiles(tile, width)] * 4
         + [held(2 * HALF, width)] * 2,
-        [tiles(tile, width), held(1, width)],
-        [shaped((rows, width), bf16), shaped((1, width), f32)],
+        tiles(tile, width),
+        shaped((rows, width), bf16),
         [],
         6 * rows * width * width,
         rows * width * 14 + 6 * width * width,
@@ -619,57 +715,132 @@
     rows, width = tokens.shape
     device = lax.axis_index(("seq", "shard"))
     last_device = lax.axis_size(("seq", "shard")) - 1
-    full_qkv, full_attn, full_mlp, full_down = gather_weights(
-        qkv_weight, attn_weight, mlp_weight, down_weight
-    )
-    gains = gather_gains(norm_gains)
     cos, sin = rope_tables(positions, width // HEADS)
     start = jnp.max(jnp.where(positions == 0, jnp.arange(rows, dtype=jnp.int32), 0))
     low = jnp.where(device > 0, -HALF, 0)
     high = jnp.where(device < last_device, rows + HALF, rows)
     meta = jnp.stack([start, low, high]).astype(jnp.int32)
-
-    h, q, k, v = project(tokens, gains, full_qkv, cos, sin)
-    k_head, k_tail = edge_rows(k)
-    v_head, v_tail = edge_rows(v)
-    left = to_right(jnp.concatenate([k_tail, v_tail], axis=1))
-    right = to_left(jnp.concatenate([k_head, v_head], axis=1))
+    shards = lax.axis_size("shard")
+    quarters = lax.axis_size("seq") // 2
+    core = lax.axis_index("seq") % 2
+    split = split_pays()
+    half = qkv_weight.shape[1] // 2
+    slot = qkv_weight.shape[0] // quarters
+    rest = down_weight.shape[0] // quarters - slot
+    wide = mlp_weight.shape[1] // 2
+    down_at = wide + attn_weight.shape[1] // 2
+    lows = [w.astype(bf16) for w in (qkv_weight, attn_weight, mlp_weight, down_weight)]
+    if split:
+        qkv_low, attn_low, mlp_low, down_low = lows
+        part = quarter_rows(halves(qkv_low, core))
+        gain_rows = jnp.pad(norm_gains.astype(bf16), ((0, 6), (0, half - norm_gains.shape[1])))
+        qkv_part, arrived = over_shard(jnp.concatenate([part, gain_rows], axis=0))
+        gains = qkv_part[:, slot : slot + 2, : norm_gains.shape[1]].astype(f32)
+        gains = gains.transpose(1, 0, 2).reshape(2, -1)
+        down_part = quarter_rows(halves(down_low, core))
+        rest_part = jnp.concatenate(
+            [quarter_rows(halves(w, core)) for w in (mlp_low, attn_low)]
+            + pack_down(down_part[None], slot),
+            axis=1,
+        )
+        rest_part, _ = over_shard(after(rest_part, *arrived[:1]))
+        qkv_part = over_quarters(qkv_part[:, :slot])
+        rest_part = after(rest_part, qkv_part)
+        full_qkv = side_by_side(*by_core(core, qkv_part, swap(qkv_part, "seq", 1)))
+    else:
+        full_qkv, full_attn, full_mlp, full_down = (
+            lax.all_gather(w, "shard", axis=0, tiled=True) for w in lows
+        )
+        gains = lax.all_gather(norm_gains.astype(bf16), "shard", axis=1, tiled=True).astype(f32)
+    edge_x, edge_cos, edge_sin = (
+        jnp.concatenate(edge_rows(value), axis=0) for value in (tokens, cos, sin)
+    )
+    kv_head, kv_tail = project_edges(edge_x, gains, full_qkv, edge_cos, edge_sin)
+    left = to_right(kv_tail)
+    right = to_left(kv_head)
+    h, q, k, v = project(after(tokens, kv_head), gains, full_qkv, cos, sin)
+    left = after(left, k)
+    right = after(right, k)
     o, lse = attend(meta, q, k, v, left, right)
-    layer_output, dmid, do, down_grad, mlp_grad, attn_grad, gain_mlp_grad = middle(
+    if split:
+        rest_part = over_quarters(rest_part, (o,))
+    if split:
+        first, second = by_core(core, rest_part, swap(rest_part, "seq", 1))
+        full_mlp = side_by_side(first[:, :wide], second[:, :wide])
+        full_attn = side_by_side(first[:, wide:down_at], second[:, wide:down_at])
+        full_down = side_by_side(
+            *(unpack_down(x[:, down_at:], shards * quarters, rest) for x in (first, second))
+        )
+    layer_output, dmid, do, down_grad, mlp_grad, attn_grad = middle(
         tokens, o, cotangent, gains, full_attn, full_mlp, full_down
     )
-    dq, dk, dv, halo_k, halo_v, edge_k, edge_v = attend_back(
-        meta, q, k, v, do, left, right, lse, cos, sin
-    )
-    halo = jnp.concatenate([halo_k, halo_v], axis=1)
+    if split:
+
+        def packed(c):
+            down = halves(down_grad, c).reshape(shards * quarters, slot + rest, -1)
+            return jnp.concatenate(
+                [halves(mlp_grad, c), halves(attn_grad, c)] + pack_down(down, slot), axis=1
+            )
+
+        rest_got = swap(packed(1 - core), "seq", 1)
+    back_args = (meta, q, k, v, do, left, right, lse, cos, sin)
+    *edges, halo_k, halo_v = attend_back_edges(*back_args)
+    halo = side_by_side(halo_k, halo_v)
     from_right = to_left(halo[:HALF])
     from_left = to_right(halo[HALF:])
-    arrived = jnp.concatenate([from_left, from_right], axis=0).astype(f32)
-    edge_cos = jnp.concatenate(edge_rows(cos), axis=0)
-    edge_sin = jnp.concatenate(edge_rows(sin), axis=0)
-    edge_k = rope_back_wide(edge_k + arrived[:, :width], edge_cos, edge_sin).astype(bf16)
-    edge_v = (edge_v + arrived[:, width:]).astype(bf16)
+    if split:
+        rest_half = keep_half(packed(core), after(rest_got, halo_k))
+        do = after(do, rest_half)
+        back_args = (meta, q, k, v, do, left, right, lse, cos, sin)
+        rest_pieces = quarter_pieces(rest_half)
+    dq, dk, dv = attend_back(*back_args, edges)
+    arrived = jnp.concatenate([after(from_left, dq), after(from_right, dq)], axis=0).astype(f32)
+    _, window_k, window_v = edges
+    span = ROWS + 2 * HALF
+
+    def own_edges(windows):
+        return jnp.concatenate(
+            [windows[HALF : 2 * HALF], windows[2 * span - 2 * HALF : 2 * span - HALF]], axis=0
+        )
+
+    edge_k = rope_back_wide(
+        own_edges(window_k) + arrived[:, :width], edge_cos, edge_sin
+    ).astype(bf16)
+    edge_v = (own_edges(window_v) + arrived[:, width:]).astype(bf16)
     qkv_grad = qkv_gradient(h, dq, dk, dv, edge_k, edge_v)
-    input_grad, gain_attn_grad = input_gradient(
-        tokens, gains, full_qkv, dmid, dq, dk, dv, edge_k, edge_v
-    )
-    gains_total = reduce_gains(jnp.concatenate([gain_attn_grad, gain_mlp_grad], axis=0))
-    if split_pays():
-        core, _, _ = places()
-        wide = mlp_weight.shape[1] // 2
-        down_total = jnp.concatenate(reduce_pair(down_grad), axis=1)
-        own, other = (
-            jnp.concatenate([halves(mlp_grad, c), halves(attn_grad, c)], axis=1)
-            for c in (core, 1 - core)
+    if split:
+        rest_part = sum_after(rest_pieces, qkv_grad)
+        qkv_got = swap(after(halves(qkv_grad, 1 - core), rest_part), "seq", 1)
+        qkv_half = keep_half(halves(qkv_grad, core), qkv_got)
+        dq = after(dq, qkv_half)
+        qkv_pieces = quarter_pieces(qkv_half)
+        rest_pieces = shard_pieces(rest_part)
+    input_grad = input_gradient(tokens, gains, full_qkv, dmid, dq, dk, dv, edge_k, edge_v)
+    if split:
+        qkv_part = sum_after(qkv_pieces, input_grad)
+        rest_part = sum_after(rest_pieces, qkv_part)
+        qkv_part = sum_after(shard_pieces(qkv_part), rest_part)
+        rest_half = owners_half(rest_part, (qkv_part,))
+        rest_got = swap(rest_half, "seq", 1)
+        qkv_half = owners_half(qkv_part, (rest_half,))
+        qkv_got = swap(qkv_half, "seq", 1)
+        first, second = by_core(core, rest_half, after(rest_got, qkv_half))
+        mlp_total = side_by_side(first[:, :wide], second[:, :wide])
+        attn_total = side_by_side(first[:, wide:down_at], second[:, wide:down_at])
+        down_total = side_by_side(
+            *(unpack_down(x[:, down_at:], quarters, rest) for x in (first, second))
         )
-        first, second = reduce_parts(own, other)
-        mlp_total = jnp.concatenate([first[:, :wide], second[:, :wide]], axis=1)
-        attn_total = jnp.concatenate([first[:, wide:], second[:, wide:]], axis=1)
-        qkv_total = jnp.concatenate(reduce_pair(qkv_grad), axis=1)
+        qkv_total = side_by_side(*by_core(core, qkv_half, qkv_got))
     else:
         down_total, mlp_total, attn_total, qkv_total = (
             reduce_whole(g) for g in (down_grad, mlp_grad, attn_grad, qkv_grad)
         )
+    gains_total = jnp.stack(
+        [
+            gain_grad(qkv_weight, qkv_total, norm_gains[0]),
+            gain_grad(mlp_weight, mlp_total, norm_gains[1]),
+        ]
+    )
     qkv_new = adam_update(qkv_weight, qkv_first, qkv_second, qkv_total, rate_matrix)
     attn_new = adam_update(attn_weight, attn_first, attn_second, attn_total, rate_matrix)
     mlp_new = adam_update(mlp_weight, mlp_first, mlp_second, mlp_total, rate_matrix)

time: 426 us -> 348 us (0.82)
  waiting for transfers between devices: 119 us -> 55.5 us
  starting transfers between devices: 90.5 us -> 59.6 us
  local copies, waits for them, and re-layouts: 22.5 us -> 49.5 us
  blocking collectives: 24 us -> 0 us
  Pallas kernels: 121 us -> 131 us
  other arithmetic: 37.9 us -> 43.2 us
    ppermute x57 -> x36, waiting for transfers between devices: 114 us -> 55.5 us  [swap(): return lax.ppermute(value, axis, [(i, i ^ flip) for i in range(count)])]
    ppermute x57 -> x36, starting transfers between devices: 78.9 us -> 50 us  [swap(): return lax.ppermute(value, axis, [(i, i ^ flip) for i in range(count)])]
    psum x2 -> x0, blocking collectives: 24 us -> none  [the longest x1 12.4 us: reduce_gains(): owned = lax.psum(grad, 'seq')]
    pallas_call x1 -> x3, Pallas kernels: 24.4 us -> 34 us  [the longest x1 20.8 us: attend_back(): call(attend_back_kernel, steps, back_specs(rows, steps) + [pairs(2 * ROWS...]
    dynamic_update_slice x36 -> x21, local copies, waits for them, and re-layouts: 4.71 us -> 12 us  [spread(): lax.dynamic_update_slice_in_dim(out, jnp.expand_dims(piece, dim), index ^...]
    slice x8 -> x28, local copies, waits for them, and re-layouts: 0.5 us -> 6.87 us  [the longest x2 2.87 us: own_edges(): windows[HALF:2 * HALF]]
    convert_element_type x4 -> x6, other arithmetic: 1.57 us -> 6.66 us  [the longest x1 1.91 us: per_device(): edge_v = (own_edges(window_v) + arrived[:, width:]).astype(bf16)]
    concatenate x10 -> x16, other arithmetic: 8.9 us -> 11.1 us  [the longest x4 6.49 us: side_by_side(): return jnp.concatenate([first, second], axis=1)]
  transfers between devices with their start and end apart: 61 -> 40, of which waited for: 27 -> 13; matrix products, arithmetic and copies ran while one was open for 10% -> 17% of each run, Pallas kernels for 13% -> 26%
where the time goes in v3:
time: 348 us; the launch traced here: 341 us
  Pallas kernels  131 us (38%)
  starting transfers between devices  59.6 us (17%)
  waiting for transfers between devices  55.5 us (16%)
  local copies, waits for them, and re-layouts  49.5 us (14%)
  other arithmetic  43.2 us (12%)
    ppermute x36, waiting for transfers between devices, swap(): return lax.ppermute(value, axis, [(i, i ^ flip) for i in range(count)])  55.5 us
    ppermute x36, starting transfers between devices, swap(): return lax.ppermute(value, axis, [(i, i ^ flip) for i in range(count)])  50 us
    pallas_call x1, Pallas kernels, middle(): call(middle_kernel, rows // tile, [tiles(tile, width)] * 3 + [held(2, wid...  42.8 us
    pallas_call x1, Pallas kernels, attend(): call(attend_kernel, steps, [pl.BlockSpec(memory_space=pltpu.SMEM)] + [pai...  21.9 us
    pallas_call x1, Pallas kernels, attend_back(): call(attend_back_kernel, steps, back_specs(rows, steps) + [pairs(2 * ROWS...  20.8 us
    dynamic_update_slice x21, local copies, waits for them, and re-layouts, spread(): lax.dynamic_update_slice_in_dim(out, jnp.expand_dims(piece, dim), index ^...  12 us
    pallas_call x1, Pallas kernels, input_gradient(): call(input_kernel, rows // tile, [tiles(tile, width), held(2, width), kep...  11.7 us
    sub x5, other arithmetic, adam_update(): master - step_rate * (decay_rate * master + first_hat / (jnp.sqrt(second_...  11 us
  transfers between devices with their start and end apart: 40, of which 13 were waited for; matrix products, arithmetic and copies ran while one was open for 17% of the time, Pallas kernels for 26%

profile of v3, /device:TPU:0, one launch (start us, length us, event | category | flops | bytes accessed | tf_op | source)
XLA Modules:
  0.0 340.9 jit_solution(5523091636085664653)
XLA Ops:
  2.6 3.1 collective-permute-start
  5.7 2.6 collective-permute-start.1
  12.4 2.4 fusion.14
  20.0 3.5 %collective-permute-start.10 = (bf16[48,2304]{1,0:T(8,128)(2,1)S(1)}, bf16[48,2304]{1,0:T(8,128)(2,1)}, u32[]{:S(2)}, u32[]{:S(2)}) collective-permute-start(bf16[48,2304]{1,0:T(8,128)(2,1)S(1)} %pad_maximum_fusion.11), channel_id=1, source_target_pairs={{0,2},{1,3},{2,0},{3,1},{4,6},{5,7},{6,4},{7,5},{8,10},{9,11},{10,... | collective-permute-start | bytes 663560 | tf_op jit(solution)/shard_map/ppermute | solution.py:36
  29.5 2.3 collective-permute-start.5
  31.8 7.6 %collective-permute-done.10 = bf16[48,2304]{1,0:T(8,128)(2,1)} collective-permute-done((bf16[48,2304]{1,0:T(8,128)(2,1)S(1)}, bf16[48,2304]{1,0:T(8,128)(2,1)}, u32[]{:S(2)}, u32[]{:S(2)}) %collective-permute-start.10) | collective-permute-done | bytes 221216 | tf_op jit(solution)/shard_map/ppermute | solution.py:36
  40.5 4.4 %collective-permute-done.4 = bf16[4,48,1152]{2,1,0:T(8,128)(2,1)S(1)} collective-permute-done((bf16[4,48,1152]{2,1,0:T(8,128)(2,1)S(1)}, bf16[4,48,1152]{2,1,0:T(8,128)(2,1)S(1)}, u32[]{:S(2)}, u32[]{:S(2)}) %collective-permute-start.4) | collective-permute-done | bytes 442400 | tf_op jit(solution)/shard_map/ppermute | solution.py:36
  54.0 2.0 pad_maximum_fusion.w_ref
  56.0 3.6 %shard_map.305 = (bf16[64,1536]{1,0:T(8,128)(2,1)}, bf16[64,1536]{1,0:T(8,128)(2,1)}) custom-call(bf16[128,768]{1,0:T(8,128)(2,1)} %pad_maximum_fusion.14.x_ref, f32[2,768]{1,0:T(2,128)} %reshape.167.gain_ref, bf16[768,2304]{1,0:T(8,128)(2,1)} %pad_maximum_fusion.w_ref, f32[128,128]{1,0:T(8,128)} %pad_maximum_fusion.15.cos_ref, ...), custom_call_target="tpu_custom_call" | custom-call | flops 37748736 | bytes 516096 | tf_op jit(solution)/shard_map/pallas_call | solution.py:520
  60.9 5.1 %collective-permute-start.7 = (bf16[64,1536]{1,0:T(8,128)(2,1)}, bf16[64,1536]{1,0:T(8,128)(2,1)S(1)}, u32[]{:S(2)}, u32[]{:S(2)}) collective-permute-start(bf16[64,1536]{1,0:T(8,128)(2,1)} %get-tuple-element.77), channel_id=1, source_target_pairs={{0,1},{1,2},{2,3},{3,4},{4,5},{5,6},{6,7},{7,8},{8,9},{9,10},{10,1... | collective-permute-start | bytes 589832 | tf_op jit(solution)/shard_map/ppermute | solution.py:154
  67.5 10.1 %shard_map.306 = (bf16[1280,768]{1,0:T(8,128)(2,1)}, bf16[1280,768]{1,0:T(8,128)(2,1)}, bf16[1280,768]{1,0:T(8,128)(2,1)}, bf16[1280,768]{1,0:T(8,128)(2,1)}) custom-call(bf16[1280,768]{1,0:T(8,128)(2,1)} %x_ref.4, f32[2,768]{1,0:T(2,128)} %reshape.167.gain_ref, bf16[768,2304]{1,0:T(8,128)(2,1)} %pad_maximum_fusion.w_ref, f32[1280,128]{1,0:T(8,128)} %copy-done.2, ...), custom_call_target="tpu_custom_call" | custom-call | flops 566231040 | bytes 1671168 | tf_op jit(solution)/shard_map/pallas_call | solution.py:506
  78.3 21.9 %shard_map.307 = (bf16[1280,768]{1,0:T(8,128)(2,1)}, f32[6,2,1280]{2,1,0:T(2,128)}) custom-call(s32[3]{0:T(128)} %pad_add_fusion.meta_ref, bf16[1280,768]{1,0:T(8,128)(2,1)} %get-tuple-element.74.q_ref, bf16[1280,768]{1,0:T(8,128)(2,1)} %get-tuple-element.75.k_ref, bf16[1280,768]{1,0:T(8,128)(2,1)} %get-tuple-element.76.v_ref, bf16[64,1536]{1,0:T(8,128)(2,1)} %copy-done.8, ...), custom_call_target="tpu_custom_call" | custom-call | flops 251658240 | bytes 983040 | tf_op jit(solution)/shard_map/pallas_call | solution.py:544
  105.7 6.0 %collective-permute-done.15 = bf16[768,2304]{1,0:T(8,128)(2,1)} collective-permute-done((bf16[768,2304]{1,0:T(8,128)(2,1)S(1)}, bf16[768,2304]{1,0:T(8,128)(2,1)}, u32[]{:S(2)}, u32[]{:S(2)}) %collective-permute-start.15) | collective-permute-done | bytes 3538976 | tf_op jit(solution)/shard_map/ppermute | solution.py:36
  111.7 2.5 broadcast_select_fusion.1
  119.6 42.8 %shard_map.308 = (bf16[1280,768]{1,0:T(8,128)(2,1)}, f32[1280,768]{1,0:T(8,128)}, bf16[1280,768]{1,0:T(8,128)(2,1)}, bf16[1152,768]{1,0:T(8,128)(2,1)}, bf16[768...) custom-call(bf16[1280,768]{1,0:T(8,128)(2,1)} %x_ref.4, bf16[1280,768]{1,0:T(8,128)(2,1)} %get-tuple-element.80.o_ref, ...), custom_call_target="tpu_custom_call" | custom-call | flops 3114270720 | bytes 3342336 | tf_op jit(solution)/shard_map/pallas_call | solution.py:609
  162.4 2.6 constant_dynamic-slice_fusion.4
  177.8 9.6 %shard_map.309 = (bf16[256,768]{1,0:T(8,128)(2,1)}, f32[512,768]{1,0:T(8,128)}, f32[512,768]{1,0:T(8,128)}, bf16[128,768]{1,0:T(8,128)(2,1)}, bf16[128,768]{1,0:T(8,128)(2,1)}) custom-call(s32[3]{0:T(128)} %pad_add_fusion.meta_ref, bf16[1280,768]{1,0:T(8,128)(2,1)} %get-tuple-element.74.q_ref, bf16[1280,768]{1,0:T(8,128)(2,1)} %get-tuple-element.75.k_ref, ...), custom_call_target="tpu_custom_call" | custom-call | flops 125829120 | bytes 1228800 | tf_op jit(solution)/shard_map/pallas_call | solution.py:576
  196.6 2.7 add_convert_fusion
  200.8 20.8 %shard_map.310 = (bf16[1280,768]{1,0:T(8,128)(2,1)}, bf16[1280,768]{1,0:T(8,128)(2,1)}, bf16[1280,768]{1,0:T(8,128)(2,1)}) custom-call(s32[3]{0:T(128)} %pad_add_fusion.meta_ref, bf16[1280,768]{1,0:T(8,128)(2,1)} %get-tuple-element.74.q_ref, bf16[1280,768]{1,0:T(8,128)(2,1)} %get-tuple-element.75.k_ref, bf16[1280,768]{1,0:T(8,128)(2,1)} %get-tuple-element.76.v_ref, ...), custom_call_target="tpu_custom_call" | custom-call | flops 629145600 | bytes 1720320 | tf_op jit(solution)/shard_map/pallas_call | solution.py:594
  221.6 6.2 %collective-permute-start.19 = (bf16[4,48,2304]{2,1,0:T(8,128)(2,1)}, bf16[4,48,2304]{2,1,0:T(8,128)(2,1)}, u32[]{:S(2)}, u32[]{:S(2)}) collective-permute-start(bf16[4,48,2304]{2,1,0:T(8,128)(2,1)} %get-tuple-element.148), channel_id=1, source_target_pairs={{0,8},{4,12},{8,0},{12,4},{16,24},{20,28},{24,16},{28,20},{1,9},{5... | collective-permute-start | bytes 2654216 | tf_op jit(solution)/shard_map/ppermute | solution.py:36
  239.1 10.5 %shard_map.311 = bf16[768,2304]{1,0:T(8,128)(2,1)} custom-call(bf16[1280,768]{1,0:T(8,128)(2,1)} %get-tuple-element.100.h_ref, bf16[1280,768]{1,0:T(8,128)(2,1)} %get-tuple-element.110.dq_ref, bf16[1280,768]{1,0:T(8,128)(2,1)} %get-tuple-element.101.dk_ref, bf16[1280,768]{1,0:T(8,128)(2,1)} %get-tuple-element.102.dv_ref, bf16[128,768]{1,0:T(8,128)(2,1)} %copy.53.ek_ref, ...), custom_call_target="tpu_custom_call" | custom-call | flops 566231040 | bytes 1425408 | tf_op jit(solution)/shard_map/pallas_call | solution.py:631
  251.3 17.7 %collective-permute-done.20 = bf16[4,48,2304]{2,1,0:T(8,128)(2,1)} collective-permute-done((bf16[4,48,2304]{2,1,0:T(8,128)(2,1)}, bf16[4,48,2304]{2,1,0:T(8,128)(2,1)}, u32[]{:S(2)}, u32[]{:S(2)}) %collective-permute-start.20) | collective-permute-done | bytes 884768 | tf_op jit(solution)/shard_map/ppermute | solution.py:36
  268.9 2.1 fusion.8
  271.2 3.7 %collective-permute-done.22 = bf16[768,1152]{1,0:T(8,128)(2,1)S(1)} collective-permute-done((bf16[768,1152]{1,0:T(8,128)(2,1)S(1)}, bf16[768,1152]{1,0:T(8,128)(2,1)S(1)}, u32[]{:S(2)}, u32[]{:S(2)}) %collective-permute-start.22) | collective-permute-done | bytes 1769504 | tf_op jit(solution)/shard_map/ppermute | solution.py:36
  280.5 2.1 collective-permute-start.28
  282.6 11.7 %shard_map.312 = bf16[1280,768]{1,0:T(8,128)(2,1)} custom-call(bf16[1280,768]{1,0:T(8,128)(2,1)} %x_ref.4, f32[2,768]{1,0:T(2,128)} %reshape.167.gain_ref, bf16[768,2304]{1,0:T(8,128)(2,1)} %pad_maximum_fusion.w_ref, f32[1280,768]{1,0:T(8,128)} %get-tuple-element.87.dmid_ref, bf16[1280,768]{1,0:T(8,128)(2,1)} %get-tuple-element.110.dq_ref, ...), custom_call_target="tpu_custom_call" | custom-call | flops 566231040 | bytes 2162688 | tf_op jit(solution)/shard_map/pallas_call | solution.py:646
  294.3 2.4 collective-permute-start.29
  298.3 4.3 %collective-permute-done.29 = bf16[48,2304]{1,0:T(8,128)(2,1)S(1)} collective-permute-done((bf16[48,2304]{1,0:T(8,128)(2,1)}, bf16[48,2304]{1,0:T(8,128)(2,1)S(1)}, u32[]{:S(2)}, u32[]{:S(2)}) %collective-permute-start.29) | collective-permute-done | bytes 221216 | tf_op jit(solution)/shard_map/ppermute | solution.py:36
  302.6 3.1 collective-permute-start.26
  319.3 3.1 collective-permute-done.34
  326.9 3.4 %multiply_subtract_fusion.1 = (f32[192,2304]{1,0:T(8,128)}, f32[192,2304]{1,0:T(8,128)}, f32[192,2304]{1,0:T(8,128)}, f32[192]{0:T(256)S(1)}) fusion(f32[192,2304]{1,0:T(8,128)S(1)} %copy-done.3, bf16[192,1152]{1,0:T(8,128)(2,1)S(1)} %get-tuple-element.173, bf16[192,1152]{1,0:T(8,128)(2,1)S(1)} %get-tuple-element.172, f32[192,2304]{1,0:T(8,128)S(1)} %copy-done.13, ...), kind=kLoop, calls=%fused_computation.27 | loop fusion | flops 10174272 | bytes 11502336 | tf_op jit(solution)/shard_map/sub | solution.py:676
  333.0 3.4 %multiply_subtract_fusion = (f32[192,2304]{1,0:T(8,128)}, f32[192,2304]{1,0:T(8,128)}, f32[192,2304]{1,0:T(8,128)}, f32[192]{0:T(256)S(1)}) fusion(f32[192,2304]{1,0:T(8,128)S(1)} %copy-done.5, bf16[192,1152]{1,0:T(8,128)(2,1)S(1)} %slice.219, bf16[192,1152]{1,0:T(8,128)(2,1)S(1)} %slice.218, f32[192,2304]{1,0:T(8,128)S(1)} %copy-done.15, ...), kind=kLoop, calls=%fused_computation.26 | loop fusion | flops 10174272 | bytes 11502336 | tf_op jit(solution)/shard_map/sub | solution.py:676
  (252 shorter events, 109.6 us)
Async XLA Ops:
  2.6 16.5 %collective-permute-start = (bf16[56,1152]{1,0:T(8,128)(2,1)S(1)}, bf16[56,1152]{1,0:T(8,128)(2,1)S(1)}, u32[]{:S(2)}, u32[]{:S(2)}) collective-permute-start(bf16[56,1152]{1,0:T(8,128)(2,1)S(1)} %fusion.25), channel_id=1, source_target_pairs={{0,1},{1,0},{2,3},{3,2},{4,5},{5,4},{6,7},{7,6},{8,9},{9,8},{10,11... | collective-permute-start | bytes 387080 | tf_op jit(solution)/shard_map/ppermute | solution.py:36
  5.7 17.8 %collective-permute-start.1 = (bf16[56,1152]{1,0:T(8,128)(2,1)S(1)}, bf16[56,1152]{1,0:T(8,128)(2,1)S(1)}, u32[]{:S(2)}, u32[]{:S(2)}) collective-permute-start(bf16[56,1152]{1,0:T(8,128)(2,1)S(1)} %fusion.25), channel_id=1, source_target_pairs={{0,2},{1,3},{2,0},{3,1},{4,6},{5,7},{6,4},{7,5},{8,10},{9,11},{10,... | collective-permute-start | bytes 387080 | tf_op jit(solution)/shard_map/ppermute | solution.py:36
  8.3 15.3 %collective-permute-start.2 = (bf16[56,1152]{1,0:T(8,128)(2,1)S(1)}, bf16[56,1152]{1,0:T(8,128)(2,1)S(1)}, u32[]{:S(2)}, u32[]{:S(2)}) collective-permute-start(bf16[56,1152]{1,0:T(8,128)(2,1)S(1)} %fusion.25), channel_id=1, source_target_pairs={{0,3},{1,2},{2,1},{3,0},{4,7},{5,6},{6,5},{7,4},{8,11},{9,10},{10,... | collective-permute-start | bytes 387080 | tf_op jit(solution)/shard_map/ppermute | solution.py:36
  19.1 10.4 %collective-permute-start.9 = (bf16[48,2304]{1,0:T(8,128)(2,1)S(1)}, bf16[48,2304]{1,0:T(8,128)(2,1)}, u32[]{:S(2)}, u32[]{:S(2)}) collective-permute-start(bf16[48,2304]{1,0:T(8,128)(2,1)S(1)} %pad_maximum_fusion.11), channel_id=1, source_target_pairs={{0,1},{1,0},{2,3},{3,2},{4,5},{5,4},{6,7},{7,6},{8,9},{9,8},{10,11... | collective-permute-start | bytes 663560 | tf_op jit(solution)/shard_map/ppermute | solution.py:36
  20.0 19.4 %collective-permute-start.10 = (bf16[48,2304]{1,0:T(8,128)(2,1)S(1)}, bf16[48,2304]{1,0:T(8,128)(2,1)}, u32[]{:S(2)}, u32[]{:S(2)}) collective-permute-start(bf16[48,2304]{1,0:T(8,128)(2,1)S(1)} %pad_maximum_fusion.11), channel_id=1, source_target_pairs={{0,2},{1,3},{2,0},{3,1},{4,6},{5,7},{6,4},{7,5},{8,10},{9,11},{10,... | collective-permute-start | bytes 663560 | tf_op jit(solution)/shard_map/ppermute | solution.py:36
  23.5 15.9 %collective-permute-start.11 = (bf16[48,2304]{1,0:T(8,128)(2,1)S(1)}, bf16[48,2304]{1,0:T(8,128)(2,1)}, u32[]{:S(2)}, u32[]{:S(2)}) collective-permute-start(bf16[48,2304]{1,0:T(8,128)(2,1)S(1)} %pad_maximum_fusion.11), channel_id=1, source_target_pairs={{0,3},{1,2},{2,1},{3,0},{4,7},{5,6},{6,5},{7,4},{8,11},{9,10},{10,... | collective-permute-start | bytes 663560 | tf_op jit(solution)/shard_map/ppermute | solution.py:36
  23.6 15.8 %collective-permute-start.3 = (bf16[4,48,1152]{2,1,0:T(8,128)(2,1)S(1)}, bf16[4,48,1152]{2,1,0:T(8,128)(2,1)}, u32[]{:S(2)}, u32[]{:S(2)}) collective-permute-start(bf16[4,48,1152]{2,1,0:T(8,128)(2,1)S(1)} %slice.187), channel_id=1, source_target_pairs={{0,8},{4,12},{8,0},{12,4},{16,24},{20,28},{24,16},{28,20},{1,9},{5... | collective-permute-start | bytes 1327112 | tf_op jit(solution)/shard_map/ppermute | solution.py:36
  25.4 19.5 %collective-permute-start.4 = (bf16[4,48,1152]{2,1,0:T(8,128)(2,1)S(1)}, bf16[4,48,1152]{2,1,0:T(8,128)(2,1)S(1)}, u32[]{:S(2)}, u32[]{:S(2)}) collective-permute-start(bf16[4,48,1152]{2,1,0:T(8,128)(2,1)S(1)} %slice.187), channel_id=1, source_target_pairs={{0,16},{4,20},{8,24},{12,28},{16,0},{20,4},{24,8},{28,12},{1,17},{... | collective-permute-start | bytes 1327112 | tf_op jit(solution)/shard_map/ppermute | solution.py:36
  29.5 15.4 %collective-permute-start.5 = (bf16[4,48,1152]{2,1,0:T(8,128)(2,1)S(1)}, bf16[4,48,1152]{2,1,0:T(8,128)(2,1)S(1)}, u32[]{:S(2)}, u32[]{:S(2)}) collective-permute-start(bf16[4,48,1152]{2,1,0:T(8,128)(2,1)S(1)} %slice.187), channel_id=1, source_target_pairs={{0,24},{4,28},{8,16},{12,20},{16,8},{20,12},{24,0},{28,4},{1,25},{... | collective-permute-start | bytes 1327112 | tf_op jit(solution)/shard_map/ppermute | solution.py:36
  50.0 50.2 %collective-permute-start.14 = (bf16[4,48,2304]{2,1,0:T(8,128)(2,1)}, bf16[4,48,2304]{2,1,0:T(8,128)(2,1)}, u32[]{:S(2)}, u32[]{:S(2)}) collective-permute-start(bf16[4,48,2304]{2,1,0:T(8,128)(2,1)} %bitcast_dynamic-update-slice_fusion.12), channel_id=1, source_target_pairs={{0,24},{4,28},{8,16},{12,20},{16,8},{20,12},{24,0},{28,4},{1,25},{... | collective-permute-start | bytes 2654216 | tf_op jit(solution)/shard_map/ppermute | solution.py:36
  51.5 48.7 %collective-permute-start.13 = (bf16[4,48,2304]{2,1,0:T(8,128)(2,1)}, bf16[4,48,2304]{2,1,0:T(8,128)(2,1)}, u32[]{:S(2)}, u32[]{:S(2)}) collective-permute-start(bf16[4,48,2304]{2,1,0:T(8,128)(2,1)} %bitcast_dynamic-update-slice_fusion.12), channel_id=1, source_target_pairs={{0,16},{4,20},{8,24},{12,28},{16,0},{20,4},{24,8},{28,12},{1,17},{... | collective-permute-start | bytes 2654216 | tf_op jit(solution)/shard_map/ppermute | solution.py:36
  52.6 47.6 %collective-permute-start.12 = (bf16[4,48,2304]{2,1,0:T(8,128)(2,1)}, bf16[4,48,2304]{2,1,0:T(8,128)(2,1)}, u32[]{:S(2)}, u32[]{:S(2)}) collective-permute-start(bf16[4,48,2304]{2,1,0:T(8,128)(2,1)} %bitcast_dynamic-update-slice_fusion.12), channel_id=1, source_target_pairs={{0,8},{4,12},{8,0},{12,4},{16,24},{20,28},{24,16},{28,20},{1,9},{5... | collective-permute-start | bytes 2654216 | tf_op jit(solution)/shard_map/ppermute | solution.py:36
  59.6 18.0 %collective-permute-start.8 = (bf16[64,1536]{1,0:T(8,128)(2,1)}, bf16[64,1536]{1,0:T(8,128)(2,1)S(1)}, u32[]{:S(2)}, u32[]{:S(2)}) collective-permute-start(bf16[64,1536]{1,0:T(8,128)(2,1)} %get-tuple-element.72), channel_id=1, source_target_pairs={{1,0},{2,1},{3,2},{4,3},{5,4},{6,5},{7,6},{8,7},{9,8},{10,9},{11,1... | collective-permute-start | bytes 589832 | tf_op jit(solution)/shard_map/ppermute | solution.py:160
  60.9 16.7 %collective-permute-start.7 = (bf16[64,1536]{1,0:T(8,128)(2,1)}, bf16[64,1536]{1,0:T(8,128)(2,1)S(1)}, u32[]{:S(2)}, u32[]{:S(2)}) collective-permute-start(bf16[64,1536]{1,0:T(8,128)(2,1)} %get-tuple-element.77), channel_id=1, source_target_pairs={{0,1},{1,2},{2,3},{3,4},{4,5},{5,6},{6,7},{7,8},{8,9},{9,10},{10,1... | collective-permute-start | bytes 589832 | tf_op jit(solution)/shard_map/ppermute | solution.py:154
  169.4 27.2 %collective-permute-start.16 = (bf16[768,2304]{1,0:T(8,128)(2,1)S(1)}, bf16[768,2304]{1,0:T(8,128)(2,1)}, u32[]{:S(2)}, u32[]{:S(2)}) collective-permute-start(bf16[768,2304]{1,0:T(8,128)(2,1)S(1)} %pad_maximum_fusion.2), channel_id=1, source_target_pairs={{0,4},{4,0},{8,12},{12,8},{16,20},{20,16},{24,28},{28,24},{1,5},{5... | collective-permute-start | bytes 10616840 | tf_op jit(solution)/shard_map/ppermute | solution.py:36
  190.3 31.3 %collective-permute-start.17 = (bf16[64,1536]{1,0:T(8,128)(2,1)}, bf16[64,1536]{1,0:T(8,128)(2,1)}, u32[]{:S(2)}, u32[]{:S(2)}) collective-permute-start(bf16[64,1536]{1,0:T(8,128)(2,1)} %get-tuple-element.186), channel_id=1, source_target_pairs={{0,1},{1,2},{2,3},{3,4},{4,5},{5,6},{6,7},{7,8},{8,9},{9,10},{10,1... | collective-permute-start | bytes 589832 | tf_op jit(solution)/shard_map/ppermute | solution.py:154
  192.3 29.3 %collective-permute-start.18 = (bf16[64,1536]{1,0:T(8,128)(2,1)}, bf16[64,1536]{1,0:T(8,128)(2,1)}, u32[]{:S(2)}, u32[]{:S(2)}) collective-permute-start(bf16[64,1536]{1,0:T(8,128)(2,1)} %get-tuple-element.187), channel_id=1, source_target_pairs={{1,0},{2,1},{3,2},{4,3},{5,4},{6,5},{7,6},{8,7},{9,8},{10,9},{11,1... | collective-permute-start | bytes 589832 | tf_op jit(solution)/shard_map/ppermute | solution.py:160
  221.6 29.6 %collective-permute-start.19 = (bf16[4,48,2304]{2,1,0:T(8,128)(2,1)}, bf16[4,48,2304]{2,1,0:T(8,128)(2,1)}, u32[]{:S(2)}, u32[]{:S(2)}) collective-permute-start(bf16[4,48,2304]{2,1,0:T(8,128)(2,1)} %get-tuple-element.148), channel_id=1, source_target_pairs={{0,8},{4,12},{8,0},{12,4},{16,24},{20,28},{24,16},{28,20},{1,9},{5... | collective-permute-start | bytes 2654216 | tf_op jit(solution)/shard_map/ppermute | solution.py:36
  227.8 41.1 %collective-permute-start.20 = (bf16[4,48,2304]{2,1,0:T(8,128)(2,1)}, bf16[4,48,2304]{2,1,0:T(8,128)(2,1)}, u32[]{:S(2)}, u32[]{:S(2)}) collective-permute-start(bf16[4,48,2304]{2,1,0:T(8,128)(2,1)} %get-tuple-element.150), channel_id=1, source_target_pairs={{0,16},{4,20},{8,24},{12,28},{16,0},{20,4},{24,8},{28,12},{1,17},{... | collective-permute-start | bytes 2654216 | tf_op jit(solution)/shard_map/ppermute | solution.py:36
  229.2 39.7 %collective-permute-start.21 = (bf16[4,48,2304]{2,1,0:T(8,128)(2,1)}, bf16[4,48,2304]{2,1,0:T(8,128)(2,1)}, u32[]{:S(2)}, u32[]{:S(2)}) collective-permute-start(bf16[4,48,2304]{2,1,0:T(8,128)(2,1)} %get-tuple-element.149), channel_id=1, source_target_pairs={{0,24},{4,28},{8,16},{12,20},{16,8},{20,12},{24,0},{28,4},{1,25},{... | collective-permute-start | bytes 2654216 | tf_op jit(solution)/shard_map/ppermute | solution.py:36
  276.2 18.1 %collective-permute-start.23 = (bf16[4,48,1152]{2,1,0:T(8,128)(2,1)}, bf16[4,48,1152]{2,1,0:T(8,128)(2,1)S(1)}, u32[]{:S(2)}, u32[]{:S(2)}) collective-permute-start(bf16[4,48,1152]{2,1,0:T(8,128)(2,1)} %get-tuple-element.159), channel_id=1, source_target_pairs={{0,8},{4,12},{8,0},{12,4},{16,24},{20,28},{24,16},{28,20},{1,9},{5... | collective-permute-start | bytes 1327112 | tf_op jit(solution)/shard_map/ppermute | solution.py:36
  276.6 21.4 %collective-permute-start.24 = (bf16[4,48,1152]{2,1,0:T(8,128)(2,1)S(1)}, bf16[4,48,1152]{2,1,0:T(8,128)(2,1)S(1)}, u32[]{:S(2)}, u32[]{:S(2)}) collective-permute-start(bf16[4,48,1152]{2,1,0:T(8,128)(2,1)S(1)} %get-tuple-element.161), channel_id=1, source_target_pairs={{0,16},{4,20},{8,24},{12,28},{16,0},{20,4},{24,8},{28,12},{1,17},{... | collective-permute-start | bytes 1327112 | tf_op jit(solution)/shard_map/ppermute | solution.py:36
  277.9 20.0 %collective-permute-start.25 = (bf16[4,48,1152]{2,1,0:T(8,128)(2,1)S(1)}, bf16[4,48,1152]{2,1,0:T(8,128)(2,1)S(1)}, u32[]{:S(2)}, u32[]{:S(2)}) collective-permute-start(bf16[4,48,1152]{2,1,0:T(8,128)(2,1)S(1)} %get-tuple-element.160), channel_id=1, source_target_pairs={{0,24},{4,28},{8,16},{12,20},{16,8},{20,12},{24,0},{28,4},{1,25},{... | collective-permute-start | bytes 1327112 | tf_op jit(solution)/shard_map/ppermute | solution.py:36
  280.5 17.7 %collective-permute-start.27 = (bf16[48,2304]{1,0:T(8,128)(2,1)}, bf16[48,2304]{1,0:T(8,128)(2,1)}, u32[]{:S(2)}, u32[]{:S(2)}) collective-permute-start(bf16[48,2304]{1,0:T(8,128)(2,1)} %get-tuple-element.174), channel_id=1, source_target_pairs={{0,1},{1,0},{2,3},{3,2},{4,5},{5,4},{6,7},{7,6},{8,9},{9,8},{10,11... | collective-permute-start | bytes 663560 | tf_op jit(solution)/shard_map/ppermute | solution.py:36
  280.5 17.7 %collective-permute-start.28 = (bf16[48,2304]{1,0:T(8,128)(2,1)}, bf16[48,2304]{1,0:T(8,128)(2,1)}, u32[]{:S(2)}, u32[]{:S(2)}) collective-permute-start(bf16[48,2304]{1,0:T(8,128)(2,1)} %get-tuple-element.176), channel_id=1, source_target_pairs={{0,2},{1,3},{2,0},{3,1},{4,6},{5,7},{6,4},{7,5},{8,10},{9,11},{10,... | collective-permute-start | bytes 663560 | tf_op jit(solution)/shard_map/ppermute | solution.py:36
  302.6 8.9 %collective-permute-start.26 = (bf16[48,1152]{1,0:T(8,128)(2,1)S(1)}, bf16[48,1152]{1,0:T(8,128)(2,1)S(1)}, u32[]{:S(2)}, u32[]{:S(2)}) collective-permute-start(bf16[48,1152]{1,0:T(8,128)(2,1)S(1)} %get-tuple-element.183), channel_id=1, source_target_pairs={{0,1},{1,0},{2,3},{3,2},{4,5},{5,4},{6,7},{7,6},{8,9},{9,8},{10,11... | collective-permute-start | bytes 331784 | tf_op jit(solution)/shard_map/ppermute | solution.py:36
  305.7 9.4 %collective-permute-start.30 = (bf16[48,1152]{1,0:T(8,128)(2,1)S(1)}, bf16[48,1152]{1,0:T(8,128)(2,1)S(1)}, u32[]{:S(2)}, u32[]{:S(2)}) collective-permute-start(bf16[48,1152]{1,0:T(8,128)(2,1)S(1)} %get-tuple-element.185), channel_id=1, source_target_pairs={{0,2},{1,3},{2,0},{3,1},{4,6},{5,7},{6,4},{7,5},{8,10},{9,11},{10,... | collective-permute-start | bytes 331784 | tf_op jit(solution)/shard_map/ppermute | solution.py:36
  306.5 8.5 %collective-permute-start.31 = (bf16[48,1152]{1,0:T(8,128)(2,1)S(1)}, bf16[48,1152]{1,0:T(8,128)(2,1)S(1)}, u32[]{:S(2)}, u32[]{:S(2)}) collective-permute-start(bf16[48,1152]{1,0:T(8,128)(2,1)S(1)} %get-tuple-element.184), channel_id=1, source_target_pairs={{0,3},{1,2},{2,1},{3,0},{4,7},{5,6},{6,5},{7,4},{8,11},{9,10},{10,... | collective-permute-start | bytes 331784 | tf_op jit(solution)/shard_map/ppermute | solution.py:36
  309.5 9.4 %collective-permute-start.35 = (bf16[48,2304]{1,0:T(8,128)(2,1)S(1)}, bf16[48,2304]{1,0:T(8,128)(2,1)S(1)}, u32[]{:S(2)}, u32[]{:S(2)}) collective-permute-start(bf16[48,2304]{1,0:T(8,128)(2,1)S(1)} %get-tuple-element.143), channel_id=1, source_target_pairs={{0,24},{4,28},{8,16},{12,20},{16,8},{20,12},{24,0},{28,4},{1,25},{... | collective-permute-start | bytes 663560 | tf_op jit(solution)/shard_map/ppermute | solution.py:36
  310.8 11.7 %collective-permute-start.34 = (bf16[48,2304]{1,0:T(8,128)(2,1)S(1)}, bf16[48,2304]{1,0:T(8,128)(2,1)S(1)}, u32[]{:S(2)}, u32[]{:S(2)}) collective-permute-start(bf16[48,2304]{1,0:T(8,128)(2,1)S(1)} %get-tuple-element.143), channel_id=1, source_target_pairs={{0,16},{4,20},{8,24},{12,28},{16,0},{20,4},{24,8},{28,12},{1,17},{... | collective-permute-start | bytes 663560 | tf_op jit(solution)/shard_map/ppermute | solution.py:36
  311.4 11.0 %collective-permute-start.33 = (bf16[48,2304]{1,0:T(8,128)(2,1)S(1)}, bf16[48,2304]{1,0:T(8,128)(2,1)S(1)}, u32[]{:S(2)}, u32[]{:S(2)}) collective-permute-start(bf16[48,2304]{1,0:T(8,128)(2,1)S(1)} %get-tuple-element.143), channel_id=1, source_target_pairs={{0,8},{4,12},{8,0},{12,4},{16,24},{20,28},{24,16},{28,20},{1,9},{5... | collective-permute-start | bytes 663560 | tf_op jit(solution)/shard_map/ppermute | solution.py:36
  315.2 8.6 %collective-permute-start.37 = (bf16[48,1152]{1,0:T(8,128)(2,1)S(1)}, bf16[48,1152]{1,0:T(8,128)(2,1)S(1)}, u32[]{:S(2)}, u32[]{:S(2)}) collective-permute-start(bf16[48,1152]{1,0:T(8,128)(2,1)S(1)} %get-tuple-element.145), channel_id=1, source_target_pairs={{0,24},{4,28},{8,16},{12,20},{16,8},{20,12},{24,0},{28,4},{1,25},{... | collective-permute-start | bytes 331784 | tf_op jit(solution)/shard_map/ppermute | solution.py:36
  (42 other events, 240.6 us)
